TPU v7x, 32 devices: a whole 2x2x4 slice. The times are simulated.
32 devices in a mesh: dp: 8 (over y, x, core), chan: 4 (over z).
Axes of the slice: x: 2, y: 2, z: 4, core: 2. Of those that a mesh axis runs over, the one named last changes fastest.
Arguments:
- stream: bfloat16 [8192, 768], P('dp', 'chan'), may hold values from -32 to 32, as said below
- segments: int32 [8192], P('dp'), may hold values from 0 to 64, as said below
- cotangent: bfloat16 [8192, 768], P('dp', 'chan'), may hold values from -6 to 6
- norm_one: float32 [2, 768], P(None, 'chan'), may hold values from 0.1 to 1.9
- in_proj: bfloat16 [2, 768, 3, 768], P(None, None, None, 'chan'), may hold values from -0.21875 to 0.21875
- short_taps: float32 [2, 3, 3, 768], P(None, None, None, 'chan'), may hold values from -3 to 3
- cond_in: float32 [2, 12, 128, 128], P(None, 'chan'), may hold values from -0.5 to 0.5
- cond_out: float32 [2, 12, 128, 128], P(None, 'chan'), may hold values from -0.5 to 0.5
- filter_spec: float32 [2, 2, 1024, 768], P(None, None, None, 'chan'), may hold values from -4 to 4
- out_proj: bfloat16 [2, 768, 768], P(None, 'chan'), may hold values from -0.21875 to 0.21875
- norm_two: float32 [2, 768], P(None, 'chan'), may hold values from 0.1 to 1.9
- gate_proj: bfloat16 [2, 768, 3072], P(None, None, 'chan'), may hold values from -0.21875 to 0.21875
- up_proj: bfloat16 [2, 768, 3072], P(None, None, 'chan'), may hold values from -0.21875 to 0.21875
- down_proj: bfloat16 [2, 3072, 768], P(None, 'chan'), may hold values from -0.109375 to 0.109375
Outputs:
- output: float32 [8192, 768], P('dp', 'chan')
- stream_grad: float32 [8192, 768], P('dp', 'chan')
- norm_one_grad: float32 [2, 768], P(None, 'chan')
- in_proj_grad: float32 [2, 768, 3, 768], P(None, None, None, 'chan')
- short_taps_grad: float32 [2, 3, 3, 768], P(None, None, None, 'chan')
- cond_in_grad: float32 [2, 12, 128, 128], P(None, 'chan')
- cond_out_grad: float32 [2, 12, 128, 128], P(None, 'chan')
- filter_spec_grad: float32 [2, 2, 1024, 768], P(None, None, None, 'chan')
- out_proj_grad: float32 [2, 768, 768], P(None, 'chan')
- norm_two_grad: float32 [2, 768], P(None, 'chan')
- gate_proj_grad: float32 [2, 768, 3072], P(None, None, 'chan')
- up_proj_grad: float32 [2, 768, 3072], P(None, None, 'chan')
- down_proj_grad: float32 [2, 3072, 768], P(None, 'chan')
Inputs may be any that keep to these rules, and one draw needn't show every extreme that they name: `stream`: activations; within each pack the channels' scales differ widely. `segments`: within each pack of 1024 rows the numbers start at 0 on its first row, rise by 0 or 1 from one row to the next, and end at 64 on its last row.
All inputs are finite; a program needn't handle non-finite values.
Results may differ from a plain program's by a relative error of at most 0.025.
Values may be sent and summed in bfloat16 or wider, within the bound.
A program may use at most 320 MiB of HBM per device.

v0:
```python
from functools import partial
import math

import jax
import jax.numpy as jnp
from jax import lax
from jax.sharding import PartitionSpec as P

EPSILON = 1e-05
PRECISE = lax.Precision.HIGHEST
TRANSFORM_PRECISION = lax.Precision.HIGH


def dft_tables(length):
    positions = jnp.arange(length, dtype=jnp.int32)
    product = positions[:, None] * positions[None, :] % length
    angles = product.astype(jnp.float32) * (2.0 * math.pi / length)
    norm_scale = 1.0 / math.sqrt(length)
    return (jnp.cos(angles) * norm_scale, jnp.sin(angles) * norm_scale)


def mix_core(mask_prev, mask_next, cosine, sine, projected, taps, weight_in, weight_out, spectrum):
    row_count = projected.shape[0]
    length = cosine.shape[0]
    pack_count = row_count // length
    chan_width = projected.shape[2]
    zero_row = jnp.zeros((1,) + projected.shape[1:], jnp.float32)
    preceding = jnp.concatenate([zero_row, projected[:-1]], 0) * mask_prev[:, None, None]
    following = jnp.concatenate([projected[1:], zero_row], 0) * mask_next[:, None, None]
    short_out = taps[0] * preceding + taps[1] * projected + taps[2] * following
    short_out = short_out.reshape(pack_count, length, 3, chan_width)
    query_part = short_out[:, :, 0]
    value_part = short_out[:, :, 1]
    cond_part = short_out[:, :, 2]
    cond_real = jnp.einsum("kt,ptc->pkc", cosine, cond_part, precision=TRANSFORM_PRECISION)
    cond_imag = -jnp.einsum("kt,ptc->pkc", sine, cond_part, precision=TRANSFORM_PRECISION)
    value_real = jnp.einsum("kt,ptc->pkc", cosine, value_part, precision=TRANSFORM_PRECISION)
    value_imag = -jnp.einsum("kt,ptc->pkc", sine, value_part, precision=TRANSFORM_PRECISION)
    head_count = weight_in.shape[0]
    group_size = chan_width // head_count
    grouped = (pack_count, length, head_count, group_size)
    features = jnp.concatenate([cond_real.reshape(grouped), cond_imag.reshape(grouped)], -1)
    inner_act = jax.nn.gelu(
        jnp.einsum("pkhi,hif->pkhf", features, weight_in, precision=PRECISE), approximate=False
    )
    filter_made = jnp.einsum("pkhf,hfo->pkho", inner_act, weight_out, precision=PRECISE)
    kernel_real = spectrum[0] + filter_made[..., :group_size].reshape(
        pack_count, length, chan_width
    )
    kernel_imag = spectrum[1] + filter_made[..., group_size:].reshape(
        pack_count, length, chan_width
    )
    prod_real = value_real * kernel_real - value_imag * kernel_imag
    prod_imag = value_real * kernel_imag + value_imag * kernel_real
    mixed_out = jnp.einsum(
        "kt,pkc->ptc", cosine, prod_real, precision=TRANSFORM_PRECISION
    ) - jnp.einsum("kt,pkc->ptc", sine, prod_imag, precision=TRANSFORM_PRECISION)
    return (query_part * mixed_out).reshape(row_count, chan_width)


def gated_unit(gate_in, up_in):
    return jax.nn.gelu(gate_in, approximate=False) * up_in


def norm_forward(values, norm_gain):
    full_width = values.shape[1] * lax.axis_size("chan")
    average = lax.psum(jnp.sum(values, 1), "chan") / full_width
    centered = values - average[:, None]
    variance = lax.psum(jnp.sum(centered * centered, 1), "chan") / full_width
    inv_std = lax.rsqrt(variance + EPSILON)[:, None]
    normed = centered * inv_std
    return (normed * norm_gain, normed, inv_std)


def norm_backward(grad_out, normed, inv_std, norm_gain):
    full_width = grad_out.shape[1] * lax.axis_size("chan")
    gain_grad = jnp.sum(grad_out * normed, 0)
    scaled = grad_out * norm_gain
    sum_plain, sum_cross = lax.psum((jnp.sum(scaled, 1), jnp.sum(scaled * normed, 1)), "chan")
    grad_in = inv_std * (
        scaled - sum_plain[:, None] / full_width - normed * sum_cross[:, None] / full_width
    )
    return (grad_in, gain_grad)


def gather_feats(normed_low):
    return lax.all_gather(normed_low, "chan", axis=1, tiled=True)


def reduce_rows(partial_rows):
    return lax.psum_scatter(
        partial_rows.astype(jnp.bfloat16), "chan", scatter_dimension=1, tiled=True
    ).astype(jnp.float32)


def gather_grads(grad_low):
    return lax.all_gather(grad_low, "chan", axis=1, tiled=True)


def reduce_grads(partial_grads):
    return lax.psum_scatter(
        partial_grads.astype(jnp.bfloat16), "chan", scatter_dimension=1, tiled=True
    ).astype(jnp.float32)


def on_device(
    stream,
    segments,
    cotangent,
    norm_one,
    in_proj,
    short_taps,
    cond_in,
    cond_out,
    filter_spec,
    out_proj,
    norm_two,
    gate_proj,
    up_proj,
    down_proj,
):
    row_count = stream.shape[0]
    length = filter_spec.shape[2]
    cosine, sine = dft_tables(length)
    position = jnp.arange(row_count, dtype=jnp.int32) % length
    same_seg = segments[1:] == segments[:-1]
    no_flag = jnp.zeros((1,), dtype=bool)
    mask_prev = jnp.where((position != 0) & jnp.concatenate([no_flag, same_seg]), 1.0, 0.0).astype(
        jnp.float32
    )
    mask_next = jnp.where(
        (position != length - 1) & jnp.concatenate([same_seg, no_flag]), 1.0, 0.0
    ).astype(jnp.float32)
    core_fn = partial(mix_core, mask_prev, mask_next, cosine, sine)
    layer_count = norm_one.shape[0]
    values = stream.astype(jnp.float32)
    saved = []
    for layer_number in range(layer_count):
        layer_in = values
        gained_one, normed_one, inv_one = norm_forward(layer_in, norm_one[layer_number])
        gathered_one = gather_feats(gained_one.astype(jnp.bfloat16))
        projected = jnp.einsum(
            "rd,dsc->rsc", gathered_one, in_proj[layer_number], preferred_element_type=jnp.float32
        )
        mixed_low = core_fn(
            projected,
            short_taps[layer_number],
            cond_in[layer_number],
            cond_out[layer_number],
            filter_spec[layer_number],
        ).astype(jnp.bfloat16)
        middle = layer_in + reduce_rows(
            jnp.dot(mixed_low, out_proj[layer_number], preferred_element_type=jnp.float32)
        )
        gained_two, normed_two, inv_two = norm_forward(middle, norm_two[layer_number])
        gathered_two = gather_feats(gained_two.astype(jnp.bfloat16))
        gate_val = jnp.dot(
            gathered_two, gate_proj[layer_number], preferred_element_type=jnp.float32
        )
        up_val = jnp.dot(gathered_two, up_proj[layer_number], preferred_element_type=jnp.float32)
        hidden_low = gated_unit(gate_val, up_val).astype(jnp.bfloat16)
        values = middle + reduce_rows(
            jnp.dot(hidden_low, down_proj[layer_number], preferred_element_type=jnp.float32)
        )
        saved.append((layer_in, middle))
    carried = cotangent.astype(jnp.float32)
    layer_grads = []
    for layer_number in reversed(range(layer_count)):
        layer_in, middle = saved[layer_number]
        gained_one, normed_one, inv_one = norm_forward(layer_in, norm_one[layer_number])
        gathered_one = gather_feats(gained_one.astype(jnp.bfloat16))
        gained_two, normed_two, inv_two = norm_forward(middle, norm_two[layer_number])
        gathered_two = gather_feats(gained_two.astype(jnp.bfloat16))
        gate_val = jnp.dot(
            gathered_two, gate_proj[layer_number], preferred_element_type=jnp.float32
        )
        up_val = jnp.dot(gathered_two, up_proj[layer_number], preferred_element_type=jnp.float32)
        hidden_val, unit_back = jax.vjp(gated_unit, gate_val, up_val)
        hidden_low = hidden_val.astype(jnp.bfloat16)
        full_two = gather_grads(carried.astype(jnp.bfloat16))
        down_weight_grad = jnp.dot(hidden_low.T, full_two, preferred_element_type=jnp.float32)
        hidden_grad = jnp.dot(
            full_two, down_proj[layer_number].T, preferred_element_type=jnp.float32
        )
        gate_grad, up_grad = unit_back(hidden_grad)
        gate_low = gate_grad.astype(jnp.bfloat16)
        up_low = up_grad.astype(jnp.bfloat16)
        gate_weight_grad = jnp.dot(gathered_two.T, gate_low, preferred_element_type=jnp.float32)
        up_weight_grad = jnp.dot(gathered_two.T, up_low, preferred_element_type=jnp.float32)
        feat_part_two = jnp.dot(
            gate_low, gate_proj[layer_number].T, preferred_element_type=jnp.float32
        ) + jnp.dot(up_low, up_proj[layer_number].T, preferred_element_type=jnp.float32)
        norm_grad_two, gain_two_grad = norm_backward(
            reduce_grads(feat_part_two), normed_two, inv_two, norm_two[layer_number]
        )
        middle_grad = carried + norm_grad_two
        projected = jnp.einsum(
            "rd,dsc->rsc", gathered_one, in_proj[layer_number], preferred_element_type=jnp.float32
        )
        mixed_val, core_back = jax.vjp(
            core_fn,
            projected,
            short_taps[layer_number],
            cond_in[layer_number],
            cond_out[layer_number],
            filter_spec[layer_number],
        )
        mixed_low = mixed_val.astype(jnp.bfloat16)
        full_one = gather_grads(middle_grad.astype(jnp.bfloat16))
        out_weight_grad = jnp.dot(mixed_low.T, full_one, preferred_element_type=jnp.float32)
        mixed_grad = jnp.dot(full_one, out_proj[layer_number].T, preferred_element_type=jnp.float32)
        proj_grad, taps_grad, first_mlp_grad, second_mlp_grad, spectrum_grad = core_back(mixed_grad)
        proj_low = proj_grad.astype(jnp.bfloat16)
        in_weight_grad = jnp.einsum(
            "rd,rsc->dsc", gathered_one, proj_low, preferred_element_type=jnp.float32
        )
        feat_part_one = jnp.einsum(
            "rsc,dsc->rd", proj_low, in_proj[layer_number], preferred_element_type=jnp.float32
        )
        norm_grad_one, gain_one_grad = norm_backward(
            reduce_grads(feat_part_one), normed_one, inv_one, norm_one[layer_number]
        )
        carried = middle_grad + norm_grad_one
        summed = (
            gain_one_grad,
            in_weight_grad,
            taps_grad,
            first_mlp_grad,
            second_mlp_grad,
            spectrum_grad,
            out_weight_grad,
            gain_two_grad,
            gate_weight_grad,
            up_weight_grad,
            down_weight_grad,
        )
        layer_grads.insert(0, summed)
    stacked = tuple(
        (
            jnp.stack([layer_grads[layer_number][member] for layer_number in range(layer_count)])
            for member in range(11)
        )
    )
    stacked = (
        lax.psum(stacked[0].astype(jnp.bfloat16), "dp").astype(jnp.float32),
        lax.psum(stacked[1].astype(jnp.bfloat16), "dp").astype(jnp.float32),
        lax.psum(stacked[2].astype(jnp.bfloat16), "dp").astype(jnp.float32),
        lax.psum(stacked[3].astype(jnp.bfloat16), "dp").astype(jnp.float32),
        lax.psum(stacked[4].astype(jnp.bfloat16), "dp").astype(jnp.float32),
        lax.psum(stacked[5].astype(jnp.bfloat16), "dp").astype(jnp.float32),
        lax.psum(stacked[6].astype(jnp.bfloat16), "dp").astype(jnp.float32),
        lax.psum(stacked[7].astype(jnp.bfloat16), "dp").astype(jnp.float32),
        lax.psum(stacked[8].astype(jnp.bfloat16), "dp").astype(jnp.float32),
        lax.psum(stacked[9].astype(jnp.bfloat16), "dp").astype(jnp.float32),
        lax.psum(stacked[10].astype(jnp.bfloat16), "dp").astype(jnp.float32),
    )
    return (
        values,
        carried,
        stacked[0],
        stacked[1],
        stacked[2],
        stacked[3],
        stacked[4],
        stacked[5],
        stacked[6],
        stacked[7],
        stacked[8],
        stacked[9],
        stacked[10],
    )


def solution(mesh):
    return jax.shard_map(
        on_device,
        mesh=mesh,
        in_specs=(
            P("dp", "chan"),
            P("dp"),
            P("dp", "chan"),
            P(None, "chan"),
            P(None, None, None, "chan"),
            P(None, None, None, "chan"),
            P(None, "chan", None, None),
            P(None, "chan", None, None),
            P(None, None, None, "chan"),
            P(None, "chan", None),
            P(None, "chan"),
            P(None, None, "chan"),
            P(None, None, "chan"),
            P(None, "chan", None),
        ),
        out_specs=(
            P("dp", "chan"),
            P("dp", "chan"),
            P(None, "chan"),
            P(None, None, None, "chan"),
            P(None, None, None, "chan"),
            P(None, "chan", None, None),
            P(None, "chan", None, None),
            P(None, None, None, "chan"),
            P(None, "chan", None),
            P(None, "chan"),
            P(None, None, "chan"),
            P(None, None, "chan"),
            P(None, "chan", None),
        ),
        check_vma=False,
    )
```

profile of v0, /device:TPU:0, one launch (start us, length us, event | category | flops | bytes accessed | tf_op | source)
XLA Modules:
  0.0 1467.3 jit_solution(14305121620407096774)
XLA Ops:
  38.1 33.5 %all-gather.9.cloned.1.call-done = bf16[1024,768]{0,1:T(8,128)(2,1)} async-done(((bf16[1024,192]{0,1:T(8,128)(2,1)}), bf16[1024,768]{0,1:T(8,128)(2,1)}) %all-gather.9.cloned.1.call-update) | async-done | bytes 1572880 | tf_op jit(solution)/shard_map/all_gather | solution.py:87
  94.6 18.6 %fusion.156 = f32[192,1024]{1,0:T(8,128)} fusion(f32[1,1024,3,192]{1,3,2,0:T(8,128)S(1)} %add_bitcast_fusion.3), kind=kOutput, calls=%fused_computation.256 | convolution fusion | flops 1223884800 | bytes 1572864 | tf_op jit(solution)/shard_map/kt,ptc->pkc/dot_general | solution.py:36
  113.2 18.4 %fusion.136 = f32[1,1024,192]{1,2,0:T(8,128)} fusion(f32[1,1024,3,192]{1,3,2,0:T(8,128)S(1)} %add_bitcast_fusion.3), kind=kOutput, calls=%fused_computation.236 | convolution fusion | flops 1223688192 | bytes 1572864 | tf_op jit(solution)/shard_map/kt,ptc->pkc/dot_general | solution.py:38
  131.6 18.3 %fusion.140 = f32[1,1024,192]{1,2,0:T(8,128)} fusion(f32[1,1024,3,192]{1,3,2,0:T(8,128)S(1)} %add_bitcast_fusion.3), kind=kOutput, calls=%fused_computation.240 | convolution fusion | flops 1223688192 | bytes 1572864 | tf_op jit(solution)/shard_map/kt,ptc->pkc/dot_general | solution.py:37
  203.6 33.7 %reduce-scatter.9.cloned.1.call-done = bf16[1024,192]{0,1:T(8,128)(2,1)} async-done(((bf16[1024,768]{0,1:T(8,128)(2,1)}), bf16[1024,192]{0,1:T(8,128)(2,1)}) %reduce-scatter.9.cloned.1.call-update) | async-done | bytes 393232 | tf_op jit(solution)/shard_map/reduce_scatter | solution.py:91
  260.4 36.1 %all-gather.11.cloned.1.call-done = bf16[1024,768]{0,1:T(8,128)(2,1)} async-done(((bf16[1024,192]{0,1:T(8,128)(2,1)}), bf16[1024,768]{0,1:T(8,128)(2,1)}) %all-gather.11.cloned.1.call-update) | async-done | bytes 1572880 | tf_op jit(solution)/shard_map/all_gather | solution.py:87
  315.2 34.2 %reduce-scatter.11.cloned.1.call-done = bf16[1024,192]{0,1:T(8,128)(2,1)} async-done(((bf16[1024,768]{0,1:T(8,128)(2,1)}), bf16[1024,192]{0,1:T(8,128)(2,1)}) %reduce-scatter.11.cloned.1.call-update) | async-done | bytes 393232 | tf_op jit(solution)/shard_map/reduce_scatter | solution.py:91
  371.3 35.3 %all-gather.13.cloned.1.call-done = bf16[1024,768]{0,1:T(8,128)(2,1)} async-done(((bf16[1024,192]{0,1:T(8,128)(2,1)}), bf16[1024,768]{0,1:T(8,128)(2,1)}) %all-gather.13.cloned.1.call-update) | async-done | bytes 1572880 | tf_op jit(solution)/shard_map/all_gather | solution.py:87
  430.6 18.4 %fusion.157 = f32[192,1024]{1,0:T(8,128)} fusion(f32[1,1024,3,192]{1,3,2,0:T(8,128)S(1)} %add_bitcast_fusion.2), kind=kOutput, calls=%fused_computation.257 | convolution fusion | flops 1223884800 | bytes 1572864 | tf_op jit(solution)/shard_map/kt,ptc->pkc/dot_general | solution.py:36
  449.0 18.6 %fusion.137 = f32[1,1024,192]{1,2,0:T(8,128)} fusion(f32[1,1024,3,192]{1,3,2,0:T(8,128)S(1)} %add_bitcast_fusion.2), kind=kOutput, calls=%fused_computation.237 | convolution fusion | flops 1223688192 | bytes 1572864 | tf_op jit(solution)/shard_map/kt,ptc->pkc/dot_general | solution.py:38
  467.6 18.2 %fusion.141 = f32[1,1024,192]{1,2,0:T(8,128)} fusion(f32[1,1024,3,192]{1,3,2,0:T(8,128)S(1)} %add_bitcast_fusion.2), kind=kOutput, calls=%fused_computation.241 | convolution fusion | flops 1223688192 | bytes 1572864 | tf_op jit(solution)/shard_map/kt,ptc->pkc/dot_general | solution.py:37
  543.6 34.2 %reduce-scatter.13.cloned.1.call-done = bf16[1024,192]{0,1:T(8,128)(2,1)} async-done(((bf16[1024,768]{0,1:T(8,128)(2,1)}), bf16[1024,192]{0,1:T(8,128)(2,1)}) %reduce-scatter.13.cloned.1.call-update) | async-done | bytes 393232 | tf_op jit(solution)/shard_map/reduce_scatter | solution.py:91
  602.6 35.4 %all-gather.15.cloned.1.call-done = bf16[1024,768]{0,1:T(8,128)(2,1)} async-done(((bf16[1024,192]{0,1:T(8,128)(2,1)}), bf16[1024,768]{0,1:T(8,128)(2,1)}) %all-gather.15.cloned.1.call-update) | async-done | bytes 1572880 | tf_op jit(solution)/shard_map/all_gather | solution.py:87
  642.9 32.7 %all-gather.17.cloned.1.call-done = bf16[1024,768]{0,1:T(8,128)(2,1)} async-done(((bf16[1024,192]{0,1:T(8,128)(2,1)}), bf16[1024,768]{0,1:T(8,128)(2,1)}) %all-gather.17.cloned.1.call-update) | async-done | bytes 1572880 | tf_op jit(solution)/shard_map/all_gather | solution.py:97
  694.2 34.3 %reduce-scatter.17.cloned.1.call-done = bf16[1024,192]{0,1:T(8,128)(2,1)} async-done(((bf16[1024,768]{0,1:T(8,128)(2,1)}), bf16[1024,192]{0,1:T(8,128)(2,1)}) %reduce-scatter.17.cloned.1.call-update) | async-done | bytes 393232 | tf_op jit(solution)/shard_map/reduce_scatter | solution.py:101
  746.0 34.3 %all-gather.19.cloned.1.call-done = bf16[1024,768]{0,1:T(8,128)(2,1)} async-done(((bf16[1024,192]{0,1:T(8,128)(2,1)}), bf16[1024,768]{0,1:T(8,128)(2,1)}) %all-gather.19.cloned.1.call-update) | async-done | bytes 1572880 | tf_op jit(solution)/shard_map/all_gather | solution.py:97
  878.7 18.1 %fusion.149 = f32[1,1024,1,192]{1,3,2,0:T(8,128)S(1)} fusion(f32[192,1024]{1,0:T(8,128)S(1)} %fusion.26, f32[192,1024]{1,0:T(8,128)S(1)} %bitcast.835), kind=kOutput, calls=%fused_computation.249 | convolution fusion | flops 1223884800 | bytes 2359296 | tf_op jit(solution)/shard_map/transpose(jvp(kt,ptc->pkc))/dot_general | solution.py:36
  911.2 30.2 %reduce-scatter.19.cloned.1.call-done = bf16[1024,192]{0,1:T(8,128)(2,1)} async-done(((bf16[1024,768]{0,1:T(8,128)(2,1)}), bf16[1024,192]{0,1:T(8,128)(2,1)}) %reduce-scatter.19.cloned.1.call-update) | async-done | bytes 393232 | tf_op jit(solution)/shard_map/reduce_scatter | solution.py:101
  953.4 24.6 %reduce-scatter.15.cloned.1.call-done = bf16[1024,192]{0,1:T(8,128)(2,1)} async-done(((bf16[1024,768]{0,1:T(8,128)(2,1)}), bf16[1024,192]{0,1:T(8,128)(2,1)}) %reduce-scatter.15.cloned.1.call-update) | async-done | bytes 393232 | tf_op jit(solution)/shard_map/reduce_scatter | solution.py:91
  981.1 36.0 %all-gather.21.cloned.1.call-done = bf16[1024,768]{0,1:T(8,128)(2,1)} async-done(((bf16[1024,192]{0,1:T(8,128)(2,1)}), bf16[1024,768]{0,1:T(8,128)(2,1)}) %all-gather.21.cloned.1.call-update) | async-done | bytes 1572880 | tf_op jit(solution)/shard_map/all_gather | solution.py:97
  1034.4 29.8 %reduce-scatter.21.cloned.1.call-done = bf16[1024,192]{0,1:T(8,128)(2,1)} async-done(((bf16[1024,768]{0,1:T(8,128)(2,1)}), bf16[1024,192]{0,1:T(8,128)(2,1)}) %reduce-scatter.21.cloned.1.call-update) | async-done | bytes 393232 | tf_op jit(solution)/shard_map/reduce_scatter | solution.py:101
  1213.3 18.1 %fusion.153 = f32[1,1024,1,192]{1,3,2,0:T(8,128)S(1)} fusion(f32[192,1024]{1,0:T(8,128)S(1)} %fusion.23, f32[192,1024]{1,0:T(8,128)S(1)} %bitcast.836), kind=kOutput, calls=%fused_computation.253 | convolution fusion | flops 1223884800 | bytes 2359296 | tf_op jit(solution)/shard_map/transpose(jvp(kt,ptc->pkc))/dot_general | solution.py:36
  1278.2 24.8 %all-reduce.32 = (bf16[2,3,3,192]{3,2,1,0:T(4,128)(2,1)S(1)}, bf16[2,192]{1,0:T(2,128)(2,1)S(1)}, bf16[2,192]{1,0:T(2,128)(2,1)S(1)}) all-reduce(bf16[2,3,3,192]{3,2,1,0:T(4,128)(2,1)S(1)} %pad_maximum_fusion.8, bf16[2,192]{1,0:T(2,128)(2,1)S(1)} %pad_maximum_fusion.9, ...), channel_id=1, replica_groups=mesh['dp'=8,'chan'=4] {'dp'}, use_global_device_ids=true, to_apply=%region_50.51 | all-reduce | flops 4224 | bytes 16896 | tf_op jit(solution)/shard_map/psum | solution.py:247
  1317.6 126.3 %all-reduce.36.cloned.1.call-done = (bf16[2,768,3,192]{1,3,2,0:T(8,128)(2,1)}, bf16[2,3,128,128]{3,2,1,0:T(8,128)(2,1)}, bf16[2,3,128,128]{3,2,1,0:T(8,128)(2,1)...) async-done(((bf16[2,768,3,192]{1,3,2,0:T(8,128)(2,1)}, ...) | async-done | bytes 11403280 | tf_op jit(solution)/shard_map/psum | solution.py:246
  (575 shorter events, 688.2 us)
Async XLA Ops:
  7.2 64.4 %all-gather.9.cloned.1.call-start = ((), (), s32[]{:S(2)}) async-start(), calls=%async_computation.8 | async-start | bytes 1966080 | tf_op jit(solution)/shard_map/all_gather | solution.py:87
  32.2 337.3 %copy-start.138 = (f32[1,192]{1,0:T(1,128)}, f32[1,192]{1,0:T(1,128)S(1)}, u32[]{:S(2)}) copy-start(f32[1,192]{1,0:T(1,128)S(1)} %get-tuple-element.114) | copy-start | bytes 2308
  34.7 202.6 %reduce-scatter.9.cloned.1.call-start = ((), (), s32[]{:S(2)}) async-start(), calls=%async_computation.9 | async-start | bytes 1966080 | tf_op jit(solution)/shard_map/reduce_scatter | solution.py:91
  203.0 93.5 %all-gather.11.cloned.1.call-start = ((), (), s32[]{:S(2)}) async-start(), calls=%async_computation.10 | async-start | bytes 1966080 | tf_op jit(solution)/shard_map/all_gather | solution.py:87
  203.6 96.2 %copy-start.130 = (f32[1,192]{1,0:T(1,128)}, f32[1,192]{1,0:T(1,128)S(1)}, u32[]{:S(2)}) copy-start(f32[1,192]{1,0:T(1,128)S(1)} %get-tuple-element.113) | copy-start | bytes 2308
  260.3 89.1 %reduce-scatter.11.cloned.1.call-start = ((), (), s32[]{:S(2)}) async-start(), calls=%async_computation.11 | async-start | bytes 1966080 | tf_op jit(solution)/shard_map/reduce_scatter | solution.py:91
  315.1 91.5 %all-gather.13.cloned.1.call-start = ((), (), s32[]{:S(2)}) async-start(), calls=%async_computation.12 | async-start | bytes 1966080 | tf_op jit(solution)/shard_map/all_gather | solution.py:87
  370.4 207.5 %reduce-scatter.13.cloned.1.call-start = ((), (), s32[]{:S(2)}) async-start(), calls=%async_computation.13 | async-start | bytes 1966080 | tf_op jit(solution)/shard_map/reduce_scatter | solution.py:91
  543.6 94.5 %all-gather.15.cloned.1.call-start = ((), (), s32[]{:S(2)}) async-start(), calls=%async_computation.14 | async-start | bytes 1966080 | tf_op jit(solution)/shard_map/all_gather | solution.py:87
  601.8 73.8 %all-gather.17.cloned.1.call-start = ((), (), s32[]{:S(2)}) async-start(), calls=%async_computation.16 | async-start | bytes 1966080 | tf_op jit(solution)/shard_map/all_gather | solution.py:97
  602.6 125.9 %reduce-scatter.17.cloned.1.call-start = ((), (), s32[]{:S(2)}) async-start(), calls=%async_computation.17 | async-start | bytes 1966080 | tf_op jit(solution)/shard_map/reduce_scatter | solution.py:101
  694.2 86.1 %all-gather.19.cloned.1.call-start = ((), (), s32[]{:S(2)}) async-start(), calls=%async_computation.18 | async-start | bytes 1966080 | tf_op jit(solution)/shard_map/all_gather | solution.py:97
  744.9 196.6 %reduce-scatter.19.cloned.1.call-start = ((), (), s32[]{:S(2)}) async-start(), calls=%async_computation.19 | async-start | bytes 1966080 | tf_op jit(solution)/shard_map/reduce_scatter | solution.py:101
  907.2 70.8 %reduce-scatter.15.cloned.1.call-start = ((), (), s32[]{:S(2)}) async-start(), calls=%async_computation.15 | async-start | bytes 1966080 | tf_op jit(solution)/shard_map/reduce_scatter | solution.py:91
  911.1 66.9 %copy-start.4 = (f32[1024,192]{0,1:T(8,128)S(1)}, f32[1024,192]{0,1:T(8,128)}, u32[]{:S(2)}) copy-start(f32[1024,192]{0,1:T(8,128)} %get-tuple-element.68) | copy-start | bytes 2359300
  911.1 66.9 %copy-start.39 = (bf16[1024,192]{0,1:T(8,128)(2,1)S(1)}, bf16[1024,192]{0,1:T(8,128)(2,1)}, u32[]{:S(2)}) copy-start(bf16[1024,192]{0,1:T(8,128)(2,1)} %reduce-scatter.17.cloned.1.call-done) | copy-start | bytes 1179652
  911.1 66.9 %copy-start.123 = (f32[1024]{0:T(1024)S(1)}, f32[1024]{0:T(1024)}, u32[]{:S(2)}) copy-start(f32[1024]{0:T(1024)} %copy-done.122) | copy-start | bytes 12292
  911.1 66.9 %copy-start.129 = (f32[1,192]{1,0:T(1,128)S(1)}, f32[1,192]{1,0:T(1,128)}, u32[]{:S(2)}) copy-start(f32[1,192]{1,0:T(1,128)} %get-tuple-element.112) | copy-start | bytes 2308
  911.1 66.9 %copy-start.135 = (f32[1024]{0:T(1024)S(1)}, f32[1024]{0:T(1024)}, u32[]{:S(2)}) copy-start(f32[1024]{0:T(1024)} %get-tuple-element.50) | copy-start | bytes 12292
  911.2 106.0 %all-gather.21.cloned.1.call-start = ((), (), s32[]{:S(2)}) async-start(), calls=%async_computation.20 | async-start | bytes 1966080 | tf_op jit(solution)/shard_map/all_gather | solution.py:97
  980.9 83.3 %reduce-scatter.21.cloned.1.call-start = ((), (), s32[]{:S(2)}) async-start(), calls=%async_computation.21 | async-start | bytes 1966080 | tf_op jit(solution)/shard_map/reduce_scatter | solution.py:101
  1030.0 83.7 %all-gather.23.cloned.1.call-start = ((), (), s32[]{:S(2)}) async-start(), calls=%async_computation.22 | async-start | bytes 1966080 | tf_op jit(solution)/shard_map/all_gather | solution.py:97
  1078.3 198.6 %reduce-scatter.23.cloned.1.call-start = ((), (), s32[]{:S(2)}) async-start(), calls=%async_computation.23 | async-start | bytes 1966080 | tf_op jit(solution)/shard_map/reduce_scatter | solution.py:101
  1242.5 201.4 %all-reduce.36.cloned.1.call-start = ((), (), s32[]{:S(2)}) async-start(), calls=%async_computation.24 | async-start | bytes 22806528 | tf_op jit(solution)/shard_map/psum | solution.py:246
  (177 other events, 2028.9 us)
Sparse Core Ops, SparseCore 0:
  34.8 36.7 all-gather.8
  203.1 34.1 reduce-scatter.8
  260.5 36.0 all-gather.10
  315.2 34.1 reduce-scatter.10
  370.5 36.0 all-gather.12
  543.7 34.1 reduce-scatter.12
  601.9 36.0 all-gather.14
  639.6 35.9 all-gather.16
  694.3 34.1 reduce-scatter.16
  745.0 35.2 all-gather.18
  907.3 34.1 reduce-scatter.18
  943.6 34.3 reduce-scatter.14
  981.0 36.0 all-gather.20
  1030.1 34.1 reduce-scatter.20
  1078.4 35.2 all-gather.22
  1242.7 34.1 reduce-scatter.22
  1282.7 161.1 all-reduce.35
where the time goes:
time: 1480 us; the launch traced here: 1470 us
  waiting for transfers between devices  613 us (41%)
  matrix products  560 us (38%)
  blocking collectives  144 us (10%)
  other arithmetic  86.4 us (6%)
  local copies, waits for them, and re-layouts  45.5 us (3%)
  between operations  16.7 us (1%)
    all_gather x4, waiting for transfers between devices, gather_feats(): return lax.all_gather(normed_low, 'chan', axis=1, tiled=True)  140 us
    reduce_scatter x4, waiting for transfers between devices, reduce_rows(): lax.psum_scatter(partial_rows.astype(jnp.bfloat16), 'chan', scatter_dimen...  127 us
    psum x1, waiting for transfers between devices, on_device(): lax.psum(stacked[1].astype(jnp.bfloat16), 'dp').astype(jnp.float32)  126 us
    all_gather x4, waiting for transfers between devices, gather_grads(): return lax.all_gather(grad_low, 'chan', axis=1, tiled=True)  116 us
    reduce_scatter x4, waiting for transfers between devices, reduce_grads(): lax.psum_scatter(partial_grads.astype(jnp.bfloat16), 'chan', scatter_dime...  103 us
    dot_general x4, matrix products, mix_core(): jnp.einsum('kt,ptc->pkc', sine, cond_part, precision=TRANSFORM_PRECISION)  73.2 us
    dot_general x4, matrix products, mix_core(): jnp.einsum('kt,ptc->pkc', sine, value_part, precision=TRANSFORM_PRECISION)  71.9 us
    dot_general x4, matrix products, mix_core(): jnp.einsum('kt,ptc->pkc', cosine, cond_part, precision=TRANSFORM_PRECISION)  71.4 us
  transfers between devices with their start and end apart: 17, of which 17 were waited for; matrix products, arithmetic and copies ran while one was open for 5% of the time, Pallas kernels for 0%

commit v1 on v0

v1 whole, which is shorter than its diff:
```python
import functools
import math
from types import SimpleNamespace

import jax
import jax.numpy as jnp
import numpy as np
from jax import lax
from jax.experimental import pallas as pl
from jax.experimental.pallas import tpu as pltpu
from jax.sharding import Mesh
from jax.sharding import PartitionSpec as P

EPSILON = 1e-05
BF = jnp.bfloat16
F32 = jnp.float32


def dft_tables(length):
    positions = np.arange(length)
    angles = (positions[:, None] * positions[None, :] % length) * (2.0 * math.pi / length)
    scale = 1.0 / math.sqrt(length)
    cosine = np.asarray(np.cos(angles) * scale, dtype=np.float32)
    sine = np.asarray(-np.sin(angles) * scale, dtype=np.float32)
    return jnp.asarray(cosine, BF), jnp.asarray(sine, BF)


def normal_cdf(x):
    return 0.5 * (1.0 + lax.erf(x * (2.0**-0.5)))


def normal_pdf(x):
    return jnp.exp(-0.5 * x * x) * (1.0 / math.sqrt(2.0 * math.pi))


MESH = pl.DeviceIdType.MESH
VMEM_LIMIT = 58 << 20
CHUNKS = 2
PARTS = 8


def nt_dot(a, b):
    return lax.dot_general(a, b, (((1,), (1,)), ((), ())), preferred_element_type=F32)


def tn_dot(a, b):
    return lax.dot_general(a, b, (((0,), (0,)), ((), ())), preferred_element_type=F32)


def nn_dot(a, b):
    return jnp.dot(a, b, preferred_element_type=F32)


def aligned(index, size):
    return pl.ds(pl.multiple_of(index * size, size), size)


class Place:
    def __init__(self):
        self.col = lax.axis_index("col")
        self.half = lax.axis_index("half")
        self.chan = lax.axis_index("chan")
        odd = lax.rem(self.chan, 2)
        self.pack = self.chan // 2
        self.own = self.half == self.pack
        self.other_half = 1 - self.half
        self.near_chan = self.chan + 1 - 2 * odd
        self.far_chan = self.chan + 2 - 4 * self.pack
        self.rank = 2 * self.half + odd
        flip_near, flip_peer = 1 - 2 * odd, 2 - 4 * self.half
        self.ranks = [
            self.rank,
            self.rank + flip_near,
            self.rank + flip_peer,
            self.rank + flip_near + flip_peer,
        ]

    def col_at(self, step):
        return lax.rem(self.col + step, 4)

    def barrier(self):
        sem = pltpu.get_barrier_semaphore()
        devices = [{"col": self.col_at(j)} for j in range(1, 4)]
        for i in range(1, 8):
            half = self.half if i < 4 else self.other_half
            devices.append({"half": half, "chan": lax.rem(self.chan + i, 4)})
        for device in devices:
            pl.semaphore_signal(sem, inc=1, device_id=device, device_id_type=MESH)
        pl.semaphore_wait(sem, len(devices))


def remote(src, dst, send_sem, recv_sem, device):
    return pltpu.make_async_remote_copy(
        src_ref=src,
        dst_ref=dst,
        send_sem=send_sem,
        recv_sem=recv_sem,
        device_id=device,
        device_id_type=MESH,
    )


def await_recv(ref, recv_sem, send_sem):
    remote(ref, ref, send_sem, recv_sem, {"half": 1 - lax.axis_index("half")}).wait_recv()


def await_send(ref, send_sem, recv_sem):
    remote(ref, ref, send_sem, recv_sem, {"half": 1 - lax.axis_index("half")}).wait_send()


class Group:
    def __init__(self, place, r, rows):
        self.place = place
        self.near = {"chan": place.near_chan}
        self.peer = {"half": place.other_half}
        self.send, self.recv = r.group_send, r.group_recv
        self.to_peer, self.from_peer = r.to_peer, r.from_peer
        self.to_near, self.from_near = r.to_near, r.from_near
        self.rows, self.size = rows, rows // CHUNKS
        self.started = []

    @staticmethod
    def scratch(rows, width):
        return dict(
            group_send=pltpu.SemaphoreType.DMA((6, CHUNKS)),
            group_recv=pltpu.SemaphoreType.DMA((6, CHUNKS)),
            to_peer=pltpu.VMEM((2, rows, width), BF),
            from_peer=pltpu.VMEM((2, rows, width), BF),
            to_near=pltpu.VMEM((rows, width), BF),
            from_near=pltpu.VMEM((rows, width), BF),
        )

    def at(self, which, chunk=None):
        start = self.place.ranks[which] * self.rows
        if chunk is None:
            return pl.ds(pl.multiple_of(start, self.rows), self.rows)
        return pl.ds(pl.multiple_of(start + chunk * self.size, self.size), self.size)

    def start(self, src, dst, kind, chunk, device):
        copy = remote(src, dst, self.send.at[kind, chunk], self.recv.at[kind, chunk], device)
        copy.start()
        self.started.append(copy)

    def arrived(self, ref, kind, chunk):
        await_recv(ref, self.recv.at[kind, chunk], self.send.at[kind, chunk])

    def gather_start(self, full):
        for chunk in range(CHUNKS):
            own = full.at[self.at(0, chunk)]
            self.start(own, own, 0, chunk, self.near)
        for chunk in range(CHUNKS):
            own = full.at[self.at(0, chunk)]
            self.start(own, own, 1, chunk, self.peer)

    def gather_peer(self, full):
        for chunk in range(CHUNKS):
            self.arrived(full.at[self.at(2, chunk)], 1, chunk)

    def gather_near(self, full, chunk):
        piece = full.at[self.at(1, chunk)]
        self.arrived(piece, 0, chunk)
        self.start(piece, piece, 2, chunk, self.peer)

    def gather_diagonal(self, full, chunk):
        self.arrived(full.at[self.at(3, chunk)], 2, chunk)

    def piece(self, chunk):
        return pl.ds(chunk * self.size, self.size)

    def reduce_peer(self, slot, chunk, value):
        at = self.piece(chunk)
        self.to_peer[slot, at] = value.astype(BF)
        self.start(self.to_peer.at[slot, at], self.from_peer.at[slot, at], 3 + slot, chunk, self.peer)

    def reduce_near(self, chunk, value):
        at = self.piece(chunk)
        self.arrived(self.from_peer.at[1, at], 4, chunk)
        self.to_near[at] = (value + self.from_peer[1, at].astype(F32)).astype(BF)
        self.start(self.to_near.at[at], self.from_near.at[at], 5, chunk, self.near)

    def reduce_end(self, chunk):
        at = self.piece(chunk)
        self.arrived(self.from_peer.at[0, at], 3, chunk)
        self.arrived(self.from_near.at[at], 5, chunk)
        return self.from_peer[0, at].astype(F32) + self.from_near[at].astype(F32)

    def reduce_whole(self, kind, part):
        for chunk in range(CHUNKS):
            value = part[chunk * self.size : (chunk + 1) * self.size]
            if kind == "near":
                self.reduce_near(chunk, value)
            else:
                self.reduce_peer({"peer": 0, "diagonal": 1}[kind], chunk, value)

    def finish(self):
        for copy in self.started:
            copy.wait_send()


class Fetch:
    def __init__(self, place, r, pairs):
        self.place, self.pairs = place, pairs
        self.send, self.recv = r.fetch_send, r.fetch_recv

    @staticmethod
    def scratch(count):
        return dict(
            fetch_send=pltpu.SemaphoreType.DMA((count, 7)),
            fetch_recv=pltpu.SemaphoreType.DMA((count, 8)),
        )

    def cut(self, ref, axis, parts, index):
        at = aligned(index, ref.shape[axis] // parts)
        return ref.at[(slice(None),) * axis + (at,)]

    def index(self, parts, col, half):
        return col * 2 + half if parts == 8 else col

    def start(self):
        p = self.place
        owner = {"half": p.pack, "chan": p.far_chan}

        for a, (src, dst, axis, parts) in enumerate(self.pairs):

            def send(a=a, src=src, dst=dst, axis=axis, parts=parts):
                index = self.index(parts, p.col, p.half)
                remote(
                    self.cut(src, axis, parts, index),
                    self.cut(dst, axis, parts, index),
                    self.send.at[a, 0],
                    self.recv.at[a, p.half if parts == 8 else 0],
                    owner,
                ).start()

            if parts == 8:
                send()
            else:
                pl.when(p.half == 0)(send)

    def forward(self):
        p = self.place

        @pl.when(jnp.logical_not(p.own))
        def _():
            for a, (src, dst, axis, parts) in enumerate(self.pairs):
                for s in range(parts // 4):
                    piece = self.cut(dst, axis, parts, self.index(parts, p.col, s))
                    await_recv(piece, self.recv.at[a, s], self.send.at[a, 0])
                    for j in range(1, 4):
                        remote(
                            piece,
                            piece,
                            self.send.at[a, 2 * j - 1 + s],
                            self.recv.at[a, 2 * j + s],
                            {"col": p.col_at(j)},
                        ).start()

    def finish(self):
        p = self.place
        for a, (src, dst, axis, parts) in enumerate(self.pairs):

            def sent(a=a, src=src, axis=axis, parts=parts):
                piece = self.cut(src, axis, parts, self.index(parts, p.col, p.half))
                await_send(piece, self.send.at[a, 0], self.recv.at[a, 0])

            if parts == 8:
                sent()
            else:
                pl.when(p.half == 0)(sent)

        @pl.when(jnp.logical_not(p.own))
        def _():
            for a, (src, dst, axis, parts) in enumerate(self.pairs):
                for s in range(parts // 4):
                    for j in range(1, 4):
                        piece = self.cut(dst, axis, parts, self.index(parts, p.col_at(4 - j), s))
                        await_recv(piece, self.recv.at[a, 2 * j + s], self.send.at[a, 0])
                        await_send(piece, self.send.at[a, 2 * j - 1 + s], self.recv.at[a, 0])


class Load:
    def __init__(self, place, r, sources):
        self.place, self.sources, self.sem = place, sources, r.load_sem

    @staticmethod
    def scratch(count):
        return dict(load_sem=pltpu.SemaphoreType.DMA((count,)))

    def start(self):
        p = self.place

        @pl.when(p.own)
        def _():
            for a, (own, fetched, to) in enumerate(self.sources):
                pltpu.make_async_copy(own, to, self.sem.at[a]).start()

        @pl.when(jnp.logical_not(p.own))
        def _():
            for a, (own, fetched, to) in enumerate(self.sources):
                pltpu.make_async_copy(fetched, to, self.sem.at[a]).start()

    def finish(self, which=None):
        for a in range(len(self.sources)) if which is None else which:
            own, fetched, to = self.sources[a]
            pltpu.make_async_copy(fetched, to, self.sem.at[a]).wait()


class Exchange:
    def __init__(self, place, r, src, dst):
        self.place, self.src, self.dst = place, src, dst
        self.send, self.recv, self.local = r.ex_send, r.ex_recv, r.ex_local
        self.size = src.shape[0] // 4

    @staticmethod
    def scratch():
        return dict(
            ex_send=pltpu.SemaphoreType.DMA((4,)),
            ex_recv=pltpu.SemaphoreType.DMA((4,)),
            ex_local=pltpu.SemaphoreType.DMA,
        )

    def each(self, act, act_self):
        p = self.place
        for j in range(4):
            chan = 2 * p.half + j % 2
            mine = (p.half == j // 2) & (p.chan == chan)
            src, dst = self.src.at[pl.ds(j * self.size, self.size)], self.dst.at[p.chan]

            def go(j=j, chan=chan, src=src, dst=dst):
                act(
                    remote(
                        src, dst, self.send.at[j], self.recv.at[p.chan],
                        {"half": j // 2, "chan": chan},
                    )
                )

            def stay(src=src, dst=dst):
                act_self(pltpu.make_async_copy(src, dst, self.local))

            pl.when(jnp.logical_not(mine))(go)
            pl.when(mine)(stay)

    def start(self):
        self.each(lambda c: c.start(), lambda c: c.start())

    def finish(self):
        p = self.place
        self.each(lambda c: c.wait_send(), lambda c: c.wait())
        for j in range(4):

            def wait(j=j):
                await_recv(self.dst.at[j], self.recv.at[j], self.send.at[0])

            pl.when(jnp.logical_not(p.own & (p.chan == j)))(wait)


class Return:
    def __init__(self, place, r, src, dst):
        self.place, self.src, self.dst = place, src, dst
        self.send, self.recv, self.local = r.back_send, r.back_recv, r.back_local
        self.size = src.shape[1]

    @staticmethod
    def scratch():
        return dict(
            back_send=pltpu.SemaphoreType.DMA((4,)),
            back_recv=pltpu.SemaphoreType.DMA((4,)),
            back_local=pltpu.SemaphoreType.DMA,
        )

    def each(self, act, act_self):
        p = self.place
        for j in range(4):
            mine = p.own & (p.chan == j)
            src, dst = self.src.at[j], self.dst.at[aligned(p.rank, self.size)]

            def go(j=j, src=src, dst=dst):
                act(
                    remote(
                        src, dst, self.send.at[j], self.recv.at[p.rank],
                        {"half": p.pack, "chan": j},
                    )
                )

            def stay(src=src, dst=dst):
                act_self(pltpu.make_async_copy(src, dst, self.local))

            pl.when(jnp.logical_not(mine))(go)
            pl.when(mine)(stay)

    def start(self):
        self.each(lambda c: c.start(), lambda c: c.start())

    def finish(self):
        p = self.place
        self.each(lambda c: c.wait_send(), lambda c: c.wait())
        for j in range(4):
            mine = (p.half == j // 2) & (p.chan == 2 * p.half + j % 2)

            def wait(j=j):
                await_recv(
                    self.dst.at[pl.ds(j * self.size, self.size)], self.recv.at[j], self.send.at[0]
                )

            pl.when(jnp.logical_not(mine))(wait)


class Scatter:
    def __init__(self, place, r, sources, totals):
        self.place, self.sources, self.totals = place, sources, totals
        self.r = r
        self.got = [getattr(r, f"sc_got{a}") for a in range(len(sources))]
        self.part = [getattr(r, f"sc_part{a}") for a in range(len(sources))]
        self.cross = [getattr(r, f"sc_cross{a}") for a in range(len(sources))]

    @staticmethod
    def scratch(shapes):
        n = len(shapes)
        out = dict(
            sc_send=pltpu.SemaphoreType.DMA((n, 5)),
            sc_recv=pltpu.SemaphoreType.DMA((n, 5)),
            sc_local=pltpu.SemaphoreType.DMA((n, 2)),
        )
        for a, (rows, width) in enumerate(shapes):
            out[f"sc_got{a}"] = pltpu.VMEM((4, rows // 4, width), BF)
            out[f"sc_part{a}"] = pltpu.VMEM((2, rows // 8, width), BF)
            out[f"sc_cross{a}"] = pltpu.VMEM((3, rows // 8, width), BF)
        return out

    def first(self, a, j):
        p, src = self.place, self.sources[a]
        return remote(
            src.at[aligned(p.col_at(j), src.shape[0] // 4)],
            self.got[a].at[j],
            self.r.sc_send.at[a, j - 1],
            self.r.sc_recv.at[a, j - 1],
            {"col": p.col_at(j)},
        )

    def kept(self, a):
        src = self.sources[a]
        return pltpu.make_async_copy(
            src.at[aligned(self.place.col, src.shape[0] // 4)],
            self.got[a].at[0],
            self.r.sc_local.at[a, 0],
        )

    def start(self, which=None):
        for a in range(len(self.sources)) if which is None else which:
            for j in range(1, 4):
                self.first(a, j).start()
            self.kept(a).start()

    def second(self, a, slot, part, half, chan):
        return remote(
            self.part[a].at[part],
            self.cross[a].at[slot],
            self.r.sc_send.at[a, 3 + slot],
            self.r.sc_recv.at[a, 3 + slot],
            {"half": half, "chan": chan},
        )

    def middle(self):
        p = self.place
        for a in range(len(self.sources)):
            self.kept(a).wait()
            for j in range(1, 4):
                self.first(a, j).wait()
            rows = self.part[a].shape[1]
            for s in range(2):
                at = pl.ds(s * rows, rows)
                got = self.got[a]
                total = (got[0, at].astype(F32) + got[1, at].astype(F32)) + (
                    got[2, at].astype(F32) + got[3, at].astype(F32)
                )
                self.part[a][s] = total.astype(BF)

            @pl.when(p.own)
            def _():
                self.second(a, 0, p.other_half, p.other_half, p.chan).start()

            @pl.when(jnp.logical_not(p.own))
            def _():
                self.second(a, 0, p.half, p.half, p.far_chan).start()
                self.second(a, 1, p.other_half, p.other_half, p.far_chan).start()

    def finish(self):
        p = self.place
        for a in range(len(self.sources)):
            cross = self.cross[a]
            await_recv(cross.at[0], self.r.sc_recv.at[a, 3], self.r.sc_send.at[a, 3])
            await_send(cross.at[0], self.r.sc_send.at[a, 3], self.r.sc_recv.at[a, 3])

            @pl.when(p.own)
            def _():
                self.totals[a][...] = (
                    cross[0].astype(F32) + self.part[a][p.half].astype(F32)
                ).astype(BF)

            @pl.when(jnp.logical_not(p.own))
            def _():
                await_recv(cross.at[1], self.r.sc_recv.at[a, 4], self.r.sc_send.at[a, 4])
                await_send(cross.at[1], self.r.sc_send.at[a, 4], self.r.sc_recv.at[a, 4])
                self.totals[a][...] = (cross[0].astype(F32) + cross[1].astype(F32)).astype(BF)


class Spread:
    def __init__(self, place, r, totals, results):
        self.place, self.totals, self.results, self.r = place, totals, results, r

    @staticmethod
    def scratch(count):
        return dict(
            sp_send=pltpu.SemaphoreType.DMA((count, 7)),
            sp_recv=pltpu.SemaphoreType.DMA((count, 7)),
            sp_local=pltpu.SemaphoreType.DMA((count,)),
        )

    def each(self, which):
        return range(len(self.totals)) if which is None else which

    def slot(self, a, col, half):
        result = self.results[a]
        return result.at[aligned(col * 2 + half, result.shape[0] // 8)]

    def local(self, a):
        p = self.place
        return pltpu.make_async_copy(
            self.totals[a], self.slot(a, p.col, p.half), self.r.sp_local.at[a]
        )

    def out(self, a, j):
        p = self.place
        device = {"col": p.col_at(j)} if j else {"half": p.other_half}
        return remote(
            self.totals[a],
            self.slot(a, p.col, p.half),
            self.r.sp_send.at[a, j],
            self.r.sp_recv.at[a, j],
            device,
        )

    def pass_on(self, a, j):
        p = self.place
        piece = self.slot(a, p.col_at(4 - j), p.half)
        return remote(
            piece, piece, self.r.sp_send.at[a, 3 + j], self.r.sp_recv.at[a, 3 + j],
            {"half": p.other_half},
        )

    def start(self, which=None):
        for a in self.each(which):
            for j in (1, 2, 3, 0):
                self.out(a, j).start()
            self.local(a).start()

    def forward(self, which=None):
        p = self.place
        for a in self.each(which):
            for j in range(1, 4):
                piece = self.slot(a, p.col_at(4 - j), p.half)
                await_recv(piece, self.r.sp_recv.at[a, j], self.r.sp_send.at[a, j])
                self.pass_on(a, j).start()

    def finish(self, which=None):
        p = self.place
        for a in self.each(which):
            for j in range(4):
                self.out(a, j).wait_send()
            self.local(a).wait()
            await_recv(
                self.slot(a, p.col, p.other_half), self.r.sp_recv.at[a, 0], self.r.sp_send.at[a, 0]
            )
            for j in range(1, 4):
                self.pass_on(a, j).wait_send()
                piece = self.slot(a, p.col_at(4 - j), p.other_half)
                await_recv(piece, self.r.sp_recv.at[a, 3 + j], self.r.sp_send.at[a, 3 + j])


def call_kernel(body, ins, outs, scratch, collective_id, flops, hbm=()):
    names = list(ins) + list(outs) + list(scratch)

    def run(*refs):
        body(SimpleNamespace(**dict(zip(names, refs))))

    def spec(name):
        return pl.BlockSpec(memory_space=pl.ANY if name in hbm else pltpu.VMEM)

    results = pl.pallas_call(
        run,
        out_shape=[jax.ShapeDtypeStruct(*o) for o in outs.values()],
        in_specs=[spec(n) for n in ins],
        out_specs=[spec(n) for n in outs],
        scratch_shapes=list(scratch.values()),
        compiler_params=pltpu.CompilerParams(
            collective_id=collective_id, has_side_effects=True, vmem_limit_bytes=VMEM_LIMIT
        ),
        cost_estimate=pl.CostEstimate(flops=flops, bytes_accessed=20 << 20, transcendentals=0),
    )(*ins.values())
    return SimpleNamespace(**dict(zip(outs, results)))


def normalized(x):
    average = jnp.mean(x, 1, keepdims=True)
    centered = x - average
    variance = jnp.mean(centered * centered, 1, keepdims=True)
    inv = lax.rsqrt(variance + EPSILON)
    return centered * inv, inv


def norm_grad_rows(grad, x, gain):
    xhat, inv = normalized(x)
    gain_part = jnp.sum(grad * xhat, 0, keepdims=True)
    scaled = grad * gain
    mean_plain = jnp.mean(scaled, 1, keepdims=True)
    mean_cross = jnp.mean(scaled * xhat, 1, keepdims=True)
    return inv * (scaled - mean_plain - xhat * mean_cross), gain_part


def start_body(r):
    place = Place()
    exchange = Exchange(place, r, r.stream, r.pieces)
    fetch = Fetch(place, r, mixer_pairs(r, 0))
    length = r.seg.shape[0]
    place.barrier()
    exchange.start()
    own, other = place.own, jnp.logical_not(place.own)

    def gain_copy(j):
        chan = lax.rem(place.chan + j, 4)
        return remote(r.small, r.gain_parts.at[j], r.gain_send.at[j], r.gain_recv.at[j], {"chan": chan})

    for j in range(1, 4):
        gain_copy(j).start()
    seg_copy = remote(r.seg, r.seg_got, r.gain_send.at[4], r.gain_recv.at[4], {"half": place.other_half})
    taps_copy = remote(r.taps, r.taps_got, r.gain_send.at[5], r.gain_recv.at[5], {"chan": place.far_chan})

    @pl.when(own)
    def _():
        seg_copy.start()
        taps_copy.start()

    fetch.start()
    r.padded[0:PAD] = jnp.full((PAD, 1), -1, jnp.int32)
    r.padded[PAD + length : 2 * PAD + length] = jnp.full((PAD, 1), -1, jnp.int32)

    @pl.when(own)
    def _():
        r.padded[PAD : PAD + length] = r.seg[...]
        r.taps_out[...] = r.taps[...]
        seg_copy.wait_send()
        taps_copy.wait_send()

    @pl.when(other)
    def _():
        seg_copy.wait_recv()
        taps_copy.wait_recv()
        r.padded[PAD : PAD + length] = r.seg_got[...]
        r.taps_out[...] = r.taps_got[...]

    here = r.padded[PAD : PAD + length]
    r.mask_prev[...] = jnp.where(r.padded[PAD - 1 : PAD - 1 + length] == here, 1.0, 0.0)
    r.mask_next[...] = jnp.where(r.padded[PAD + 1 : PAD + 1 + length] == here, 1.0, 0.0)
    for j in range(1, 4):
        gain_copy(j).wait()
    r.gain_parts[0] = r.small[...]
    parts = []
    for c in range(4):
        parts.append(r.gain_parts[lax.rem(place.chan - c + 4, 4)])
    r.gains[...] = jnp.concatenate(parts, 1)
    exchange.finish()
    r.values[...] = jnp.concatenate([r.pieces[j] for j in range(4)], 1).astype(F32)
    fetch.forward()
    fetch.finish()


def mixer_pairs(r, l):
    return [
        (r.in_proj.at[l], r.n_in, 1, 8),
        (r.cond_in.at[l], r.n_ci, 1, 8),
        (r.cond_out.at[l], r.n_co, 1, 8),
        (r.out_proj.at[l], r.n_out, 0, 4),
        (r.filter_spec.at[l], r.n_spec, 1, 8),
    ]


def ffn_pairs(r, l):
    return [
        (r.gate_proj.at[l], r.n_gate, 0, 8),
        (r.up_proj.at[l], r.n_up, 0, 8),
        (r.down_proj.at[l], r.n_down, 0, 8),
    ]


SOURCES = {
    "mixer": dict(
        in_proj="in", cond_in="ci", cond_out="co", out_proj="out", filter_spec="spec"
    ),
    "ffn": dict(gate_proj="gate", up_proj="up", down_proj="down"),
}


def fetch_sources(arrays, kind):
    return {n: arrays[n] for n in SOURCES[kind]}


def fetch_results(arrays, kind):
    return {"n_" + t: (arrays[n].shape[1:], arrays[n].dtype) for n, t in SOURCES[kind].items()}


def loaded(r, l, kind, skip=()):
    return [
        (getattr(r, n).at[l], getattr(r, "f_" + t), getattr(r, "w_" + t))
        for n, t in SOURCES[kind].items()
        if t not in skip
    ]


def load_inputs(arrays, fetched, kind, skip=()):
    keep = {n: t for n, t in SOURCES[kind].items() if t not in skip}
    ins = {n: arrays[n] for n in keep}
    ins.update({"f_" + t: getattr(fetched, "n_" + t) for t in keep.values()})
    scratch = {
        "w_" + t: pltpu.VMEM(arrays[n].shape[1:], arrays[n].dtype) for n, t in keep.items()
    }
    return ins, dict(scratch, **Load.scratch(len(keep))), tuple(ins)


def begin(arrays, stream, seg, small, taps):
    length, shard = stream.shape
    rows, width = length // 4, arrays["in_proj"].shape[2]
    sources = fetch_sources(arrays, "mixer")
    gains = small.shape[0]
    return call_kernel(
        start_body,
        dict(stream=stream, seg=seg, small=small, taps=taps, **sources),
        dict(
            values=((rows, width), F32),
            gains=((gains, width), F32),
            taps_out=(taps.shape, F32),
            mask_prev=((length, 1), F32),
            mask_next=((length, 1), F32),
            **fetch_results(arrays, "mixer"),
        ),
        dict(
            pieces=pltpu.VMEM((4, rows, shard), BF),
            gain_parts=pltpu.VMEM((4, gains, shard), F32),
            gain_send=pltpu.SemaphoreType.DMA((6,)),
            gain_recv=pltpu.SemaphoreType.DMA((6,)),
            seg_got=pltpu.VMEM((length, 1), jnp.int32),
            taps_got=pltpu.VMEM(taps.shape, F32),
            padded=pltpu.VMEM((length + 2 * PAD, 1), jnp.int32),
            **Exchange.scratch(),
            **Fetch.scratch(5),
        ),
        1,
        10**6,
        ("stream",) + tuple(sources),
    )


def ffn_forward_body(l, last, r):
    place = Place()
    rows = r.mid.shape[0]
    group = Group(place, r, rows)
    load = Load(place, r, loaded(r, l, "ffn"))
    load.start()
    layers = r.gains.shape[0] // 2
    gain = r.gains[layers + l : layers + l + 1]
    xhat, _ = normalized(r.mid[...])
    r.h_all[group.at(0)] = (xhat * gain).astype(BF)
    place.barrier()
    group.gather_start(r.h_all)
    if last:
        extra = Exchange(place, r, r.cotangent, r.pieces)
    else:
        extra = Fetch(place, r, mixer_pairs(r, l + 1))
    extra.start()
    load.finish()

    def block(at):
        h = r.h_all[at]
        gate = nn_dot(h, r.w_gate[...])
        up = nn_dot(h, r.w_up[...])
        r.gate_all[at] = gate.astype(BF)
        r.up_all[at] = up.astype(BF)
        hidden = (gate * normal_cdf(gate) * up).astype(BF)
        return nn_dot(hidden, r.w_down[...])

    r.out[...] = r.mid[...] + block(group.at(0))
    group.gather_peer(r.h_all)
    group.reduce_whole("peer", block(group.at(2)))
    for chunk in range(CHUNKS):
        group.gather_near(r.h_all, chunk)
        r.near_part[group.piece(chunk)] = block(group.at(1, chunk))
        group.gather_diagonal(r.h_all, chunk)
        group.reduce_peer(1, chunk, block(group.at(3, chunk)))
        group.reduce_near(chunk, r.near_part[group.piece(chunk)])
    if not last:
        extra.forward()
    for chunk in range(CHUNKS):
        r.out[group.piece(chunk)] += group.reduce_end(chunk)
    group.finish()
    extra.finish()
    if last:
        r.carried[...] = jnp.concatenate([r.pieces[j] for j in range(4)], 1).astype(F32)


def ffn_forward(l, arrays, mid, gains, fetched, cotangent):
    rows, width = mid.shape
    units = arrays["gate_proj"].shape[2]
    full = rows * 4
    last = l + 1 == arrays["in_proj"].shape[0]
    ins, scratch, hbm = load_inputs(arrays, fetched, "ffn")
    outs = dict(
        out=((rows, width), F32),
        h_all=((full, width), BF),
        gate_all=((full, units), BF),
        up_all=((full, units), BF),
    )
    if last:
        ins.update(cotangent=cotangent)
        outs.update(carried=((rows, width), F32))
        scratch.update(
            pieces=pltpu.VMEM((4, rows, cotangent.shape[1]), BF), **Exchange.scratch()
        )
        hbm += ("cotangent",)
    else:
        sources = fetch_sources(arrays, "mixer")
        ins.update(sources)
        outs.update(fetch_results(arrays, "mixer"))
        scratch.update(Fetch.scratch(5))
        hbm += tuple(sources)
    return call_kernel(
        functools.partial(ffn_forward_body, l, last),
        dict(mid=mid, gains=gains, **ins),
        outs,
        dict(
            near_part=pltpu.VMEM((rows, width), F32), **Group.scratch(rows, width), **scratch
        ),
        10 + l,
        6 * full * width * units,
        hbm,
    )


def ffn_backward_body(l, last, r):
    place = Place()
    rows, width = r.mid.shape
    units = r.gate_all.shape[1]
    group = Group(place, r, rows)
    load = Load(place, r, loaded(r, l, "ffn"))
    load.start()
    layers = r.gains.shape[0] // 2
    gain = r.gains[layers + l : layers + l + 1]
    r.g_all[group.at(0)] = r.carried[...].astype(BF)
    if last:
        shard = r.returned.shape[1]
        for j in range(4):
            r.leaving[j] = r.values[:, j * shard : (j + 1) * shard].astype(BF)
        back = Return(place, r, r.leaving, r.returned)
    place.barrier()
    group.gather_start(r.g_all)
    if last:
        back.start()
    else:
        spread = Spread(place, r, [r.ffn_total], [r.ffn_result])
        scatter = Scatter(place, r, mixer_grads(r), mixer_totals(r))
        spread.start()
        scatter.start()

    load.finish()

    def block(at):
        hidden_grad = nt_dot(r.g_all[at], r.w_down[...])
        gate = r.gate_all[at].astype(F32)
        up = r.up_all[at].astype(F32)
        cdf = normal_cdf(gate)
        act = gate * cdf
        r.hidden_all[at] = (act * up).astype(BF)
        gate_grad = (hidden_grad * up * (cdf + gate * normal_pdf(gate))).astype(BF)
        up_grad = (hidden_grad * act).astype(BF)
        r.gate_grads[at] = gate_grad
        r.up_grads[at] = up_grad
        return nt_dot(gate_grad, r.w_gate[...]) + nt_dot(up_grad, r.w_up[...])

    r.own_part[...] = block(group.at(0))
    group.gather_peer(r.g_all)
    group.reduce_whole("peer", block(group.at(2)))
    for chunk in range(CHUNKS):
        group.gather_near(r.g_all, chunk)
        r.near_part[group.piece(chunk)] = block(group.at(1, chunk))
        group.gather_diagonal(r.g_all, chunk)
        group.reduce_peer(1, chunk, block(group.at(3, chunk)))
        group.reduce_near(chunk, r.near_part[group.piece(chunk)])
    step = 256
    for u in range(units // step):
        cols = pl.ds(u * step, step)
        r.weight_grads[0 * width : 1 * width, cols] = tn_dot(r.h_all[...], r.gate_grads[:, cols]).astype(BF)
        r.weight_grads[1 * width : 2 * width, cols] = tn_dot(r.h_all[...], r.up_grads[:, cols]).astype(BF)
        r.weight_grads[pl.ds(2 * width + u * step, step)] = tn_dot(r.hidden_all[:, cols], r.g_all[...]).astype(BF)
    if not last:
        spread.forward()
        scatter.middle()
    for chunk in range(CHUNKS):
        r.own_part[group.piece(chunk)] += group.reduce_end(chunk)
    grad, gain_part = norm_grad_rows(r.own_part[...], r.mid[...], gain)
    r.mid_grad[...] = r.carried[...] + grad
    r.gain_grad[...] = gain_part
    group.finish()
    if last:
        back.finish()
        r.output[...] = r.returned[...].astype(F32)
    else:
        spread.finish()
        scatter.finish()


def mixer_grads(r):
    return [r.g_in, r.g_spec, r.g_out, r.g_mlp, r.g_small]


def mixer_totals(r):
    return [r.t_in, r.t_spec, r.t_out, r.t_mlp, r.t_small]


def mixer_results(r):
    return [r.r_in, r.r_spec, r.r_out, r.r_mlp, r.r_small]


GRADS = ("in", "spec", "out", "mlp", "small")


def ffn_backward(l, arrays, carried, mid, gains, fetched, saved, values, shard, pending):
    rows, width = mid.shape
    units = arrays["gate_proj"].shape[2]
    full = rows * 4
    last = values is not None
    big = pltpu.VMEM((full, units), BF)
    load_ins, load_scratch, hbm = load_inputs(arrays, fetched, "ffn")
    ins = dict(carried=carried, mid=mid, gains=gains, **load_ins, **saved)
    outs = dict(
        mid_grad=((rows, width), F32),
        weight_grads=((3 * width, units), BF),
        gain_grad=((1, width), F32),
    )
    if last:
        ins.update(values=values)
        outs.update(output=((full, shard), F32))
        scratch = dict(
            leaving=pltpu.VMEM((4, rows, shard), BF),
            returned=pltpu.VMEM((full, shard), BF),
            **Return.scratch(),
        )
    else:
        grads, ffn_total = pending
        ins.update(ffn_total=ffn_total, **{"g_" + n: grads[n] for n in GRADS})
        outs.update(
            ffn_result=((8 * ffn_total.shape[0], ffn_total.shape[1]), BF),
            **totals_of(grads),
        )
        scratch = dict(**Spread.scratch(1), **Scatter.scratch([grads[n].shape for n in GRADS]))
        hbm += tuple("g_" + n for n in GRADS)
    return call_kernel(
        functools.partial(ffn_backward_body, l, last),
        ins,
        outs,
        dict(
            near_part=pltpu.VMEM((rows, width), F32),
            own_part=pltpu.VMEM((rows, width), F32),
            g_all=pltpu.VMEM((full, width), BF),
            hidden_all=big,
            gate_grads=big,
            up_grads=big,
            **Group.scratch(rows, width),
            **load_scratch,
            **scratch,
        ),
        20 + l,
        12 * full * width * units,
        hbm,
    )


def totals_of(grads):
    return {"t_" + n: ((grads[n].shape[0] // 8, grads[n].shape[1]), BF) for n in GRADS}


PAD = 8


def shifted(ref, s, tile, size, offset):
    return ref[s, pl.ds(PAD + tile * size + offset, size)]


def mlp_tables(r):
    groups, feats, inner = r.w_ci.shape
    half = feats // 2
    for table in (r.in_re, r.in_im, r.out_re, r.out_im):
        table[...] = jnp.zeros_like(table)
    for g in range(groups):
        rows, cols = pl.ds(g * half, half), pl.ds(g * inner, inner)
        r.in_re[rows, cols] = r.w_ci[g, 0:half].astype(BF)
        r.in_im[rows, cols] = r.w_ci[g, half:feats].astype(BF)
        turned = r.w_co[g].T
        r.out_re[rows, cols] = turned[0:half].astype(BF)
        r.out_im[rows, cols] = turned[half:feats].astype(BF)


def mlp_scratch(shard, inner):
    table = pltpu.VMEM((shard, inner), BF)
    return dict(in_re=table, in_im=table, out_re=table, out_im=table)


def mixer_forward_body(l, r):
    place = Place()
    rows = r.values.shape[0]
    length = r.h_all.shape[0]
    lanes = r.w_in.shape[2]
    wide = r.both.shape[1] // 2
    tiles = 4
    size = length // tiles
    group = Group(place, r, rows)
    load = Load(place, r, loaded(r, l, "mixer"))
    load.start()
    xhat, _ = normalized(r.values[...])
    r.h_all[group.at(0)] = (xhat * r.gains[l : l + 1]).astype(BF)
    place.barrier()
    group.gather_start(r.h_all)
    fetch = Fetch(place, r, ffn_pairs(r, l))
    fetch.start()
    for s in range(3):
        r.padded[s, 0:PAD] = jnp.zeros((PAD, lanes), F32)
        r.padded[s, PAD + length : 2 * PAD + length] = jnp.zeros((PAD, lanes), F32)
    r.both[...] = jnp.zeros_like(r.both)
    load.finish()
    mlp_tables(r)

    def project(which, chunk=None):
        at = group.at(which, chunk)
        h = r.h_all[at]
        for s in range(3):
            proj = nn_dot(h, r.w_in[s])
            r.padded[s, pl.ds(pl.multiple_of(at.start + PAD, 8), at.size)] = proj
            r.proj_all[s, at] = proj.astype(BF)

    project(0)
    group.gather_peer(r.h_all)
    project(2)
    for chunk in range(CHUNKS):
        group.gather_near(r.h_all, chunk)
        project(1, chunk)
        group.gather_diagonal(r.h_all, chunk)
        project(3, chunk)

    def tap(o, s):
        at = 9 * l + 3 * o + s
        return r.taps[at : at + 1]

    for t in range(tiles):
        at = pl.ds(t * size, size)
        prev = r.mask_prev[at]
        following = r.mask_next[at]
        shorts = []
        for s in range(3):
            shorts.append(
                tap(0, s) * shifted(r.padded, s, t, size, -1) * prev
                + tap(1, s) * shifted(r.padded, s, t, size, 0)
                + tap(2, s) * shifted(r.padded, s, t, size, 1) * following
            )
        r.query_all[at] = shorts[0].astype(BF)
        r.both[at, 0:lanes] = shorts[1].astype(BF)
        r.both[at, wide : wide + lanes] = shorts[2].astype(BF)

    @pl.loop(0, tiles)
    def _(t):
        at = aligned(t, size)
        real = nn_dot(r.cosine[at], r.both[...])
        imag = nn_dot(r.sine[at], r.both[...])
        value_re, cond_re = real[:, :lanes], real[:, wide : wide + lanes].astype(BF)
        value_im, cond_im = imag[:, :lanes], imag[:, wide : wide + lanes].astype(BF)
        pre = nn_dot(cond_re, r.in_re[...]) + nn_dot(cond_im, r.in_im[...])
        inner = (pre * normal_cdf(pre)).astype(BF)
        kernel_re = r.w_spec[0, at] + nt_dot(inner, r.out_re[...])
        kernel_im = r.w_spec[1, at] + nt_dot(inner, r.out_im[...])
        r.prod_re[at] = (value_re * kernel_re - value_im * kernel_im).astype(BF)
        r.prod_im[at] = (value_re * kernel_im + value_im * kernel_re).astype(BF)
        r.pre_all[at] = pre.astype(BF)
        for i, x in enumerate((value_re, value_im, kernel_re, kernel_im, cond_re, cond_im)):
            r.spectra[i, at] = x.astype(BF)

    fetch.forward()

    def project_out(which):
        at = group.at(which)
        mixed = nn_dot(r.cosine[at], r.prod_re[...]) + nn_dot(r.sine[at], r.prod_im[...])
        r.mixed_all[at] = mixed.astype(BF)
        gated = (r.query_all[at].astype(F32) * mixed).astype(BF)
        r.gated_all[at] = gated
        return nn_dot(gated, r.w_out[...])

    group.reduce_whole("diagonal", project_out(3))
    group.reduce_whole("near", project_out(1))
    group.reduce_whole("peer", project_out(2))
    r.out[...] = r.values[...] + project_out(0)
    for chunk in range(CHUNKS):
        r.out[group.piece(chunk)] += group.reduce_end(chunk)
    group.finish()
    fetch.finish()


def mixer_forward(l, arrays, values, gains, taps, masks, fetched, tables):
    rows, width = values.shape
    length, lanes = arrays["filter_spec"].shape[2:]
    groups, _, units = arrays["cond_in"].shape[1:]
    wide = -(-lanes // 128) * 128
    inner = groups * units
    ins, scratch, hbm = load_inputs(arrays, fetched, "mixer")
    sources = fetch_sources(arrays, "ffn")
    return call_kernel(
        functools.partial(mixer_forward_body, l),
        dict(
            values=values, gains=gains, taps=taps, mask_prev=masks[0], mask_next=masks[1],
            cosine=tables[0], sine=tables[1], **ins, **sources,
        ),
        dict(
            out=((rows, width), F32),
            h_all=((length, width), BF),
            proj_all=((3, length, lanes), BF),
            query_all=((length, lanes), BF),
            mixed_all=((length, lanes), BF),
            spectra=((6, length, lanes), BF),
            pre_all=((length, inner), BF),
            gated_all=((length, lanes), BF),
            **fetch_results(arrays, "ffn"),
        ),
        dict(
            padded=pltpu.VMEM((3, length + 2 * PAD, lanes), F32),
            both=pltpu.VMEM((length, 2 * wide), BF),
            prod_re=pltpu.VMEM((length, lanes), BF),
            prod_im=pltpu.VMEM((length, lanes), BF),
            **mlp_scratch(lanes, inner),
            **Group.scratch(rows, width),
            **Fetch.scratch(3),
            **scratch,
        ),
        30 + l,
        6 * 10**9,
        hbm + tuple(sources),
    )


def mixer_backward_body(l, last, r):
    place = Place()
    rows = r.values.shape[0]
    length, width = r.h_all.shape
    lanes = r.w_in.shape[2]
    groups, feats, units = r.w_ci.shape
    half = feats // 2
    wide = r.both_re.shape[1] // 2
    tiles = 4
    size = length // tiles
    group = Group(place, r, rows)
    load = Load(place, r, loaded(r, l, "mixer", ("spec",)))
    load.start()
    r.m_all[group.at(0)] = r.mid_grad[...].astype(BF)
    place.barrier()
    group.gather_start(r.m_all)
    scatter = Scatter(place, r, [r.ffn_grads], [r.ffn_total])
    scatter.start()
    if not last:
        spread = Spread(place, r, mixer_totals(r), mixer_results(r))
        spread.start()
    for s in range(3):
        r.padded[s, 0:PAD] = jnp.zeros((PAD, lanes), F32)
        r.padded[s, PAD + length : 2 * PAD + length] = jnp.zeros((PAD, lanes), F32)
    r.both_re[...] = jnp.zeros_like(r.both_re)
    r.both_im[...] = jnp.zeros_like(r.both_im)
    r.sum_in[...] = jnp.zeros_like(r.sum_in)
    r.sum_out[...] = jnp.zeros_like(r.sum_out)
    load.finish()
    mlp_tables(r)

    def gated_back(which, chunk=None):
        at = group.at(which, chunk)
        gated_grad = nt_dot(r.m_all[at], r.w_out[...])
        to = pl.ds(pl.multiple_of(at.start + PAD, 8), at.size)
        r.padded[0, to] = gated_grad * r.mixed_all[at].astype(F32)
        r.q_g[at] = (gated_grad * r.query_all[at].astype(F32)).astype(BF)

    gated_back(0)
    group.gather_peer(r.m_all)
    gated_back(2)
    for chunk in range(CHUNKS):
        group.gather_near(r.m_all, chunk)
        gated_back(1, chunk)
        group.gather_diagonal(r.m_all, chunk)
        gated_back(3, chunk)

    @pl.loop(0, tiles)
    def _(t):
        at = aligned(t, size)
        real = nn_dot(r.cosine[at], r.q_g[...])
        imag = nn_dot(r.sine[at], r.q_g[...])
        value_re, value_im, kernel_re, kernel_im = [r.spectra[i, at].astype(F32) for i in range(4)]
        kernel_re_grad = (real * value_re + imag * value_im).astype(BF)
        kernel_im_grad = (imag * value_re - real * value_im).astype(BF)
        r.both_re[at, 0:lanes] = (real * kernel_re + imag * kernel_im).astype(BF)
        r.both_im[at, 0:lanes] = (imag * kernel_re - real * kernel_im).astype(BF)
        r.g_spec[at] = kernel_re_grad
        r.g_spec[pl.ds(pl.multiple_of(length + t * size, size), size)] = kernel_im_grad
        pre = r.pre_all[at].astype(F32)
        cdf = normal_cdf(pre)
        inner = (pre * cdf).astype(BF)
        inner_grad = nn_dot(kernel_re_grad, r.out_re[...]) + nn_dot(kernel_im_grad, r.out_im[...])
        pre_grad = (inner_grad * (cdf + pre * normal_pdf(pre))).astype(BF)
        r.both_re[at, wide : wide + lanes] = nt_dot(pre_grad, r.in_re[...]).astype(BF)
        r.both_im[at, wide : wide + lanes] = nt_dot(pre_grad, r.in_im[...]).astype(BF)
        r.sum_out[0] += tn_dot(kernel_re_grad, inner)
        r.sum_out[1] += tn_dot(kernel_im_grad, inner)
        r.sum_in[0] += tn_dot(r.spectra[4, at], pre_grad)
        r.sum_in[1] += tn_dot(r.spectra[5, at], pre_grad)

    @pl.loop(0, tiles)
    def _(t):
        at = aligned(t, size)
        both = nn_dot(r.cosine[at], r.both_re[...]) + nn_dot(r.sine[at], r.both_im[...])
        to = pl.ds(pl.multiple_of(t * size + PAD, 8), size)
        r.padded[1, to] = both[:, :lanes]
        r.padded[2, to] = both[:, wide : wide + lanes]

    def tap(o, s):
        at = 9 * l + 3 * o + s
        return r.taps[at : at + 1]

    r.g_small[...] = jnp.zeros_like(r.g_small)
    totals = [[None] * 3 for _ in range(3)]
    for t in range(tiles):
        at = pl.ds(t * size, size)
        prev = r.mask_prev[at]
        following = r.mask_next[at]
        for s in range(3):
            here = shifted(r.padded, s, t, size, 0)
            after = shifted(r.padded, s, t, size, 1) * following
            before = shifted(r.padded, s, t, size, -1) * prev
            r.proj_grads[s, at] = (
                tap(0, s) * after + tap(1, s) * here + tap(2, s) * before
            ).astype(BF)
            proj = r.proj_all[s, at].astype(F32)
            for o, g in enumerate((after, here, before)):
                part = jnp.sum(g * proj, 0, keepdims=True)
                totals[o][s] = part if t == 0 else totals[o][s] + part
    small = [totals[o][s] for o in range(3) for s in range(3)]

    def feats_grad(which):
        at = group.at(which)
        return sum(nt_dot(r.proj_grads[s, at], r.w_in[s]) for s in range(3))

    group.reduce_whole("diagonal", feats_grad(3))
    group.reduce_whole("near", feats_grad(1))
    group.reduce_whole("peer", feats_grad(2))
    r.own_part[...] = feats_grad(0)
    if not last:
        spread.forward()
    for s in range(3):
        r.g_in[s * width : (s + 1) * width] = tn_dot(r.h_all[...], r.proj_grads[s]).astype(BF)
    shard = r.w_out.shape[0]
    r.g_out[0:shard] = tn_dot(r.gated_all[...], r.m_all[...]).astype(BF)
    r.g_out[shard:] = jnp.zeros((r.g_out.shape[0] - shard, width), BF)
    for g in range(groups):
        rows_at, cols = slice(g * half, (g + 1) * half), slice(g * units, (g + 1) * units)
        at = g * feats
        r.g_mlp[at : at + half] = r.sum_in[0, rows_at, cols].astype(BF)
        r.g_mlp[at + half : at + feats] = r.sum_in[1, rows_at, cols].astype(BF)
        turned = jnp.concatenate([r.sum_out[0, rows_at, cols], r.sum_out[1, rows_at, cols]], 0)
        at += groups * feats
        r.g_mlp[at : at + units] = turned.T.astype(BF)
    for chunk in range(CHUNKS):
        r.own_part[group.piece(chunk)] += group.reduce_end(chunk)
    grad, gain_part = norm_grad_rows(r.own_part[...], r.values[...], r.gains[l : l + 1])
    r.carried[...] = r.mid_grad[...] + grad
    third = width // 3
    for i in range(3):
        small.append(gain_part[:, i * third : (i + 1) * third])
    for i in range(3):
        small.append(r.gain_two[:, i * third : (i + 1) * third])
    for i, x in enumerate(small):
        r.small_rows[i : i + 1, 0 : x.shape[1]] = x
    r.g_small[0:16] = r.small_rows[...].astype(BF)
    scatter.middle()
    group.finish()
    scatter.finish()
    if not last:
        spread.finish()


def mixer_backward(
    l, arrays, mid_grad, values, gains, taps, masks, fetched, tables, saved, gain_two, ffn_grads,
    pending,
):
    rows, width = values.shape
    length, lanes = saved["query_all"].shape
    groups, feats, units = arrays["cond_in"].shape[1:]
    inner = groups * units
    wide = -(-lanes // 128) * 128
    last = pending is None
    load_ins, load_scratch, hbm = load_inputs(arrays, fetched, "mixer", ("spec",))
    ins = dict(
        mid_grad=mid_grad, values=values, gains=gains, taps=taps, mask_prev=masks[0],
        mask_next=masks[1], cosine=tables[0], sine=tables[1], gain_two=gain_two,
        ffn_grads=ffn_grads, **load_ins, **saved,
    )
    grads = dict(
        g_in=((3 * width, lanes), BF),
        g_spec=((2 * length, lanes), BF),
        g_out=((-(-lanes // 128) * 128, width), BF),
        g_mlp=((2 * groups * feats, units), BF),
        g_small=((128, width // 3), BF),
    )
    outs = dict(
        carried=((rows, width), F32),
        ffn_total=((ffn_grads.shape[0] // 8, ffn_grads.shape[1]), BF),
        **grads,
    )
    scratch = dict(Scatter.scratch([ffn_grads.shape]), **load_scratch)
    hbm += ("ffn_grads",)
    if not last:
        ins.update(**{"t_" + n: pending[n] for n in GRADS})
        outs.update(
            **{"r_" + n: ((pending[n].shape[0] * 8, pending[n].shape[1]), BF) for n in GRADS}
        )
        scratch.update(Spread.scratch(len(GRADS)))
    return call_kernel(
        functools.partial(mixer_backward_body, l, last),
        ins,
        outs,
        dict(
            m_all=pltpu.VMEM((length, width), BF),
            padded=pltpu.VMEM((3, length + 2 * PAD, lanes), F32),
            q_g=pltpu.VMEM((length, lanes), BF),
            both_re=pltpu.VMEM((length, 2 * wide), BF),
            both_im=pltpu.VMEM((length, 2 * wide), BF),
            proj_grads=pltpu.VMEM((3, length, lanes), BF),
            own_part=pltpu.VMEM((rows, width), F32),
            sum_in=pltpu.VMEM((2, lanes, inner), F32),
            sum_out=pltpu.VMEM((2, lanes, inner), F32),
            small_rows=pltpu.VMEM((16, width // 3), F32),
            **mlp_scratch(lanes, inner),
            **Group.scratch(rows, width),
            **scratch,
        ),
        40 + l,
        9 * 10**9,
        hbm,
    )


def end_body(r):
    place = Place()
    scatter = Scatter(place, r, mixer_grads(r), mixer_totals(r))
    shard = r.returned.shape[1]
    for j in range(4):
        r.leaving[j] = r.carried[:, j * shard : (j + 1) * shard].astype(BF)
    back = Return(place, r, r.leaving, r.returned)
    spread = Spread(
        place, r, mixer_totals(r) + [r.ffn_total], mixer_results(r) + [r.ffn_result]
    )
    place.barrier()
    scatter.start()
    back.start()
    spread.start([5])
    scatter.middle()
    spread.forward([5])
    scatter.finish()
    spread.start(range(5))
    back.finish()
    r.stream_grad[...] = r.returned[...].astype(F32)
    spread.forward(range(5))
    spread.finish(range(6))

    layers = r.gain_parts.shape[1]
    r.gain_parts[0, 0] = r.r_small[0:16]
    for l in range(1, layers):
        r.gain_parts[0, l] = r.above[l - 1]

    def gain_copy(j):
        chan = lax.rem(place.chan + j, 4)
        return remote(
            r.gain_parts.at[0], r.gain_parts.at[j], r.gain_send.at[j], r.gain_recv.at[j], {"chan": chan}
        )

    for j in range(1, 4):
        gain_copy(j).start()
    for j in range(1, 4):
        gain_copy(j).wait()
    total = r.gain_parts[0].astype(F32)
    for j in range(1, 4):
        total += r.gain_parts[j].astype(F32)
    r.gain_grads[...] = total


def end(carried, shard, grads, ffn_total, above):
    rows, width = carried.shape
    layers = 1 + above.shape[0]
    shapes = [grads[n].shape for n in GRADS]
    hbm = tuple("g_" + n for n in GRADS)
    return call_kernel(
        end_body,
        dict(
            carried=carried, ffn_total=ffn_total, above=above,
            **{"g_" + n: grads[n] for n in GRADS},
        ),
        dict(
            stream_grad=((rows * 4, shard), F32),
            gain_grads=((layers, 16, width // 3), F32),
            ffn_result=((8 * ffn_total.shape[0], ffn_total.shape[1]), BF),
            **{"r_" + n: (grads[n].shape, BF) for n in GRADS},
        ),
        dict(
            leaving=pltpu.VMEM((4, rows, shard), BF),
            returned=pltpu.VMEM((rows * 4, shard), BF),
            gain_parts=pltpu.VMEM((4, layers, 16, width // 3), BF),
            gain_send=pltpu.SemaphoreType.DMA((4,)),
            gain_recv=pltpu.SemaphoreType.DMA((4,)),
            **{n: pltpu.VMEM(*s) for n, s in totals_of(grads).items()},
            **Return.scratch(),
            **Scatter.scratch(shapes),
            **Spread.scratch(len(GRADS) + 1),
        ),
        50,
        10**6,
        hbm,
    )


def on_device(
    stream,
    segments,
    cotangent,
    norm_one,
    in_proj,
    short_taps,
    cond_in,
    cond_out,
    filter_spec,
    out_proj,
    norm_two,
    gate_proj,
    up_proj,
    down_proj,
):
    chan = lax.axis_index("chan")
    layers, width = in_proj.shape[:2]
    shard = norm_one.shape[1]
    length = filter_spec.shape[2]
    groups, feats = cond_in.shape[1:3]
    tables = dft_tables(length)
    arrays = dict(
        in_proj=in_proj.transpose(0, 2, 1, 3),
        cond_in=cond_in,
        cond_out=cond_out,
        filter_spec=filter_spec,
        out_proj=out_proj,
        gate_proj=gate_proj,
        up_proj=up_proj,
        down_proj=down_proj,
    )

    def kept(result, names):
        return {n: getattr(result, n) for n in names}

    first = begin(
        arrays,
        stream,
        segments[:, None],
        jnp.concatenate([norm_one, norm_two], 0),
        short_taps.reshape(-1, shard),
    )
    gains, taps = first.gains, first.taps_out
    masks = (first.mask_prev, first.mask_next)
    values = first.values
    mixer_fetched = first
    saved = []
    for l in range(layers):
        mixed = mixer_forward(l, arrays, values, gains, taps, masks, mixer_fetched, tables)
        after = ffn_forward(l, arrays, mixed.out, gains, mixed, cotangent)
        saved.append((values, mixer_fetched, mixed, after))
        values, mixer_fetched = after.out, after
    carried = after.carried

    ffn_results, mixer_results_ = {}, {}
    grads, ffn_total, output = None, None, None
    for l in reversed(range(layers)):
        layer_in, mixer_fetched, mixed, after = saved[l]
        last = l + 1 == layers
        back = ffn_backward(
            l, arrays, carried, mixed.out, gains, mixed,
            kept(after, ("h_all", "gate_all", "up_all")),
            values if last else None, shard, None if last else (grads, ffn_total),
        )
        if last:
            output, pending = back.output, None
        else:
            ffn_results[l + 1] = back.ffn_result
            pending = {n: getattr(back, "t_" + n) for n in GRADS}
        saves = kept(
            mixed,
            ("h_all", "proj_all", "query_all", "mixed_all", "spectra", "pre_all", "gated_all"),
        )
        down = mixer_backward(
            l, arrays, back.mid_grad, layer_in, gains, taps, masks, mixer_fetched, tables, saves,
            back.gain_grad, back.weight_grads, pending,
        )
        if not last:
            mixer_results_[l + 1] = {n: getattr(down, "r_" + n) for n in GRADS}
        carried, ffn_total = down.carried, down.ffn_total
        grads = {n: getattr(down, "g_" + n) for n in GRADS}
    above = jnp.stack([mixer_results_[l]["small"][:16] for l in range(1, layers)])
    final = end(carried, shard, grads, ffn_total, above)
    ffn_results[0] = final.ffn_result
    mixer_results_[0] = {n: getattr(final, "r_" + n) for n in GRADS}

    def everywhere(x):
        return lax.psum(x, "outer") if lax.axis_size("outer") > 1 else x

    def stacked(get):
        return everywhere(jnp.stack([get(l) for l in range(layers)])).astype(F32)

    def mixer_stack(name, get):
        return stacked(lambda l: get(mixer_results_[l][name]))

    def ffn_stack(index):
        return stacked(lambda l: ffn_results[l][index * width : (index + 1) * width])

    gain_grads = everywhere(final.gain_grads)

    def gain_stack(at):
        whole = gain_grads[:, at : at + 3].reshape(layers, width)
        return lax.dynamic_slice_in_dim(whole, chan * shard, shard, 1)

    mlp_rows = groups * feats
    return (
        output,
        final.stream_grad,
        gain_stack(9),
        mixer_stack("in", lambda x: x.reshape(3, width, shard).transpose(1, 0, 2)),
        mixer_stack("small", lambda x: x[:9, :shard].reshape(short_taps.shape[1:])),
        mixer_stack("mlp", lambda x: x[:mlp_rows].reshape(cond_in.shape[1:])),
        mixer_stack("mlp", lambda x: x[mlp_rows:].reshape(cond_out.shape[1:])),
        mixer_stack("spec", lambda x: x.reshape(filter_spec.shape[1:])),
        mixer_stack("out", lambda x: x[:shard]),
        gain_stack(12),
        ffn_stack(0),
        ffn_stack(1),
        ffn_stack(2),
    )


def solution(mesh):
    dp_count, chan_count = mesh.devices.shape
    fine = Mesh(
        mesh.devices.reshape(dp_count // 8, 4, 2, chan_count), ("outer", "col", "half", "chan")
    )
    dp = ("outer", "col", "half")
    weight_specs = (
        P(None, "chan"),
        P(None, None, None, "chan"),
        P(None, None, None, "chan"),
        P(None, "chan", None, None),
        P(None, "chan", None, None),
        P(None, None, None, "chan"),
        P(None, "chan", None),
        P(None, "chan"),
        P(None, None, "chan"),
        P(None, None, "chan"),
        P(None, "chan", None),
    )
    return jax.shard_map(
        on_device,
        mesh=fine,
        in_specs=(P(dp, "chan"), P(dp), P(dp, "chan")) + weight_specs,
        out_specs=(P(dp, "chan"), P(dp, "chan")) + weight_specs,
        check_vma=False,
    )
```

time: 1480 us -> 665 us (0.45)
  Pallas kernels: 0 us -> 618 us
  waiting for transfers between devices: 613 us -> 0 us
  matrix products: 560 us -> 0 us
  blocking collectives: 144 us -> 0 us
  other arithmetic: 86.4 us -> 14 us
  local copies, waits for them, and re-layouts: 45.5 us -> 25.7 us
  between operations: 16.7 us -> 1.16 us
    pallas_call x0 -> x10, Pallas kernels: none -> 618 us  [call_kernel(): pl.pallas_call(run, out_shape=[jax.ShapeDtypeStruct(*o) for o in outs.val...]
    dot_general x62 -> x0, matrix products: 552 us -> none  [the longest x4 73.2 us: mix_core(): jnp.einsum('kt,ptc->pkc', sine, cond_part, precision=TRANSFORM_PRECISION)]
    all_gather x8 -> x0, waiting for transfers between devices: 256 us -> none  [the longest x4 140 us: gather_feats(): return lax.all_gather(normed_low, 'chan', axis=1, tiled=True)]
    reduce_scatter x8 -> x0, waiting for transfers between devices: 230 us -> none  [the longest x4 127 us: reduce_rows(): lax.psum_scatter(partial_rows.astype(jnp.bfloat16), 'chan', scatter_dimen...]
    psum x13 -> x0, blocking collectives: 144 us -> none  [the longest x4 42.7 us: norm_forward(): average = lax.psum(jnp.sum(values, 1), 'chan') / full_width]
    psum x1 -> x0, waiting for transfers between devices: 126 us -> none  [on_device(): lax.psum(stacked[1].astype(jnp.bfloat16), 'dp').astype(jnp.float32)]
    reduce_sum x14 -> x0, other arithmetic: 23.7 us -> none  [the longest x2 7.34 us: mix_core(): short_out = taps[0] * preceding + taps[1] * projected + taps[2] * following]
    convert_element_type x19 -> x7, other arithmetic: 33.8 us -> 13.4 us  [stacked(): return everywhere(jnp.stack([get(l) for l in range(layers)])).astype(F32)]
  transfers between devices with their start and end apart: 17 -> 0, of which waited for: 17 -> 0; matrix products, arithmetic and copies ran while one was open for 5% -> 0% of each run, Pallas kernels for 0% -> 0%
where the time goes in v1:
time: 665 us; the launch traced here: 659 us
  Pallas kernels  618 us (93%)
  local copies, waits for them, and re-layouts  25.7 us (4%)
  other arithmetic  14 us (2%)
    pallas_call x10, Pallas kernels, call_kernel(): pl.pallas_call(run, out_shape=[jax.ShapeDtypeStruct(*o) for o in outs.val...  618 us
    unnamed x42, local copies, waits for them, and re-layouts  14.7 us
    convert_element_type x7, other arithmetic, stacked(): return everywhere(jnp.stack([get(l) for l in range(layers)])).astype(F32)  13.4 us

profile of v1, /device:TPU:0, one launch (start us, length us, event | category | flops | bytes accessed | tf_op | source)
XLA Modules:
  0.0 658.8 jit_solution(4283739027262842859)
XLA Ops:
  0.7 4.2 copy.46
  4.8 3.4 copy.49.refs_8_.refs_11_.refs_12_
  9.3 1.0 copy.48.refs_1_
  12.3 39.2 %shard_map.255 = (f32[256,768]{1,0:T(8,128)}, f32[4,768]{1,0:T(4,128)}, f32[18,192]{1,0:T(8,128)}, f32[1024,1]{1,0:T(8,128)}, f32[1024,1]{1,0:T(8,128)}, /*index...) custom-call(bf16[1024,192]{1,0:T(8,128)(2,1)} %copy.47.refs_0_, ...), custom_call_target="tpu_custom_call" | custom-call | flops 1000000 | bytes 20971520 | tf_op jit(solution)/shard_map/pallas_call | solution.py:589
  51.5 73.3 %shard_map.256 = (f32[256,768]{1,0:T(8,128)}, bf16[1024,768]{1,0:T(8,128)(2,1)}, bf16[3,1024,192]{2,1,0:T(8,128)(2,1)}, bf16[1024,192]{1,0:T(8,128)(2,1)}, bf16[...) custom-call(f32[256,768]{1,0:T(8,128)} %get-tuple-element.99.refs_0_, ...), custom_call_target="tpu_custom_call" | custom-call | flops 6000000000 | bytes 20971520 | tf_op jit(solution)/shard_map/pallas_call | solution.py:589
  124.9 47.6 %shard_map.257 = (f32[256,768]{1,0:T(8,128)}, bf16[1024,768]{1,0:T(8,128)(2,1)}, bf16[1024,768]{1,0:T(8,128)(2,1)}, bf16[1024,768]{1,0:T(8,128)(2,1)}, bf16[3,76...) custom-call(f32[256,768]{1,0:T(8,128)} %get-tuple-element.109.refs_0, ...), custom_call_target="tpu_custom_call" | custom-call | flops 3623878656 | bytes 20971520 | tf_op jit(solution)/shard_map/pallas_call | solution.py:589
  172.5 66.5 %shard_map.258 = (f32[256,768]{1,0:T(8,128)}, bf16[1024,768]{1,0:T(8,128)(2,1)}, bf16[3,1024,192]{2,1,0:T(8,128)(2,1)}, bf16[1024,192]{1,0:T(8,128)(2,1)}, bf16[...) custom-call(f32[256,768]{1,0:T(8,128)} %get-tuple-element.113.refs_0, ...), custom_call_target="tpu_custom_call" | custom-call | flops 6000000000 | bytes 20971520 | tf_op jit(solution)/shard_map/pallas_call | solution.py:589
  239.0 1.0 copy.53.refs_8_
  240.0 43.1 %shard_map.259 = (f32[256,768]{1,0:T(8,128)}, bf16[1024,768]{1,0:T(8,128)(2,1)}, bf16[1024,768]{1,0:T(8,128)(2,1)}, bf16[1024,768]{1,0:T(8,128)(2,1)}, f32[256,768]{1,0:T(8,128)}) custom-call(f32[256,768]{1,0:T(8,128)} %get-tuple-element.119.refs_0_.refs_1_, f32[4,768]{1,0:T(4,128)} %get-tuple-element.100.refs_1_.refs_2_, bf16[2,768,768]{2,1,0:T(8,128)(2,1)} %refs_3_.7, ...), custom_call_target="tpu_custom_call" | custom-call | flops 3623878656 | bytes 20971520 | tf_op jit(solution)/shard_map/pallas_call | solution.py:589
  283.1 35.1 %shard_map.260 = (f32[256,768]{1,0:T(8,128)}, bf16[2304,768]{1,0:T(8,128)(2,1)}, f32[1,768]{1,0:T(1,128)}, f32[1024,192]{1,0:T(8,128)}) custom-call(f32[256,768]{1,0:T(8,128)} %get-tuple-element.123.refs_0_, f32[256,768]{1,0:T(8,128)} %get-tuple-element.119.refs_0_.refs_1_, f32[4,768]{1,0:T(4,128)} %get-tuple-element.100.refs_1_.refs_2_, ...), custom_call_target="tpu_custom_call" | custom-call | flops 7247757312 | bytes 20971520 | tf_op jit(solution)/shard_map/pallas_call | solution.py:589
  318.1 67.6 %shard_map.261 = (f32[256,768]{1,0:T(8,128)}, bf16[288,768]{1,0:T(8,128)(2,1)}, bf16[2304,192]{1,0:T(8,128)(2,1)}, bf16[2048,192]{1,0:T(8,128)(2,1)}, bf16[256,7...) custom-call(f32[256,768]{1,0:T(8,128)} %get-tuple-element.129.refs_0_, ...), custom_call_target="tpu_custom_call" | custom-call | flops 8999999488 | bytes 20971520 | tf_op jit(solution)/shard_map/pallas_call | solution.py:589
  385.8 71.0 %shard_map.262 = (f32[256,768]{1,0:T(8,128)}, bf16[2304,768]{1,0:T(8,128)(2,1)}, f32[1,768]{1,0:T(1,128)}, bf16[2304,768]{1,0:T(8,128)(2,1)}, bf16[288,192]{1,0:...) custom-call(f32[256,768]{1,0:T(8,128)} %get-tuple-element.139.refs_0, ...), custom_call_target="tpu_custom_call" | custom-call | flops 7247757312 | bytes 20971520 | tf_op jit(solution)/shard_map/pallas_call | solution.py:589
  456.8 87.8 %shard_map.263 = (f32[256,768]{1,0:T(8,128)}, bf16[288,768]{1,0:T(8,128)(2,1)}, bf16[2304,192]{1,0:T(8,128)(2,1)}, bf16[2048,192]{1,0:T(8,128)(2,1)}, bf16[256,7...) custom-call(f32[256,768]{1,0:T(8,128)} %get-tuple-element.149.refs_0, ...), custom_call_target="tpu_custom_call" | custom-call | flops 8999999488 | bytes 20971520 | tf_op jit(solution)/shard_map/pallas_call | solution.py:589
  544.5 1.3 slice_bitcast_fusion.10.refs_2_
  545.8 86.8 %shard_map.264 = (f32[1024,192]{1,0:T(8,128)}, f32[2,16,256]{2,1,0:T(8,128)}, bf16[2304,768]{1,0:T(8,128)(2,1)}, bf16[2304,192]{1,0:T(8,128)(2,1)}, bf16[2048,19...) custom-call(f32[256,768]{1,0:T(8,128)} %get-tuple-element.164.refs_0_, ...), custom_call_target="tpu_custom_call" | custom-call | flops 1000000 | bytes 20971520 | tf_op jit(solution)/shard_map/pallas_call | solution.py:589
  632.6 2.4 slice_bitcast_fusion.1
  635.9 2.5 maximum_convert_fusion.2
  638.4 4.3 maximum_convert_fusion
  642.8 1.1 maximum_convert_fusion.5
  643.9 1.4 copy.58
  645.9 1.9 maximum_convert_fusion.4
  652.2 2.0 maximum_convert_fusion.3
  655.0 2.4 copy.61
  657.4 1.2 copy.60
  (53 shorter events, 9.5 us)
Async XLA Ops:
  0.6 4.2 copy-start.1
  4.8 3.5 copy-start.6
  4.8 4.5 copy-start.13
  4.8 6.9 %copy-start.14 = (f32[2,192]{1,0:T(2,128)S(1)}, f32[2,192]{1,0:T(2,128)}, u32[]{:S(2)}) copy-start(f32[2,192]{1,0:T(2,128)} %param.26) | copy-start | bytes 4612
  4.8 6.8 %copy-start.15 = (f32[2,192]{1,0:T(2,128)S(1)}, f32[2,192]{1,0:T(2,128)}, u32[]{:S(2)}) copy-start(f32[2,192]{1,0:T(2,128)} %param.19) | copy-start | bytes 4612
  172.4 66.5 %copy-start.7 = (bf16[1024,192]{0,1:T(8,128)(2,1)S(1)}, bf16[1024,192]{0,1:T(8,128)(2,1)}, u32[]{:S(2)}) copy-start(bf16[1024,192]{0,1:T(8,128)(2,1)} %param.18) | copy-start | bytes 1179652
  632.6 3.1 copy-start
  638.4 4.4 copy-start.8
  638.4 4.4 copy-start.9
  642.8 2.6 copy-start.5
  645.9 1.9 copy-start.11
  645.9 1.9 copy-start.10
  647.8 3.1 copy-start.3
  647.8 3.7 copy-start.2
  652.2 2.0 copy-start.12
  654.3 3.1 copy-start.4

commit v2 on v1

v2 whole, which is shorter than its diff:
```python
import functools
import math
from types import SimpleNamespace

import jax
import jax.numpy as jnp
import numpy as np
from jax import lax
from jax.experimental import pallas as pl
from jax.experimental.pallas import tpu as pltpu
from jax.sharding import Mesh
from jax.sharding import PartitionSpec as P

EPSILON = 1e-05
BF = jnp.bfloat16
F32 = jnp.float32


def dft_tables(length):
    positions = np.arange(length)
    angles = (positions[:, None] * positions[None, :] % length) * (2.0 * math.pi / length)
    scale = 1.0 / math.sqrt(length)
    cosine = np.asarray(np.cos(angles) * scale, dtype=np.float32)
    sine = np.asarray(-np.sin(angles) * scale, dtype=np.float32)
    return jnp.asarray(cosine, BF), jnp.asarray(sine, BF)


def normal_cdf(x):
    return 0.5 * (1.0 + lax.erf(x * (2.0**-0.5)))


def normal_pdf(x):
    return jnp.exp(-0.5 * x * x) * (1.0 / math.sqrt(2.0 * math.pi))


MESH = pl.DeviceIdType.MESH
VMEM_LIMIT = 58 << 20
CHUNKS = 2
PARTS = 8


def nt_dot(a, b):
    return lax.dot_general(a, b, (((1,), (1,)), ((), ())), preferred_element_type=F32)


def tn_dot(a, b):
    return lax.dot_general(a, b, (((0,), (0,)), ((), ())), preferred_element_type=F32)


def nn_dot(a, b):
    return jnp.dot(a, b, preferred_element_type=F32)


def aligned(index, size):
    return pl.ds(pl.multiple_of(index * size, size), size)


class Place:
    def __init__(self):
        self.col = lax.axis_index("col")
        self.half = lax.axis_index("half")
        self.chan = lax.axis_index("chan")
        odd = lax.rem(self.chan, 2)
        self.pack = self.chan // 2
        self.own = self.half == self.pack
        self.other_half = 1 - self.half
        self.near_chan = self.chan + 1 - 2 * odd
        self.far_chan = self.chan + 2 - 4 * self.pack
        self.rank = 2 * self.half + odd
        flip_near, flip_peer = 1 - 2 * odd, 2 - 4 * self.half
        self.ranks = [
            self.rank,
            self.rank + flip_near,
            self.rank + flip_peer,
            self.rank + flip_near + flip_peer,
        ]

    def col_at(self, step):
        return lax.rem(self.col + step, 4)

    def barrier(self):
        sem = pltpu.get_barrier_semaphore()
        devices = [{"col": self.col_at(j)} for j in range(1, 4)]
        for i in range(1, 8):
            half = self.half if i < 4 else self.other_half
            devices.append({"half": half, "chan": lax.rem(self.chan + i, 4)})
        for device in devices:
            pl.semaphore_signal(sem, inc=1, device_id=device, device_id_type=MESH)
        pl.semaphore_wait(sem, len(devices))


def remote(src, dst, send_sem, recv_sem, device):
    return pltpu.make_async_remote_copy(
        src_ref=src,
        dst_ref=dst,
        send_sem=send_sem,
        recv_sem=recv_sem,
        device_id=device,
        device_id_type=MESH,
    )


def await_recv(ref, recv_sem, send_sem):
    remote(ref, ref, send_sem, recv_sem, {"half": 1 - lax.axis_index("half")}).wait_recv()


def await_send(ref, send_sem, recv_sem):
    remote(ref, ref, send_sem, recv_sem, {"half": 1 - lax.axis_index("half")}).wait_send()


class Group:
    def __init__(self, place, r, rows, turn=0):
        self.place = place
        self.near = {"chan": place.near_chan}
        self.peer = {"half": place.other_half}
        self.send, self.recv = r.group_send.at[turn], r.group_recv.at[turn]
        self.to_peer, self.from_peer = r.to_peer.at[turn], r.from_peer.at[turn]
        self.to_near, self.from_near = r.to_near.at[turn], r.from_near.at[turn]
        self.rows, self.size = rows, rows // CHUNKS
        self.started = []

    @staticmethod
    def scratch(rows, width, turns=1):
        return dict(
            group_send=pltpu.SemaphoreType.DMA((turns, 6, CHUNKS)),
            group_recv=pltpu.SemaphoreType.DMA((turns, 6, CHUNKS)),
            to_peer=pltpu.VMEM((turns, 2, rows, width), BF),
            from_peer=pltpu.VMEM((turns, 2, rows, width), BF),
            to_near=pltpu.VMEM((turns, rows, width), BF),
            from_near=pltpu.VMEM((turns, rows, width), BF),
        )

    def at(self, which, chunk=None):
        start = self.place.ranks[which] * self.rows
        if chunk is None:
            return pl.ds(pl.multiple_of(start, self.rows), self.rows)
        return pl.ds(pl.multiple_of(start + chunk * self.size, self.size), self.size)

    def start(self, src, dst, kind, chunk, device):
        copy = remote(src, dst, self.send.at[kind, chunk], self.recv.at[kind, chunk], device)
        copy.start()
        self.started.append(copy)

    def arrived(self, ref, kind, chunk):
        await_recv(ref, self.recv.at[kind, chunk], self.send.at[kind, chunk])

    def gather_start(self, full):
        for chunk in range(CHUNKS):
            own = full.at[self.at(0, chunk)]
            self.start(own, own, 0, chunk, self.near)
        for chunk in range(CHUNKS):
            own = full.at[self.at(0, chunk)]
            self.start(own, own, 1, chunk, self.peer)

    def gather_peer(self, full):
        for chunk in range(CHUNKS):
            self.arrived(full.at[self.at(2, chunk)], 1, chunk)

    def gather_near(self, full, chunk):
        piece = full.at[self.at(1, chunk)]
        self.arrived(piece, 0, chunk)
        self.start(piece, piece, 2, chunk, self.peer)

    def gather_diagonal(self, full, chunk):
        self.arrived(full.at[self.at(3, chunk)], 2, chunk)

    def piece(self, chunk):
        return pl.ds(chunk * self.size, self.size)

    def reduce_peer(self, slot, chunk, value):
        at = self.piece(chunk)
        self.to_peer[slot, at] = value.astype(BF)
        self.start(self.to_peer.at[slot, at], self.from_peer.at[slot, at], 3 + slot, chunk, self.peer)

    def reduce_near(self, chunk, value):
        at = self.piece(chunk)
        self.arrived(self.from_peer.at[1, at], 4, chunk)
        self.to_near[at] = (value + self.from_peer[1, at].astype(F32)).astype(BF)
        self.start(self.to_near.at[at], self.from_near.at[at], 5, chunk, self.near)

    def reduce_end(self, chunk):
        at = self.piece(chunk)
        self.arrived(self.from_peer.at[0, at], 3, chunk)
        self.arrived(self.from_near.at[at], 5, chunk)
        return self.from_peer[0, at].astype(F32) + self.from_near[at].astype(F32)

    def reduce_whole(self, kind, part):
        for chunk in range(CHUNKS):
            value = part[chunk * self.size : (chunk + 1) * self.size]
            if kind == "near":
                self.reduce_near(chunk, value)
            else:
                self.reduce_peer({"peer": 0, "diagonal": 1}[kind], chunk, value)

    def finish(self):
        for copy in self.started:
            copy.wait_send()


class Weights:
    def __init__(self, place, sems, pairs):
        self.place, self.pairs = place, pairs
        self.send, self.recv, self.local = sems

    def cut(self, ref, axis, parts, index):
        at = aligned(index, ref.shape[axis] // parts)
        return ref.at[(slice(None),) * axis + (at,)]

    def index(self, parts, col, half):
        return col * 2 + half if parts == 8 else col

    def each_sent(self, act):
        p = self.place
        owner = {"half": p.pack, "chan": p.far_chan}
        for a, (src, dst, axis, parts) in enumerate(self.pairs):

            def send(a=a, src=src, dst=dst, axis=axis, parts=parts):
                index = self.index(parts, p.col, p.half)
                act(
                    remote(
                        self.cut(src, axis, parts, index),
                        self.cut(dst, axis, parts, index),
                        self.send.at[a, 0],
                        self.recv.at[a, p.half if parts == 8 else 0],
                        owner,
                    )
                )

            if parts == 8:
                send()
            else:
                pl.when(p.half == 0)(send)

    def start(self):
        self.each_sent(lambda c: c.start())

        @pl.when(self.place.own)
        def _():
            for a, (src, dst, axis, parts) in enumerate(self.pairs):
                pltpu.make_async_copy(src, dst, self.local.at[a]).start()

    def forward(self):
        p = self.place

        @pl.when(jnp.logical_not(p.own))
        def _():
            for a, (src, dst, axis, parts) in enumerate(self.pairs):
                for s in range(parts // 4):
                    piece = self.cut(dst, axis, parts, self.index(parts, p.col, s))
                    await_recv(piece, self.recv.at[a, s], self.send.at[a, 0])
                    for j in range(1, 4):
                        remote(
                            piece,
                            piece,
                            self.send.at[a, 2 * j - 1 + s],
                            self.recv.at[a, 2 * j + s],
                            {"col": p.col_at(j)},
                        ).start()

    def ready(self, which=None):
        p = self.place
        which = range(len(self.pairs)) if which is None else which

        @pl.when(p.own)
        def _():
            for a in which:
                src, dst, axis, parts = self.pairs[a]
                pltpu.make_async_copy(src, dst, self.local.at[a]).wait()

        @pl.when(jnp.logical_not(p.own))
        def _():
            for a in which:
                src, dst, axis, parts = self.pairs[a]
                for s in range(parts // 4):
                    for j in range(1, 4):
                        piece = self.cut(dst, axis, parts, self.index(parts, p.col_at(4 - j), s))
                        await_recv(piece, self.recv.at[a, 2 * j + s], self.send.at[a, 0])

    def finish(self):
        p = self.place
        self.each_sent(lambda c: c.wait_send())

        @pl.when(jnp.logical_not(p.own))
        def _():
            for a, (src, dst, axis, parts) in enumerate(self.pairs):
                for s in range(parts // 4):
                    for j in range(1, 4):
                        piece = self.cut(dst, axis, parts, self.index(parts, p.col_at(4 - j), s))
                        await_send(piece, self.send.at[a, 2 * j - 1 + s], self.recv.at[a, 0])


class Load:
    def __init__(self, r, pairs):
        self.copies = [
            pltpu.make_async_copy(src, dst, r.load_sem.at[a]) for a, (src, dst) in enumerate(pairs)
        ]

    def start(self):
        for copy in self.copies:
            copy.start()

    def finish(self, which=None):
        for a in range(len(self.copies)) if which is None else which:
            self.copies[a].wait()


class Exchange:
    def __init__(self, place, r, src, dst, name="ex"):
        self.place, self.src, self.dst = place, src, dst
        self.send, self.recv, self.local = [
            getattr(r, f"{name}_{n}") for n in ("send", "recv", "local")
        ]
        self.size = src.shape[0] // 4

    @staticmethod
    def scratch(name="ex"):
        return {
            f"{name}_send": pltpu.SemaphoreType.DMA((4,)),
            f"{name}_recv": pltpu.SemaphoreType.DMA((4,)),
            f"{name}_local": pltpu.SemaphoreType.DMA,
        }

    def each(self, act, act_self):
        p = self.place
        for j in range(4):
            chan = 2 * p.half + j % 2
            mine = (p.half == j // 2) & (p.chan == chan)
            src, dst = self.src.at[pl.ds(j * self.size, self.size)], self.dst.at[p.chan]

            def go(j=j, chan=chan, src=src, dst=dst):
                act(
                    remote(
                        src, dst, self.send.at[j], self.recv.at[p.chan],
                        {"half": j // 2, "chan": chan},
                    )
                )

            def stay(src=src, dst=dst):
                act_self(pltpu.make_async_copy(src, dst, self.local))

            pl.when(jnp.logical_not(mine))(go)
            pl.when(mine)(stay)

    def start(self):
        self.each(lambda c: c.start(), lambda c: c.start())

    def finish(self):
        p = self.place
        self.each(lambda c: c.wait_send(), lambda c: c.wait())
        for j in range(4):

            def wait(j=j):
                await_recv(self.dst.at[j], self.recv.at[j], self.send.at[0])

            pl.when(jnp.logical_not(p.own & (p.chan == j)))(wait)


class Return:
    def __init__(self, place, r, src, dst):
        self.place, self.src, self.dst = place, src, dst
        self.send, self.recv, self.local = r.back_send, r.back_recv, r.back_local
        self.size = src.shape[1]

    @staticmethod
    def scratch():
        return dict(
            back_send=pltpu.SemaphoreType.DMA((4,)),
            back_recv=pltpu.SemaphoreType.DMA((4,)),
            back_local=pltpu.SemaphoreType.DMA,
        )

    def each(self, act, act_self):
        p = self.place
        for j in range(4):
            mine = p.own & (p.chan == j)
            src, dst = self.src.at[j], self.dst.at[aligned(p.rank, self.size)]

            def go(j=j, src=src, dst=dst):
                act(
                    remote(
                        src, dst, self.send.at[j], self.recv.at[p.rank],
                        {"half": p.pack, "chan": j},
                    )
                )

            def stay(src=src, dst=dst):
                act_self(pltpu.make_async_copy(src, dst, self.local))

            pl.when(jnp.logical_not(mine))(go)
            pl.when(mine)(stay)

    def start(self):
        self.each(lambda c: c.start(), lambda c: c.start())

    def finish(self):
        p = self.place
        self.each(lambda c: c.wait_send(), lambda c: c.wait())
        for j in range(4):
            mine = (p.half == j // 2) & (p.chan == 2 * p.half + j % 2)

            def wait(j=j):
                await_recv(
                    self.dst.at[pl.ds(j * self.size, self.size)], self.recv.at[j], self.send.at[0]
                )

            pl.when(jnp.logical_not(mine))(wait)


class Scatter:
    def __init__(self, place, r, sources, totals, name="sc"):
        self.place, self.sources, self.totals = place, sources, totals
        self.send, self.recv = getattr(r, name + "_send"), getattr(r, name + "_recv")
        self.local = getattr(r, name + "_local")
        self.kept, self.got, self.late, self.cross = [
            [getattr(r, f"{name}_{part}{a}") for a in range(len(sources))]
            for part in ("kept", "got", "late", "cross")
        ]
        self.x = lax.rem(place.col, 2)
        self.y = place.col // 2
        self.to_x = {"col": place.col + 1 - 2 * self.x}
        self.to_y = {"col": lax.rem(place.col + 2, 4)}

    @staticmethod
    def scratch(shapes, name="sc"):
        n = len(shapes)
        out = {
            f"{name}_send": pltpu.SemaphoreType.DMA((n, 8)),
            f"{name}_recv": pltpu.SemaphoreType.DMA((n, 8)),
            f"{name}_local": pltpu.SemaphoreType.DMA((n, 4)),
        }
        for a, (rows, width) in enumerate(shapes):
            for part, count in (("kept", 4), ("got", 4), ("late", 2), ("cross", 2)):
                out[f"{name}_{part}{a}"] = pltpu.VMEM((count, rows // 8, width), BF)
        return out

    def each(self, which):
        return range(len(self.sources)) if which is None else which

    def piece(self, a, y, x, half):
        src = self.sources[a]
        return src.at[aligned((2 * y + x) * 2 + half, src.shape[0] // 8)]

    def firsts(self, a):
        out = []
        for i in range(2):
            out.append((self.piece(a, i, 1 - self.x, 0), i, self.to_x))
            out.append((self.piece(a, 1 - self.y, i, 1), 2 + i, self.to_y))
        return [
            remote(src, self.got[a].at[k], self.send.at[a, k], self.recv.at[a, k], device)
            for src, k, device in out
        ]

    def keeps(self, a):
        out = []
        for i in range(2):
            out.append((self.piece(a, i, self.x, 0), i))
            out.append((self.piece(a, self.y, i, 1), 2 + i))
        return [
            pltpu.make_async_copy(src, self.kept[a].at[k], self.local.at[a, k]) for src, k in out
        ]

    def seconds(self, a):
        kept, late = self.kept[a], self.late[a]
        return [
            remote(kept.at[1 - self.y], late.at[0], self.send.at[a, 4], self.recv.at[a, 4], self.to_y),
            remote(kept.at[3 - self.x], late.at[1], self.send.at[a, 5], self.recv.at[a, 5], self.to_x),
        ]

    def third(self, a, slot, part, half, chan):
        return remote(
            self.got[a].at[part],
            self.cross[a].at[slot],
            self.send.at[a, 6 + slot],
            self.recv.at[a, 6 + slot],
            {"half": half, "chan": chan},
        )

    def start(self, which=None):
        for a in self.each(which):
            for copy in self.firsts(a) + self.keeps(a):
                copy.start()

    def second(self, which=None):
        for a in self.each(which):
            for copy in self.firsts(a) + self.keeps(a):
                copy.wait()
            for k in range(4):
                total = self.kept[a][k].astype(F32) + self.got[a][k].astype(F32)
                self.kept[a][k] = total.astype(BF)
            for copy in self.seconds(a):
                copy.start()

    def middle(self, which=None):
        p = self.place
        for a in self.each(which):
            for copy in self.seconds(a):
                copy.wait()
            kept, late, got = self.kept[a], self.late[a], self.got[a]
            got[0] = (kept[self.y].astype(F32) + late[0].astype(F32)).astype(BF)
            got[1] = (kept[2 + self.x].astype(F32) + late[1].astype(F32)).astype(BF)

            @pl.when(p.own)
            def _():
                self.third(a, 0, p.other_half, p.other_half, p.chan).start()

            @pl.when(jnp.logical_not(p.own))
            def _():
                self.third(a, 0, p.half, p.half, p.far_chan).start()
                self.third(a, 1, p.other_half, p.other_half, p.far_chan).start()

    def finish(self, which=None):
        p = self.place
        for a in self.each(which):
            cross = self.cross[a]
            await_recv(cross.at[0], self.recv.at[a, 6], self.send.at[a, 6])
            await_send(cross.at[0], self.send.at[a, 6], self.recv.at[a, 6])

            @pl.when(p.own)
            def _():
                self.totals[a][...] = (
                    cross[0].astype(F32) + self.got[a][p.half].astype(F32)
                ).astype(BF)

            @pl.when(jnp.logical_not(p.own))
            def _():
                await_recv(cross.at[1], self.recv.at[a, 7], self.send.at[a, 7])
                await_send(cross.at[1], self.send.at[a, 7], self.recv.at[a, 7])
                self.totals[a][...] = (cross[0].astype(F32) + cross[1].astype(F32)).astype(BF)


class Spread:
    def __init__(self, place, r, totals, results, name="sp"):
        self.place, self.totals, self.results = place, totals, results
        self.send, self.recv, self.kept = [
            getattr(r, f"{name}_{n}") for n in ("send", "recv", "local")
        ]

    @staticmethod
    def scratch(count, name="sp"):
        return {
            f"{name}_send": pltpu.SemaphoreType.DMA((count, 7)),
            f"{name}_recv": pltpu.SemaphoreType.DMA((count, 7)),
            f"{name}_local": pltpu.SemaphoreType.DMA((count,)),
        }

    def each(self, which):
        return range(len(self.totals)) if which is None else which

    def slot(self, a, col, half):
        result = self.results[a]
        return result.at[aligned(col * 2 + half, result.shape[0] // 8)]

    def local(self, a):
        p = self.place
        return pltpu.make_async_copy(
            self.totals[a], self.slot(a, p.col, p.half), self.kept.at[a]
        )

    def out(self, a, j):
        p = self.place
        device = {"col": p.col_at(j)} if j else {"half": p.other_half}
        return remote(
            self.totals[a],
            self.slot(a, p.col, p.half),
            self.send.at[a, j],
            self.recv.at[a, j],
            device,
        )

    def pass_on(self, a, j):
        p = self.place
        piece = self.slot(a, p.col_at(4 - j), p.half)
        return remote(
            piece, piece, self.send.at[a, 3 + j], self.recv.at[a, 3 + j],
            {"half": p.other_half},
        )

    def start(self, which=None):
        for a in self.each(which):
            for j in (1, 2, 3, 0):
                self.out(a, j).start()
            self.local(a).start()

    def forward(self, which=None):
        p = self.place
        for a in self.each(which):
            for j in range(1, 4):
                piece = self.slot(a, p.col_at(4 - j), p.half)
                await_recv(piece, self.recv.at[a, j], self.send.at[a, j])
                self.pass_on(a, j).start()

    def finish(self, which=None):
        p = self.place
        for a in self.each(which):
            for j in range(4):
                self.out(a, j).wait_send()
            self.local(a).wait()
            await_recv(
                self.slot(a, p.col, p.other_half), self.recv.at[a, 0], self.send.at[a, 0]
            )
            for j in range(1, 4):
                self.pass_on(a, j).wait_send()
                piece = self.slot(a, p.col_at(4 - j), p.other_half)
                await_recv(piece, self.recv.at[a, 3 + j], self.send.at[a, 3 + j])


def call_kernel(body, ins, outs, scratch, collective_id, flops, hbm=()):
    names = list(ins) + list(outs) + list(scratch)

    def run(*refs):
        body(SimpleNamespace(**dict(zip(names, refs))))

    def spec(name):
        return pl.BlockSpec(memory_space=pl.ANY if name in hbm else pltpu.VMEM)

    results = pl.pallas_call(
        run,
        out_shape=[jax.ShapeDtypeStruct(*o) for o in outs.values()],
        in_specs=[spec(n) for n in ins],
        out_specs=[spec(n) for n in outs],
        scratch_shapes=list(scratch.values()),
        compiler_params=pltpu.CompilerParams(
            collective_id=collective_id, has_side_effects=True, vmem_limit_bytes=VMEM_LIMIT
        ),
        cost_estimate=pl.CostEstimate(flops=flops, bytes_accessed=20 << 20, transcendentals=0),
    )(*ins.values())
    return SimpleNamespace(**dict(zip(outs, results)))


def normalized(x):
    average = jnp.mean(x, 1, keepdims=True)
    centered = x - average
    variance = jnp.mean(centered * centered, 1, keepdims=True)
    inv = lax.rsqrt(variance + EPSILON)
    return centered * inv, inv


def norm_grad_rows(grad, x, gain):
    xhat, inv = normalized(x)
    gain_part = jnp.sum(grad * xhat, 0, keepdims=True)
    scaled = grad * gain
    mean_plain = jnp.mean(scaled, 1, keepdims=True)
    mean_cross = jnp.mean(scaled * xhat, 1, keepdims=True)
    return inv * (scaled - mean_plain - xhat * mean_cross), gain_part


PAD = 8


def shifted(ref, s, tile, size, offset):
    return ref[s, pl.ds(PAD + tile * size + offset, size)]


def mlp_tables(r, l):
    groups, feats, inner = r.w_ci.shape[1:]
    half = feats // 2
    for table in (r.in_re, r.in_im, r.out_re, r.out_im):
        table[...] = jnp.zeros_like(table)
    for g in range(groups):
        rows, cols = pl.ds(g * half, half), pl.ds(g * inner, inner)
        r.in_re[rows, cols] = r.w_ci[l, g, 0:half].astype(BF)
        r.in_im[rows, cols] = r.w_ci[l, g, half:feats].astype(BF)
        turned = r.w_co[l, g].T
        r.out_re[rows, cols] = turned[0:half].astype(BF)
        r.out_im[rows, cols] = turned[half:feats].astype(BF)


def mlp_scratch(shard, inner):
    table = pltpu.VMEM((shard, inner), BF)
    return dict(in_re=table, in_im=table, out_re=table, out_im=table)


MIXER = dict(in_proj="w_in", cond_in="w_ci", cond_out="w_co", out_proj="w_out", filter_spec="w_spec")
FFN = dict(gate_proj="w_gate", up_proj="w_up", down_proj="w_down")
CUTS = dict(in_proj=1, cond_in=1, cond_out=1, filter_spec=1, out_proj=0, gate_proj=0, up_proj=0, down_proj=0)
PROJ, QUERY, MIXED, GATED, SPECTRA, MIX_ROWS = 0, 3, 4, 5, 6, 12


def forward_body(r):
    place = Place()
    layers, rows, width = r.mids.shape
    length = r.seg.shape[0]
    lanes = r.w_in.shape[3]
    wide = r.both.shape[1] // 2
    tiles = 4
    size = length // tiles
    exchange = Exchange(place, r, r.stream, r.pieces)
    tables = [
        pltpu.make_async_copy(r.cosine, r.cos, r.table_sem.at[0]),
        pltpu.make_async_copy(r.sine, r.sin, r.table_sem.at[1]),
    ]

    def weights(kind, names, l):
        sems = [getattr(r, f"{kind}_{n}").at[l] for n in ("send", "recv", "local")]
        pairs = [
            (getattr(r, n).at[l], getattr(r, to).at[l], CUTS[n], 4 if n == "out_proj" else 8)
            for n, to in names.items()
        ]
        return Weights(place, sems, pairs)

    mixer_weights = [weights("mw", MIXER, l) for l in range(layers)]
    ffn_weights = [weights("fw", FFN, l) for l in range(layers)]
    place.barrier()
    exchange.start()
    own, other = place.own, jnp.logical_not(place.own)

    def gain_copy(j):
        chan = lax.rem(place.chan + j, 4)
        return remote(r.small, r.gain_parts.at[j], r.gain_send.at[j], r.gain_recv.at[j], {"chan": chan})

    for j in range(1, 4):
        gain_copy(j).start()
    seg_copy = remote(r.seg, r.seg_got, r.gain_send.at[4], r.gain_recv.at[4], {"half": place.other_half})
    taps_copy = remote(r.taps, r.taps_got, r.gain_send.at[5], r.gain_recv.at[5], {"chan": place.far_chan})

    @pl.when(own)
    def _():
        seg_copy.start()
        taps_copy.start()

    mixer_weights[0].start()
    for copy in tables:
        copy.start()
    r.edges[0:PAD] = jnp.full((PAD, 1), -1, jnp.int32)
    r.edges[PAD + length : 2 * PAD + length] = jnp.full((PAD, 1), -1, jnp.int32)
    for s in range(3):
        r.padded[s, 0:PAD] = jnp.zeros((PAD, lanes), F32)
        r.padded[s, PAD + length : 2 * PAD + length] = jnp.zeros((PAD, lanes), F32)
    r.both[...] = jnp.zeros_like(r.both)

    @pl.when(own)
    def _():
        r.edges[PAD : PAD + length] = r.seg[...]
        r.taps_out[...] = r.taps[...]
        seg_copy.wait_send()
        taps_copy.wait_send()

    @pl.when(other)
    def _():
        seg_copy.wait_recv()
        taps_copy.wait_recv()
        r.edges[PAD : PAD + length] = r.seg_got[...]
        r.taps_out[...] = r.taps_got[...]

    here = r.edges[PAD : PAD + length]
    r.mask_prev[...] = jnp.where(r.edges[PAD - 1 : PAD - 1 + length] == here, 1.0, 0.0)
    r.mask_next[...] = jnp.where(r.edges[PAD + 1 : PAD + 1 + length] == here, 1.0, 0.0)
    for j in range(1, 4):
        gain_copy(j).wait()
    r.gain_parts[0] = r.small[...]
    parts = []
    for c in range(4):
        parts.append(r.gain_parts[lax.rem(place.chan - c + 4, 4)])
    r.gains[...] = jnp.concatenate(parts, 1)
    exchange.finish()
    r.values[0] = jnp.concatenate([r.pieces[j] for j in range(4)], 1).astype(F32)

    def tap(l, o, s):
        at = 9 * l + 3 * o + s
        return r.taps_out[at : at + 1]

    saves = {}

    def save(name, *copies):
        saves[name] = [pltpu.make_async_copy(src, dst, r.save_sem.at[i]) for i, src, dst in copies]
        for copy in saves[name]:
            copy.start()

    def saved(name):
        for copy in saves.pop(name, ()):
            copy.wait()

    def mixer(l):
        group = Group(place, r, rows, 0)
        h_all = r.h_mixer.at[l]
        xhat, _ = normalized(r.values[l])
        h_all[group.at(0)] = (xhat * r.gains[l : l + 1]).astype(BF)
        group.gather_start(h_all)
        if l == 0:
            mixer_weights[0].forward()
            ffn_weights[0].start()
        mixer_weights[l].ready()
        mlp_tables(r, l)
        saved("mixer")

        def project(which, chunk=None):
            at = group.at(which, chunk)
            h = h_all[at]
            for s in range(3):
                proj = nn_dot(h, r.w_in[l, s])
                r.padded[s, pl.ds(pl.multiple_of(at.start + PAD, 8), at.size)] = proj
                r.mix[PROJ + s, at] = proj.astype(BF)

        project(0)
        group.gather_peer(h_all)
        project(2)
        for chunk in range(CHUNKS):
            group.gather_near(h_all, chunk)
            project(1, chunk)
            group.gather_diagonal(h_all, chunk)
            project(3, chunk)

        for t in range(tiles):
            at = pl.ds(t * size, size)
            prev = r.mask_prev[at]
            following = r.mask_next[at]
            shorts = []
            for s in range(3):
                shorts.append(
                    tap(l, 0, s) * shifted(r.padded, s, t, size, -1) * prev
                    + tap(l, 1, s) * shifted(r.padded, s, t, size, 0)
                    + tap(l, 2, s) * shifted(r.padded, s, t, size, 1) * following
                )
            r.mix[QUERY, at] = shorts[0].astype(BF)
            r.both[at, 0:lanes] = shorts[1].astype(BF)
            r.both[at, wide : wide + lanes] = shorts[2].astype(BF)
        if l == 0:
            for copy in tables:
                copy.wait()

        @pl.loop(0, tiles)
        def _(t):
            at = aligned(t, size)
            real = nn_dot(r.cos[at], r.both[...])
            imag = nn_dot(r.sin[at], r.both[...])
            value_re, cond_re = real[:, :lanes], real[:, wide : wide + lanes].astype(BF)
            value_im, cond_im = imag[:, :lanes], imag[:, wide : wide + lanes].astype(BF)
            pre = nn_dot(cond_re, r.in_re[...]) + nn_dot(cond_im, r.in_im[...])
            inner = (pre * normal_cdf(pre)).astype(BF)
            kernel_re = r.w_spec[l, 0, at] + nt_dot(inner, r.out_re[...])
            kernel_im = r.w_spec[l, 1, at] + nt_dot(inner, r.out_im[...])
            r.prod_re[at] = (value_re * kernel_re - value_im * kernel_im).astype(BF)
            r.prod_im[at] = (value_re * kernel_im + value_im * kernel_re).astype(BF)
            r.pre[at] = pre.astype(BF)
            for i, x in enumerate((value_re, value_im, kernel_re, kernel_im, cond_re, cond_im)):
                r.mix[SPECTRA + i, at] = x.astype(BF)

        ffn_weights[l].forward()
        if l + 1 < layers:
            mixer_weights[l + 1].start()

        def project_out(which):
            at = group.at(which)
            mixed = nn_dot(r.cos[at], r.prod_re[...]) + nn_dot(r.sin[at], r.prod_im[...])
            r.mix[MIXED, at] = mixed.astype(BF)
            gated = (r.mix[QUERY, at].astype(F32) * mixed).astype(BF)
            r.mix[GATED, at] = gated
            return nn_dot(gated, r.w_out[l])

        group.reduce_whole("diagonal", project_out(3))
        group.reduce_whole("near", project_out(1))
        group.reduce_whole("peer", project_out(2))
        r.mids[l] = r.values[l] + project_out(0)
        save("mixer", (0, r.mix, r.s_mix.at[l]), (1, r.pre, r.s_pre.at[l]), (2, h_all, r.s_h_mixer.at[l]))
        for chunk in range(CHUNKS):
            r.mids[l, group.piece(chunk)] += group.reduce_end(chunk)
        group.finish()

    def ffn(l):
        group = Group(place, r, rows, 1)
        h_all = r.h_ffn.at[l]
        xhat, _ = normalized(r.mids[l])
        h_all[group.at(0)] = (xhat * r.gains[layers + l : layers + l + 1]).astype(BF)
        group.gather_start(h_all)
        ffn_weights[l].ready()
        saved("ffn")

        def block(at):
            h = h_all[at]
            gate = nn_dot(h, r.w_gate[l])
            up = nn_dot(h, r.w_up[l])
            r.units[0, at] = gate.astype(BF)
            r.units[1, at] = up.astype(BF)
            hidden = (gate * normal_cdf(gate) * up).astype(BF)
            return nn_dot(hidden, r.w_down[l])

        r.values[l + 1] = r.mids[l] + block(group.at(0))
        group.gather_peer(h_all)
        group.reduce_whole("peer", block(group.at(2)))
        if l + 1 < layers:
            mixer_weights[l + 1].forward()
            ffn_weights[l + 1].start()
        else:
            cotangent.start()
        for chunk in range(CHUNKS):
            group.gather_near(h_all, chunk)
            r.near_part[group.piece(chunk)] = block(group.at(1, chunk))
            group.gather_diagonal(h_all, chunk)
            group.reduce_peer(1, chunk, block(group.at(3, chunk)))
            group.reduce_near(chunk, r.near_part[group.piece(chunk)])
        save("ffn", (3, r.units, r.s_units.at[l]), (4, h_all, r.s_h_ffn.at[l]))
        for chunk in range(CHUNKS):
            r.values[l + 1, group.piece(chunk)] += group.reduce_end(chunk)
        group.finish()

    cotangent = Exchange(place, r, r.cotangent, r.cot_pieces, "cot")
    for l in range(layers):
        mixer(l)
        ffn(l)
    kept = []
    for i, name in enumerate(list(MIXER.values()) + list(FFN.values())):
        if name != "w_spec":
            kept.append(
                pltpu.make_async_copy(getattr(r, name), getattr(r, name + "_out"), r.keep_sem.at[i])
            )
    for copy in kept:
        copy.start()
    cotangent.finish()
    r.carried[...] = jnp.concatenate([r.cot_pieces[j] for j in range(4)], 1).astype(F32)
    for l in range(layers):
        mixer_weights[l].finish()
        ffn_weights[l].finish()
    saved("mixer")
    saved("ffn")
    for copy in kept:
        copy.wait()


def forward(arrays, stream, cotangent, seg, small, taps, tables):
    length, shard = stream.shape
    layers, _, width, lanes = arrays["in_proj"].shape
    rows = length // 4
    units = arrays["gate_proj"].shape[2]
    groups, _, inner = arrays["cond_in"].shape[1:]
    inner *= groups
    wide = -(-lanes // 128) * 128
    gains = small.shape[0]
    held = {to: pltpu.VMEM(arrays[n].shape, arrays[n].dtype) for n, to in {**MIXER, **FFN}.items()}
    kept = {
        to + "_out": (arrays[n].shape, arrays[n].dtype)
        for n, to in {**MIXER, **FFN}.items()
        if to != "w_spec"
    }
    saves = dict(
        s_mix=((layers, MIX_ROWS, length, lanes), BF),
        s_pre=((layers, length, inner), BF),
        s_h_mixer=((layers, length, width), BF),
        s_units=((layers, 2, length, units), BF),
        s_h_ffn=((layers, length, width), BF),
    )

    def semaphores(kind, count):
        return {
            f"{kind}_send": pltpu.SemaphoreType.DMA((layers, count, 7)),
            f"{kind}_recv": pltpu.SemaphoreType.DMA((layers, count, 8)),
            f"{kind}_local": pltpu.SemaphoreType.DMA((layers, count)),
        }

    return call_kernel(
        forward_body,
        dict(
            stream=stream, cotangent=cotangent, seg=seg, small=small, taps=taps,
            cosine=tables[0], sine=tables[1], **arrays,
        ),
        dict(
            values=((layers + 1, rows, width), F32),
            mids=((layers, rows, width), F32),
            carried=((rows, width), F32),
            gains=((gains, width), F32),
            taps_out=(taps.shape, F32),
            mask_prev=((length, 1), F32),
            mask_next=((length, 1), F32),
            **saves,
            **kept,
        ),
        dict(
            pieces=pltpu.VMEM((4, rows, shard), BF),
            cot_pieces=pltpu.VMEM((4, rows, shard), BF),
            gain_parts=pltpu.VMEM((4, gains, shard), F32),
            gain_send=pltpu.SemaphoreType.DMA((6,)),
            gain_recv=pltpu.SemaphoreType.DMA((6,)),
            table_sem=pltpu.SemaphoreType.DMA((2,)),
            save_sem=pltpu.SemaphoreType.DMA((5,)),
            keep_sem=pltpu.SemaphoreType.DMA((8,)),
            seg_got=pltpu.VMEM((length, 1), jnp.int32),
            taps_got=pltpu.VMEM(taps.shape, F32),
            edges=pltpu.VMEM((length + 2 * PAD, 1), jnp.int32),
            cos=pltpu.VMEM((length, length), BF),
            sin=pltpu.VMEM((length, length), BF),
            h_mixer=pltpu.VMEM((layers, length, width), BF),
            h_ffn=pltpu.VMEM((layers, length, width), BF),
            mix=pltpu.VMEM((MIX_ROWS, length, lanes), BF),
            pre=pltpu.VMEM((length, inner), BF),
            units=pltpu.VMEM((2, length, units), BF),
            near_part=pltpu.VMEM((rows, width), F32),
            padded=pltpu.VMEM((3, length + 2 * PAD, lanes), F32),
            both=pltpu.VMEM((length, 2 * wide), BF),
            prod_re=pltpu.VMEM((length, lanes), BF),
            prod_im=pltpu.VMEM((length, lanes), BF),
            **held,
            **semaphores("mw", 5),
            **semaphores("fw", 3),
            **mlp_scratch(lanes, inner),
            **Group.scratch(rows, width, 2),
            **Exchange.scratch(),
            **Exchange.scratch("cot"),
        ),
        1,
        30 * 10**9,
        ("stream", "cotangent", "cosine", "sine") + tuple(arrays) + tuple(saves) + tuple(kept),
    )


def ffn_backward_body(l, last, r):
    place = Place()
    rows, width = r.mids.shape[1:]
    units = r.units.shape[2]
    group = Group(place, r, rows)
    load = Load(
        r,
        [
            (r.w_gate_out.at[l], r.w_gate),
            (r.w_up_out.at[l], r.w_up),
            (r.w_down_out.at[l], r.w_down),
            (r.s_units.at[l], r.units),
            (r.s_h_ffn.at[l], r.h_all),
        ],
    )
    load.start()
    layers = r.gains.shape[0] // 2
    gain = r.gains[layers + l : layers + l + 1]
    r.g_all[group.at(0)] = r.carried[...].astype(BF)
    if last:
        shard = r.returned.shape[1]
        for j in range(4):
            r.leaving[j] = r.values[l + 1, :, j * shard : (j + 1) * shard].astype(BF)
        back = Return(place, r, r.leaving, r.returned)
    place.barrier()
    group.gather_start(r.g_all)
    if last:
        back.start()
    else:
        spread = Spread(place, r, [r.ffn_total], [r.ffn_result])
        scatter = Scatter(place, r, of(r, "g_"), of(r, "t_"))
        scatter.start()
        spread.start()

    load.finish()

    def block(at):
        hidden_grad = nt_dot(r.g_all[at], r.w_down[...])
        gate = r.units[0, at].astype(F32)
        up = r.units[1, at].astype(F32)
        cdf = normal_cdf(gate)
        act = gate * cdf
        r.hidden_all[at] = (act * up).astype(BF)
        gate_grad = (hidden_grad * up * (cdf + gate * normal_pdf(gate))).astype(BF)
        up_grad = (hidden_grad * act).astype(BF)
        r.gate_grads[at] = gate_grad
        r.up_grads[at] = up_grad
        return nt_dot(gate_grad, r.w_gate[...]) + nt_dot(up_grad, r.w_up[...])

    r.own_part[...] = block(group.at(0))
    group.gather_peer(r.g_all)
    group.reduce_whole("peer", block(group.at(2)))
    if not last:
        scatter.second()
    for chunk in range(CHUNKS):
        group.gather_near(r.g_all, chunk)
        r.near_part[group.piece(chunk)] = block(group.at(1, chunk))
        group.gather_diagonal(r.g_all, chunk)
        group.reduce_peer(1, chunk, block(group.at(3, chunk)))
        group.reduce_near(chunk, r.near_part[group.piece(chunk)])
    if not last:
        scatter.middle()
        spread.forward()
    step = 256
    for u in range(units // step):
        cols = pl.ds(u * step, step)
        r.weight_grads[0 * width : 1 * width, cols] = tn_dot(r.h_all[...], r.gate_grads[:, cols]).astype(BF)
        r.weight_grads[1 * width : 2 * width, cols] = tn_dot(r.h_all[...], r.up_grads[:, cols]).astype(BF)
        r.weight_grads[pl.ds(2 * width + u * step, step)] = tn_dot(r.hidden_all[:, cols], r.g_all[...]).astype(BF)
    for chunk in range(CHUNKS):
        r.own_part[group.piece(chunk)] += group.reduce_end(chunk)
    grad, gain_part = norm_grad_rows(r.own_part[...], r.mids[l], gain)
    r.mid_grad[...] = r.carried[...] + grad
    r.gain_grad[...] = gain_part
    group.finish()
    if last:
        back.finish()
        r.output[...] = r.returned[...].astype(F32)
    else:
        spread.finish()
        scatter.finish()


GRADS = ("proj", "spec", "mlp", "small")


def of(r, prefix):
    return [getattr(r, prefix + n) for n in GRADS]


def totals_of(grads):
    return {"t_" + n: ((grads[n].shape[0] // 8, grads[n].shape[1]), BF) for n in GRADS}


def ffn_backward(l, fwd, carried, last, shard, pending):
    layers, rows, width = fwd.mids.shape
    units = fwd.w_gate_out.shape[2]
    full = rows * 4
    big = pltpu.VMEM((full, units), BF)
    held = ("w_gate_out", "w_up_out", "w_down_out", "s_units", "s_h_ffn")
    ins = dict(carried=carried, mids=fwd.mids, gains=fwd.gains)
    ins.update({n: getattr(fwd, n) for n in held})
    outs = dict(
        mid_grad=((rows, width), F32),
        weight_grads=((3 * width, units), BF),
        gain_grad=((1, width), F32),
    )
    hbm = held
    if last:
        ins.update(values=fwd.values)
        outs.update(output=((full, shard), F32))
        scratch = dict(
            leaving=pltpu.VMEM((4, rows, shard), BF),
            returned=pltpu.VMEM((full, shard), BF),
            **Return.scratch(),
        )
    else:
        grads, ffn_total = pending
        ins.update(ffn_total=ffn_total, **{"g_" + n: grads[n] for n in GRADS})
        outs.update(
            ffn_result=((8 * ffn_total.shape[0], ffn_total.shape[1]), BF),
            **totals_of(grads),
        )
        scratch = dict(**Spread.scratch(1), **Scatter.scratch([grads[n].shape for n in GRADS]))
        hbm += tuple("g_" + n for n in GRADS)
    return call_kernel(
        functools.partial(ffn_backward_body, l, last),
        ins,
        outs,
        dict(
            near_part=pltpu.VMEM((rows, width), F32),
            own_part=pltpu.VMEM((rows, width), F32),
            g_all=pltpu.VMEM((full, width), BF),
            h_all=pltpu.VMEM((full, width), BF),
            units=pltpu.VMEM((2, full, units), BF),
            w_gate=pltpu.VMEM((width, units), BF),
            w_up=pltpu.VMEM((width, units), BF),
            w_down=pltpu.VMEM((units, width), BF),
            load_sem=pltpu.SemaphoreType.DMA((5,)),
            hidden_all=big,
            gate_grads=big,
            up_grads=big,
            **Group.scratch(rows, width),
            **scratch,
        ),
        20 + l,
        12 * full * width * units,
        hbm,
    )


def mixer_backward_body(l, above, r):
    bottom = l == 0
    place = Place()
    rows = r.mid_grad.shape[0]
    length, width = r.h_all.shape
    lanes = r.w_in.shape[3]
    groups, feats, units = r.w_ci.shape[1:]
    half = feats // 2
    wide = r.both_re.shape[1] // 2
    tiles = 4
    size = length // tiles
    group = Group(place, r, rows)
    load = Load(
        r,
        [
            (r.w_out_out.at[l], r.w_out.at[0]),
            (r.w_ci_out.at[l], r.w_ci.at[0]),
            (r.w_co_out.at[l], r.w_co.at[0]),
            (r.s_mix.at[l], r.mix),
            (r.s_pre.at[l], r.pre_all),
            (r.w_in_out.at[l], r.w_in.at[0]),
            (r.s_h_mixer.at[l], r.h_all),
            (r.cosine, r.cos),
            (r.sine, r.sin),
            (r.values.at[l], r.layer_in),
        ],
    )
    load.start()
    r.m_all[group.at(0)] = r.mid_grad[...].astype(BF)
    place.barrier()
    group.gather_start(r.m_all)
    ffn_scatter = Scatter(place, r, [r.ffn_grads], [r.ffn_total], "fs")
    ffn_scatter.start()
    if above:
        spread = Spread(place, r, of(r, "t_"), of(r, "r_"))
        spread.start()
    if bottom:
        scatter = Scatter(place, r, of(r, "g_"), of(r, "u_"))
        ffn_spread = Spread(place, r, [r.ffn_total], [r.ffn_result], "fp")
        mix_spread = Spread(place, r, of(r, "u_"), of(r, "q_"), "mp")
    for s in range(3):
        r.padded[s, 0:PAD] = jnp.zeros((PAD, lanes), F32)
        r.padded[s, PAD + length : 2 * PAD + length] = jnp.zeros((PAD, lanes), F32)
    r.both_re[...] = jnp.zeros_like(r.both_re)
    r.both_im[...] = jnp.zeros_like(r.both_im)
    r.sum_in[...] = jnp.zeros_like(r.sum_in)
    r.sum_out[...] = jnp.zeros_like(r.sum_out)
    load.finish()
    mlp_tables(r, 0)

    def gated_back(which, chunk=None):
        at = group.at(which, chunk)
        gated_grad = nt_dot(r.m_all[at], r.w_out[0])
        to = pl.ds(pl.multiple_of(at.start + PAD, 8), at.size)
        r.padded[0, to] = gated_grad * r.mix[MIXED, at].astype(F32)
        r.q_g[at] = (gated_grad * r.mix[QUERY, at].astype(F32)).astype(BF)

    gated_back(0)
    group.gather_peer(r.m_all)
    gated_back(2)
    for chunk in range(CHUNKS):
        group.gather_near(r.m_all, chunk)
        gated_back(1, chunk)
        group.gather_diagonal(r.m_all, chunk)
        gated_back(3, chunk)

    @pl.loop(0, tiles)
    def _(t):
        at = aligned(t, size)
        real = nn_dot(r.cos[at], r.q_g[...])
        imag = nn_dot(r.sin[at], r.q_g[...])
        value_re, value_im, kernel_re, kernel_im = [
            r.mix[SPECTRA + i, at].astype(F32) for i in range(4)
        ]
        kernel_re_grad = real * value_re + imag * value_im
        kernel_im_grad = imag * value_re - real * value_im
        r.both_re[at, 0:lanes] = (real * kernel_re + imag * kernel_im).astype(BF)
        r.both_im[at, 0:lanes] = (imag * kernel_re - real * kernel_im).astype(BF)
        r.g_spec[at] = jnp.concatenate([kernel_re_grad, kernel_im_grad], 1).astype(BF)
        kernel_re_grad = kernel_re_grad.astype(BF)
        kernel_im_grad = kernel_im_grad.astype(BF)
        pre = r.pre_all[at].astype(F32)
        cdf = normal_cdf(pre)
        inner = (pre * cdf).astype(BF)
        inner_grad = nn_dot(kernel_re_grad, r.out_re[...]) + nn_dot(kernel_im_grad, r.out_im[...])
        pre_grad = (inner_grad * (cdf + pre * normal_pdf(pre))).astype(BF)
        r.both_re[at, wide : wide + lanes] = nt_dot(pre_grad, r.in_re[...]).astype(BF)
        r.both_im[at, wide : wide + lanes] = nt_dot(pre_grad, r.in_im[...]).astype(BF)
        r.sum_out[0] += tn_dot(kernel_re_grad, inner)
        r.sum_out[1] += tn_dot(kernel_im_grad, inner)
        r.sum_in[0] += tn_dot(r.mix[SPECTRA + 4, at], pre_grad)
        r.sum_in[1] += tn_dot(r.mix[SPECTRA + 5, at], pre_grad)

    ffn_scatter.second()
    if above:
        spread.forward()
    for g in range(groups):
        rows_at, cols = slice(g * half, (g + 1) * half), slice(g * units, (g + 1) * units)
        at = g * feats
        r.g_mlp[at : at + half] = r.sum_in[0, rows_at, cols].astype(BF)
        r.g_mlp[at + half : at + feats] = r.sum_in[1, rows_at, cols].astype(BF)
        turned = jnp.concatenate([r.sum_out[0, rows_at, cols], r.sum_out[1, rows_at, cols]], 0)
        at += groups * feats
        r.g_mlp[at : at + units] = turned.T.astype(BF)
    if bottom:
        scatter.start((1, 2))

    @pl.loop(0, tiles)
    def _(t):
        at = aligned(t, size)
        both = nn_dot(r.cos[at], r.both_re[...]) + nn_dot(r.sin[at], r.both_im[...])
        to = pl.ds(pl.multiple_of(t * size + PAD, 8), size)
        r.padded[1, to] = both[:, :lanes]
        r.padded[2, to] = both[:, wide : wide + lanes]

    def tap(o, s):
        at = 9 * l + 3 * o + s
        return r.taps[at : at + 1]

    totals = [[None] * 3 for _ in range(3)]
    for t in range(tiles):
        at = pl.ds(t * size, size)
        prev = r.mask_prev[at]
        following = r.mask_next[at]
        for s in range(3):
            here = shifted(r.padded, s, t, size, 0)
            after = shifted(r.padded, s, t, size, 1) * following
            before = shifted(r.padded, s, t, size, -1) * prev
            r.proj_grads[s, at] = (
                tap(0, s) * after + tap(1, s) * here + tap(2, s) * before
            ).astype(BF)
            proj = r.mix[PROJ + s, at].astype(F32)
            for o, g in enumerate((after, here, before)):
                part = jnp.sum(g * proj, 0, keepdims=True)
                totals[o][s] = part if t == 0 else totals[o][s] + part
    ffn_scatter.middle()

    def feats_grad(which):
        at = group.at(which)
        return sum(nt_dot(r.proj_grads[s, at], r.w_in[0, s]) for s in range(3))

    group.reduce_whole("diagonal", feats_grad(3))
    group.reduce_whole("near", feats_grad(1))
    group.reduce_whole("peer", feats_grad(2))
    for s in range(3):
        r.g_proj[s * lanes : (s + 1) * lanes] = tn_dot(r.proj_grads[s], r.h_all[...]).astype(BF)
    r.g_proj[3 * lanes :] = tn_dot(r.mix[GATED], r.m_all[...]).astype(BF)
    if bottom:
        scatter.start((0,))
        scatter.second((1, 2))
    r.own_part[...] = feats_grad(0)
    for chunk in range(CHUNKS):
        r.own_part[group.piece(chunk)] += group.reduce_end(chunk)
    grad, gain_part = norm_grad_rows(r.own_part[...], r.layer_in[...], r.gains[l : l + 1])
    carried = r.mid_grad[...] + grad
    if bottom:
        shard = r.returned.shape[1]
        for j in range(4):
            r.leaving[j] = carried[:, j * shard : (j + 1) * shard].astype(BF)
        back = Return(place, r, r.leaving, r.returned)
        back.start()
    else:
        r.carried[...] = carried
    r.small_rows[...] = jnp.zeros_like(r.small_rows)
    small = [totals[o][s] for o in range(3) for s in range(3)] + [gain_part, r.gain_two[...]]
    at = 0
    for x in small:
        for start in range(0, x.shape[1], 128):
            part = x[:, start : start + 128]
            r.small_rows[at : at + 1, 0 : part.shape[1]] = part
            at += 1
    r.g_small[...] = jnp.zeros_like(r.g_small)
    r.g_small[0 : r.small_rows.shape[0]] = r.small_rows[...].astype(BF)
    if bottom:
        scatter.start((3,))
    ffn_scatter.finish()
    if bottom:
        ffn_spread.start()
        scatter.middle((1, 2))
        scatter.second((0, 3))
        scatter.finish((1, 2))
        mix_spread.start((1, 2))
        scatter.middle((0, 3))
        ffn_spread.forward()
        scatter.finish((0, 3))
        mix_spread.start((0, 3))
        mix_spread.forward((1, 2))
        back.finish()
        r.stream_grad[...] = r.returned[...].astype(F32)
        mix_spread.forward((0, 3))
        mix_spread.finish((3,))
        if above:
            spread.finish()
        gain_sums(place, r, above)
        mix_spread.finish((0, 1, 2))
        ffn_spread.finish()
    elif above:
        spread.finish()
    group.finish()


def gain_sums(place, r, above):
    count = r.small_rows.shape[0]
    r.gain_parts[0, 0] = r.q_small[0:count]
    if above:
        r.gain_parts[0, 1] = r.r_small[0:count]

    def gain_copy(j):
        chan = lax.rem(place.chan + j, 4)
        return remote(
            r.gain_parts.at[0], r.gain_parts.at[j], r.gain_send.at[j], r.gain_recv.at[j], {"chan": chan}
        )

    for j in range(1, 4):
        gain_copy(j).start()
    for j in range(1, 4):
        gain_copy(j).wait()
    total = r.gain_parts[0].astype(F32)
    for j in range(1, 4):
        total += r.gain_parts[j].astype(F32)
    r.gain_grads[...] = total


def mixer_backward(l, fwd, mid_grad, tables, gain_two, ffn_grads, pending):
    rows, width = mid_grad.shape
    layers, _, length, lanes = fwd.s_mix.shape
    groups, feats, units = fwd.w_ci_out.shape[1:]
    inner = groups * units
    wide = -(-lanes // 128) * 128
    above = pending is not None
    held = ("w_out_out", "w_ci_out", "w_co_out", "s_mix", "s_pre", "w_in_out", "s_h_mixer")
    ins = dict(
        mid_grad=mid_grad, values=fwd.values, gains=fwd.gains, taps=fwd.taps_out,
        mask_prev=fwd.mask_prev, mask_next=fwd.mask_next, cosine=tables[0], sine=tables[1],
        gain_two=gain_two, ffn_grads=ffn_grads, **{n: getattr(fwd, n) for n in held},
    )
    grads = dict(
        g_proj=((4 * lanes, width), BF),
        g_spec=((length, 2 * lanes), BF),
        g_mlp=((2 * groups * feats, units), BF),
        g_small=((256, 128), BF),
    )
    shapes = [g[0] for g in grads.values()]
    ffn_total = ((ffn_grads.shape[0] // 8, ffn_grads.shape[1]), BF)
    outs, scratch = {}, Scatter.scratch([ffn_grads.shape], "fs")
    hbm = held + ("ffn_grads", "cosine", "sine", "values")
    if above:
        ins.update(**{"t_" + n: pending[n] for n in GRADS})
        outs.update(
            **{"r_" + n: ((pending[n].shape[0] * 8, pending[n].shape[1]), BF) for n in GRADS}
        )
        scratch.update(Spread.scratch(len(GRADS)))
    count = 32
    if l == 0:
        shard = lanes
        outs.update(
            stream_grad=((length, shard), F32),
            gain_grads=((2 if above else 1, count, 128), F32),
            ffn_result=(ffn_grads.shape, BF),
            **{"q_" + n: grads["g_" + n] for n in GRADS},
        )
        scratch.update(
            ffn_total=pltpu.VMEM(*ffn_total),
            leaving=pltpu.VMEM((4, rows, shard), BF),
            returned=pltpu.VMEM((length, shard), BF),
            gain_parts=pltpu.VMEM((4, 2 if above else 1, count, 128), BF),
            gain_send=pltpu.SemaphoreType.DMA((4,)),
            gain_recv=pltpu.SemaphoreType.DMA((4,)),
            **{n: pltpu.VMEM(*g) for n, g in grads.items()},
            **{
                "u_" + n: pltpu.VMEM((g[0][0] // 8, g[0][1]), BF)
                for n, g in zip(GRADS, grads.values())
            },
            **Return.scratch(),
            **Scatter.scratch(shapes),
            **Spread.scratch(1, "fp"),
            **Spread.scratch(len(GRADS), "mp"),
        )
    else:
        outs.update(carried=((rows, width), F32), ffn_total=ffn_total, **grads)
    return call_kernel(
        functools.partial(mixer_backward_body, l, above),
        ins,
        outs,
        dict(
            m_all=pltpu.VMEM((length, width), BF),
            h_all=pltpu.VMEM((length, width), BF),
            mix=pltpu.VMEM((MIX_ROWS, length, lanes), BF),
            pre_all=pltpu.VMEM((length, inner), BF),
            w_in=pltpu.VMEM((1,) + fwd.w_in_out.shape[1:], BF),
            w_out=pltpu.VMEM((1,) + fwd.w_out_out.shape[1:], BF),
            w_ci=pltpu.VMEM((1,) + fwd.w_ci_out.shape[1:], F32),
            w_co=pltpu.VMEM((1,) + fwd.w_co_out.shape[1:], F32),
            cos=pltpu.VMEM((length, length), BF),
            sin=pltpu.VMEM((length, length), BF),
            load_sem=pltpu.SemaphoreType.DMA((10,)),
            layer_in=pltpu.VMEM((rows, width), F32),
            padded=pltpu.VMEM((3, length + 2 * PAD, lanes), F32),
            q_g=pltpu.VMEM((length, lanes), BF),
            both_re=pltpu.VMEM((length, 2 * wide), BF),
            both_im=pltpu.VMEM((length, 2 * wide), BF),
            proj_grads=pltpu.VMEM((3, length, lanes), BF),
            own_part=pltpu.VMEM((rows, width), F32),
            sum_in=pltpu.VMEM((2, lanes, inner), F32),
            sum_out=pltpu.VMEM((2, lanes, inner), F32),
            small_rows=pltpu.VMEM((count, 128), F32),
            **mlp_scratch(lanes, inner),
            **Group.scratch(rows, width),
            **scratch,
        ),
        40 + l,
        9 * 10**9,
        hbm,
    )


def on_device(
    stream,
    segments,
    cotangent,
    norm_one,
    in_proj,
    short_taps,
    cond_in,
    cond_out,
    filter_spec,
    out_proj,
    norm_two,
    gate_proj,
    up_proj,
    down_proj,
):
    chan = lax.axis_index("chan")
    layers, width = in_proj.shape[:2]
    shard = norm_one.shape[1]
    length = filter_spec.shape[2]
    groups, feats = cond_in.shape[1:3]
    tables = dft_tables(length)
    arrays = dict(
        in_proj=in_proj.transpose(0, 2, 1, 3),
        cond_in=cond_in,
        cond_out=cond_out,
        filter_spec=filter_spec,
        out_proj=out_proj,
        gate_proj=gate_proj,
        up_proj=up_proj,
        down_proj=down_proj,
    )

    fwd = forward(
        arrays,
        stream,
        cotangent,
        segments[:, None],
        jnp.concatenate([norm_one, norm_two], 0),
        short_taps.reshape(-1, shard),
        tables,
    )
    carried = fwd.carried
    ffn_results, mixer_results = {}, {}
    grads, ffn_total, output = None, None, None
    for l in reversed(range(layers)):
        last = l + 1 == layers
        back = ffn_backward(
            l, fwd, carried, last, shard, None if last else (grads, ffn_total)
        )
        if last:
            output, pending = back.output, None
        else:
            ffn_results[l + 1] = back.ffn_result
            pending = {n: getattr(back, "t_" + n) for n in GRADS}
        down = mixer_backward(
            l, fwd, back.mid_grad, tables, back.gain_grad, back.weight_grads, pending
        )
        if not last:
            mixer_results[l + 1] = {n: getattr(down, "r_" + n) for n in GRADS}
        if l > 0:
            carried, ffn_total = down.carried, down.ffn_total
            grads = {n: getattr(down, "g_" + n) for n in GRADS}
    ffn_results[0] = down.ffn_result
    mixer_results[0] = {n: getattr(down, "q_" + n) for n in GRADS}

    def everywhere(x):
        return lax.psum(x, "outer") if lax.axis_size("outer") > 1 else x

    def stacked(get):
        return everywhere(jnp.stack([get(l) for l in range(layers)])).astype(F32)

    def mixer_stack(name, get):
        return stacked(lambda l: get(mixer_results[l][name]))

    def ffn_stack(index):
        return stacked(lambda l: ffn_results[l][index * width : (index + 1) * width])

    gain_grads = everywhere(down.gain_grads)
    steps = -(-shard // 128)
    taps_rows, gain_rows = 9 * steps, width // 128

    def gain_stack(at):
        whole = gain_grads[:, at : at + gain_rows].reshape(layers, width)
        return lax.dynamic_slice_in_dim(whole, chan * shard, shard, 1)

    mlp_rows = groups * feats
    return (
        output,
        down.stream_grad,
        gain_stack(taps_rows),
        mixer_stack("proj", lambda x: x[: 3 * shard].reshape(3, shard, width).transpose(2, 0, 1)),
        mixer_stack(
            "small",
            lambda x: x[:taps_rows].reshape(9, steps * 128)[:, :shard].reshape(short_taps.shape[1:]),
        ),
        mixer_stack("mlp", lambda x: x[:mlp_rows].reshape(cond_in.shape[1:])),
        mixer_stack("mlp", lambda x: x[mlp_rows:].reshape(cond_out.shape[1:])),
        mixer_stack("spec", lambda x: jnp.stack([x[:, :shard], x[:, shard:]])),
        mixer_stack("proj", lambda x: x[3 * shard :]),
        gain_stack(taps_rows + gain_rows),
        ffn_stack(0),
        ffn_stack(1),
        ffn_stack(2),
    )


def solution(mesh):
    dp_count, chan_count = mesh.devices.shape
    fine = Mesh(
        mesh.devices.reshape(dp_count // 8, 4, 2, chan_count), ("outer", "col", "half", "chan")
    )
    dp = ("outer", "col", "half")
    weight_specs = (
        P(None, "chan"),
        P(None, None, None, "chan"),
        P(None, None, None, "chan"),
        P(None, "chan", None, None),
        P(None, "chan", None, None),
        P(None, None, None, "chan"),
        P(None, "chan", None),
        P(None, "chan"),
        P(None, None, "chan"),
        P(None, None, "chan"),
        P(None, "chan", None),
    )
    return jax.shard_map(
        on_device,
        mesh=fine,
        in_specs=(P(dp, "chan"), P(dp), P(dp, "chan")) + weight_specs,
        out_specs=(P(dp, "chan"), P(dp, "chan")) + weight_specs,
        check_vma=False,
    )
```

time: 665 us -> 524 us (0.79)
  Pallas kernels: 618 us -> 469 us
  local copies, waits for them, and re-layouts: 25.7 us -> 32.5 us
    pallas_call x10 -> x5, Pallas kernels: 618 us -> 469 us  [call_kernel(): pl.pallas_call(run, out_shape=[jax.ShapeDtypeStruct(*o) for o in outs.val...]
    unnamed x42 -> x34, local copies, waits for them, and re-layouts: 14.7 us -> 24.9 us
    convert_element_type x7 -> x8, other arithmetic: 13.4 us -> 14.1 us  [stacked(): return everywhere(jnp.stack([get(l) for l in range(layers)])).astype(F32)]
where the time goes in v2:
time: 524 us; the launch traced here: 518 us
  Pallas kernels  469 us (90%)
  local copies, waits for them, and re-layouts  32.5 us (6%)
  other arithmetic  15.1 us (3%)
    pallas_call x5, Pallas kernels, call_kernel(): pl.pallas_call(run, out_shape=[jax.ShapeDtypeStruct(*o) for o in outs.val...  469 us
    unnamed x34, local copies, waits for them, and re-layouts  24.9 us
    convert_element_type x8, other arithmetic, stacked(): return everywhere(jnp.stack([get(l) for l in range(layers)])).astype(F32)  14.1 us

profile of v2, /device:TPU:0, one launch (start us, length us, event | category | flops | bytes accessed | tf_op | source)
XLA Modules:
  0.0 517.5 jit_solution(4083787579959818440)
XLA Ops:
  0.7 2.0 copy.39.refs_0_
  2.7 2.0 copy.40.refs_1_
  4.7 1.9 copy.41.refs_2_
  7.8 4.0 copy.38
  11.8 3.4 copy.42.refs_10_
  15.2 190.2 %shard_map.255 = (f32[3,256,768]{2,1,0:T(8,128)}, f32[2,256,768]{2,1,0:T(8,128)}, f32[256,768]{1,0:T(8,128)}, f32[4,768]{1,0:T(4,128)}, f32[18,192]{1,0:T(8,128)...) custom-call(bf16[1024,192]{1,0:T(8,128)(2,1)} %copy.39.refs_0_, ...), custom_call_target="tpu_custom_call" | custom-call | flops 30000001024 | bytes 20971520 | tf_op jit(solution)/shard_map/pallas_call | solution.py:616
  205.4 36.1 %shard_map.256 = (f32[256,768]{1,0:T(8,128)}, bf16[2304,768]{1,0:T(8,128)(2,1)}, f32[1,768]{1,0:T(1,128)}, f32[1024,192]{1,0:T(8,128)}) custom-call(f32[256,768]{1,0:T(8,128)} %get-tuple-element.61.refs_0_, f32[2,256,768]{2,1,0:T(8,128)} %get-tuple-element.62.refs_1_, f32[4,768]{1,0:T(4,128)} %get-tuple-element.63.refs_2_, ...), custom_call_target="tpu_custom_call" | custom-call | flops 7247757312 | bytes 20971520 | tf_op jit(solution)/shard_map/pallas_call | solution.py:616
  241.5 2.4 copy.43
  243.9 58.9 %shard_map.257 = (f32[256,768]{1,0:T(8,128)}, bf16[288,768]{1,0:T(8,128)(2,1)}, bf16[768,768]{1,0:T(8,128)(2,1)}, bf16[1024,384]{1,0:T(8,128)(2,1)}, bf16[768,128]{1,0:T(8,128)(2,1)}, /*index=5*/bf16[256,128]{1,0:T(8,128)(2,1)}) custom-call(f32[256,768]{1,0:T(8,128)} %get-tuple-element.71.refs_0_, f32[3,256,768]{2,1,0:T(8,128)} %get-tuple-element.69.refs_8_.refs_1_, ...), custom_call_target="tpu_custom_call" | custom-call | flops 8999999488 | bytes 20971520 | tf_op jit(solution)/shard_map/pallas_call | solution.py:616
  302.8 62.8 %shard_map.258 = (f32[256,768]{1,0:T(8,128)}, bf16[2304,768]{1,0:T(8,128)(2,1)}, f32[1,768]{1,0:T(1,128)}, bf16[2304,768]{1,0:T(8,128)(2,1)}, bf16[96,768]{1,0:T...) custom-call(f32[256,768]{1,0:T(8,128)} %get-tuple-element.84.refs_0_, ...), custom_call_target="tpu_custom_call" | custom-call | flops 7247757312 | bytes 20971520 | tf_op jit(solution)/shard_map/pallas_call | solution.py:616
  365.7 120.9 %shard_map.259 = (bf16[768,768]{1,0:T(8,128)(2,1)}, bf16[1024,384]{1,0:T(8,128)(2,1)}, bf16[768,128]{1,0:T(8,128)(2,1)}, bf16[256,128]{1,0:T(8,128)(2,1)}, f32[1...) custom-call(f32[256,768]{1,0:T(8,128)} %get-tuple-element.90.refs_0_, ...), custom_call_target="tpu_custom_call" | custom-call | flops 8999999488 | bytes 20971520 | tf_op jit(solution)/shard_map/pallas_call | solution.py:616
  486.6 2.6 copy.44
  489.2 0.7 slice_bitcast_fusion.12
  490.8 2.0 maximum_convert_fusion.4
  492.8 0.8 slice.77
  495.0 0.8 maximum_convert_fusion.6
  495.8 0.8 maximum_convert_fusion.7
  497.5 2.6 maximum_convert_fusion.3
  500.0 5.4 %copy.46 = f32[2,2,1024,192]{2,3,1,0:T(8,128)} copy(f32[2,2,1024,192]{3,2,1,0:T(8,128)} %maximum_convert_fusion.3) | data formatting | bytes 6291456
  505.4 1.1 slice_bitcast_fusion.10
  506.5 1.1 maximum_convert_fusion.5
  508.5 1.8 copy-done.1
  510.5 4.3 maximum_convert_fusion
  514.8 2.5 maximum_convert_fusion.2
  (44 shorter events, 5.5 us)
Async XLA Ops:
  0.6 5.9 %copy-start.10 = (f32[2,192]{1,0:T(2,128)S(1)}, f32[2,192]{1,0:T(2,128)}, u32[]{:S(2)}) copy-start(f32[2,192]{1,0:T(2,128)} %param.26) | copy-start | bytes 4612
  0.7 5.9 %copy-start.11 = (f32[2,192]{1,0:T(2,128)S(1)}, f32[2,192]{1,0:T(2,128)}, u32[]{:S(2)}) copy-start(f32[2,192]{1,0:T(2,128)} %param.19) | copy-start | bytes 4612
  0.7 6.5 %copy-start.9 = (f32[2,3,3,192]{3,0,2,1:T(2,128)S(1)}, f32[2,3,3,192]{3,0,2,1:T(2,128)}, u32[]{:S(2)}) copy-start(f32[2,3,3,192]{3,0,2,1:T(2,128)} %param.21) | copy-start | bytes 41476
  4.7 7.1 %copy-start.2 = (f32[2,2,1024,192]{2,3,1,0:T(8,128)S(1)}, f32[2,2,1024,192]{2,3,1,0:T(8,128)}, u32[]{:S(2)}) copy-start(f32[2,2,1024,192]{2,3,1,0:T(8,128)} %param.24) | copy-start | bytes 9437188
  486.6 4.0 copy-start.5
  486.6 4.0 copy-start.6
  490.7 4.3 copy-start.7
  490.7 4.2 copy-start.8
  492.8 3.8 copy-start.3
  492.8 3.8 copy-start.4
  500.0 8.2 %copy-start = (bf16[2304,768]{1,0:T(8,128)(2,1)S(1)}, bf16[2304,768]{1,0:T(8,128)(2,1)}, u32[]{:S(2)}) copy-start(bf16[2304,768]{1,0:T(8,128)(2,1)} %get-tuple-element.108) | copy-start | bytes 10616836
  508.2 2.0 copy-start.1

commit v3 on v2

--- a/solution.py
+++ b/solution.py
@@ -34,7 +34,7 @@
 
 
 MESH = pl.DeviceIdType.MESH
-VMEM_LIMIT = 58 << 20
+VMEM_LIMIT = 63 << 20
 CHUNKS = 2
 PARTS = 8
 
@@ -114,8 +114,8 @@
         self.near = {"chan": place.near_chan}
         self.peer = {"half": place.other_half}
         self.send, self.recv = r.group_send.at[turn], r.group_recv.at[turn]
-        self.to_peer, self.from_peer = r.to_peer.at[turn], r.from_peer.at[turn]
-        self.to_near, self.from_near = r.to_near.at[turn], r.from_near.at[turn]
+        self.to_peer, self.from_peer = r.to_peer, r.from_peer.at[turn]
+        self.to_near, self.from_near = r.to_near, r.from_near.at[turn]
         self.rows, self.size = rows, rows // CHUNKS
         self.started = []
 
@@ -124,9 +124,9 @@
         return dict(
             group_send=pltpu.SemaphoreType.DMA((turns, 6, CHUNKS)),
             group_recv=pltpu.SemaphoreType.DMA((turns, 6, CHUNKS)),
-            to_peer=pltpu.VMEM((turns, 2, rows, width), BF),
+            to_peer=pltpu.VMEM((2, rows, width), BF),
             from_peer=pltpu.VMEM((turns, 2, rows, width), BF),
-            to_near=pltpu.VMEM((turns, rows, width), BF),
+            to_near=pltpu.VMEM((rows, width), BF),
             from_near=pltpu.VMEM((turns, rows, width), BF),
         )
 
@@ -209,10 +209,14 @@
     def index(self, parts, col, half):
         return col * 2 + half if parts == 8 else col
 
-    def each_sent(self, act):
+    def each(self, which):
+        which = range(len(self.pairs)) if which is None else which
+        return [(a, self.pairs[a]) for a in which]
+
+    def each_sent(self, act, which=None):
         p = self.place
         owner = {"half": p.pack, "chan": p.far_chan}
-        for a, (src, dst, axis, parts) in enumerate(self.pairs):
+        for a, (src, dst, axis, parts) in self.each(which):
 
             def send(a=a, src=src, dst=dst, axis=axis, parts=parts):
                 index = self.index(parts, p.col, p.half)
@@ -231,20 +235,20 @@
             else:
                 pl.when(p.half == 0)(send)
 
-    def start(self):
-        self.each_sent(lambda c: c.start())
+    def start(self, which=None):
+        self.each_sent(lambda c: c.start(), which)
 
         @pl.when(self.place.own)
         def _():
-            for a, (src, dst, axis, parts) in enumerate(self.pairs):
+            for a, (src, dst, axis, parts) in self.each(which):
                 pltpu.make_async_copy(src, dst, self.local.at[a]).start()
 
-    def forward(self):
+    def forward(self, which=None):
         p = self.place
 
         @pl.when(jnp.logical_not(p.own))
         def _():
-            for a, (src, dst, axis, parts) in enumerate(self.pairs):
+            for a, (src, dst, axis, parts) in self.each(which):
                 for s in range(parts // 4):
                     piece = self.cut(dst, axis, parts, self.index(parts, p.col, s))
                     await_recv(piece, self.recv.at[a, s], self.send.at[a, 0])
@@ -259,18 +263,15 @@
 
     def ready(self, which=None):
         p = self.place
-        which = range(len(self.pairs)) if which is None else which
 
         @pl.when(p.own)
         def _():
-            for a in which:
-                src, dst, axis, parts = self.pairs[a]
+            for a, (src, dst, axis, parts) in self.each(which):
                 pltpu.make_async_copy(src, dst, self.local.at[a]).wait()
 
         @pl.when(jnp.logical_not(p.own))
         def _():
-            for a in which:
-                src, dst, axis, parts = self.pairs[a]
+            for a, (src, dst, axis, parts) in self.each(which):
                 for s in range(parts // 4):
                     for j in range(1, 4):
                         piece = self.cut(dst, axis, parts, self.index(parts, p.col_at(4 - j), s))
@@ -290,9 +291,10 @@
 
 
 class Load:
-    def __init__(self, r, pairs):
+    def __init__(self, r, pairs, first=0):
         self.copies = [
-            pltpu.make_async_copy(src, dst, r.load_sem.at[a]) for a, (src, dst) in enumerate(pairs)
+            pltpu.make_async_copy(src, dst, r.load_sem.at[first + a])
+            for a, (src, dst) in enumerate(pairs)
         ]
 
     def start(self):
@@ -356,17 +358,18 @@
 
 
 class Return:
-    def __init__(self, place, r, src, dst):
+    def __init__(self, place, r, src, dst, turn):
         self.place, self.src, self.dst = place, src, dst
-        self.send, self.recv, self.local = r.back_send, r.back_recv, r.back_local
+        self.send, self.recv = r.back_send.at[turn], r.back_recv.at[turn]
+        self.local = r.back_local.at[turn]
         self.size = src.shape[1]
 
     @staticmethod
     def scratch():
         return dict(
-            back_send=pltpu.SemaphoreType.DMA((4,)),
-            back_recv=pltpu.SemaphoreType.DMA((4,)),
-            back_local=pltpu.SemaphoreType.DMA,
+            back_send=pltpu.SemaphoreType.DMA((2, 4)),
+            back_recv=pltpu.SemaphoreType.DMA((2, 4)),
+            back_local=pltpu.SemaphoreType.DMA((2,)),
         )
 
     def each(self, act, act_self):
@@ -407,30 +410,33 @@
 
 
 class Scatter:
-    def __init__(self, place, r, sources, totals, name="sc"):
+    def __init__(self, place, r, sources, totals, name, turn):
         self.place, self.sources, self.totals = place, sources, totals
-        self.send, self.recv = getattr(r, name + "_send"), getattr(r, name + "_recv")
-        self.local = getattr(r, name + "_local")
+        self.send, self.recv, self.local = [
+            getattr(r, f"{name}_{n}").at[turn] for n in ("send", "recv", "local")
+        ]
         self.kept, self.got, self.late, self.cross = [
             [getattr(r, f"{name}_{part}{a}") for a in range(len(sources))]
             for part in ("kept", "got", "late", "cross")
         ]
+        self.cross = [c.at[turn] for c in self.cross]
         self.x = lax.rem(place.col, 2)
         self.y = place.col // 2
         self.to_x = {"col": place.col + 1 - 2 * self.x}
         self.to_y = {"col": lax.rem(place.col + 2, 4)}
 
     @staticmethod
-    def scratch(shapes, name="sc"):
+    def scratch(shapes, name, turns):
         n = len(shapes)
         out = {
-            f"{name}_send": pltpu.SemaphoreType.DMA((n, 8)),
-            f"{name}_recv": pltpu.SemaphoreType.DMA((n, 8)),
-            f"{name}_local": pltpu.SemaphoreType.DMA((n, 4)),
+            f"{name}_send": pltpu.SemaphoreType.DMA((turns, n, 8)),
+            f"{name}_recv": pltpu.SemaphoreType.DMA((turns, n, 8)),
+            f"{name}_local": pltpu.SemaphoreType.DMA((turns, n, 4)),
         }
         for a, (rows, width) in enumerate(shapes):
-            for part, count in (("kept", 4), ("got", 4), ("late", 2), ("cross", 2)):
+            for part, count in (("kept", 4), ("got", 4), ("late", 2)):
                 out[f"{name}_{part}{a}"] = pltpu.VMEM((count, rows // 8, width), BF)
+            out[f"{name}_cross{a}"] = pltpu.VMEM((turns, 2, rows // 8, width), BF)
         return out
 
     def each(self, which):
@@ -466,9 +472,12 @@
             remote(kept.at[3 - self.x], late.at[1], self.send.at[a, 5], self.recv.at[a, 5], self.to_x),
         ]
 
+    def summed(self, part):
+        return self.y + part * (2 + self.x - self.y)
+
     def third(self, a, slot, part, half, chan):
         return remote(
-            self.got[a].at[part],
+            self.kept[a].at[self.summed(part)],
             self.cross[a].at[slot],
             self.send.at[a, 6 + slot],
             self.recv.at[a, 6 + slot],
@@ -495,9 +504,10 @@
         for a in self.each(which):
             for copy in self.seconds(a):
                 copy.wait()
-            kept, late, got = self.kept[a], self.late[a], self.got[a]
-            got[0] = (kept[self.y].astype(F32) + late[0].astype(F32)).astype(BF)
-            got[1] = (kept[2 + self.x].astype(F32) + late[1].astype(F32)).astype(BF)
+            kept, late = self.kept[a], self.late[a]
+            for part in range(2):
+                at = self.summed(part)
+                kept[at] = (kept[at].astype(F32) + late[part].astype(F32)).astype(BF)
 
             @pl.when(p.own)
             def _():
@@ -518,7 +528,7 @@
             @pl.when(p.own)
             def _():
                 self.totals[a][...] = (
-                    cross[0].astype(F32) + self.got[a][p.half].astype(F32)
+                    cross[0].astype(F32) + self.kept[a][self.summed(p.half)].astype(F32)
                 ).astype(BF)
 
             @pl.when(jnp.logical_not(p.own))
@@ -529,18 +539,18 @@
 
 
 class Spread:
-    def __init__(self, place, r, totals, results, name="sp"):
+    def __init__(self, place, r, totals, results, name, turn):
         self.place, self.totals, self.results = place, totals, results
         self.send, self.recv, self.kept = [
-            getattr(r, f"{name}_{n}") for n in ("send", "recv", "local")
+            getattr(r, f"{name}_{n}").at[turn] for n in ("send", "recv", "local")
         ]
 
     @staticmethod
-    def scratch(count, name="sp"):
+    def scratch(count, name, turns):
         return {
-            f"{name}_send": pltpu.SemaphoreType.DMA((count, 7)),
-            f"{name}_recv": pltpu.SemaphoreType.DMA((count, 7)),
-            f"{name}_local": pltpu.SemaphoreType.DMA((count,)),
+            f"{name}_send": pltpu.SemaphoreType.DMA((turns, count, 7)),
+            f"{name}_recv": pltpu.SemaphoreType.DMA((turns, count, 7)),
+            f"{name}_local": pltpu.SemaphoreType.DMA((turns, count)),
         }
 
     def each(self, which):
@@ -673,7 +683,7 @@
 MIXER = dict(in_proj="w_in", cond_in="w_ci", cond_out="w_co", out_proj="w_out", filter_spec="w_spec")
 FFN = dict(gate_proj="w_gate", up_proj="w_up", down_proj="w_down")
 CUTS = dict(in_proj=1, cond_in=1, cond_out=1, filter_spec=1, out_proj=0, gate_proj=0, up_proj=0, down_proj=0)
-PROJ, QUERY, MIXED, GATED, SPECTRA, MIX_ROWS = 0, 3, 4, 5, 6, 12
+PROJ, QUERY, MIXED, SPECTRA, MIX_ROWS = 0, 3, 4, 5, 11
 
 
 def forward_body(r):
@@ -698,6 +708,7 @@
         ]
         return Weights(place, sems, pairs)
 
+    rest = (1, 2, 3, 4)
     mixer_weights = [weights("mw", MIXER, l) for l in range(layers)]
     ffn_weights = [weights("fw", FFN, l) for l in range(layers)]
     place.barrier()
@@ -718,7 +729,7 @@
         seg_copy.start()
         taps_copy.start()
 
-    mixer_weights[0].start()
+    mixer_weights[0].start((0,))
     for copy in tables:
         copy.start()
     r.edges[0:PAD] = jnp.full((PAD, 1), -1, jnp.int32)
@@ -743,8 +754,8 @@
         r.taps_out[...] = r.taps_got[...]
 
     here = r.edges[PAD : PAD + length]
-    r.mask_prev[...] = jnp.where(r.edges[PAD - 1 : PAD - 1 + length] == here, 1.0, 0.0)
-    r.mask_next[...] = jnp.where(r.edges[PAD + 1 : PAD + 1 + length] == here, 1.0, 0.0)
+    r.masks[:, 0:1] = jnp.where(r.edges[PAD - 1 : PAD - 1 + length] == here, 1.0, 0.0)
+    r.masks[:, 1:2] = jnp.where(r.edges[PAD + 1 : PAD + 1 + length] == here, 1.0, 0.0)
     for j in range(1, 4):
         gain_copy(j).wait()
     r.gain_parts[0] = r.small[...]
@@ -753,6 +764,7 @@
         parts.append(r.gain_parts[lax.rem(place.chan - c + 4, 4)])
     r.gains[...] = jnp.concatenate(parts, 1)
     exchange.finish()
+    mixer_weights[0].start(rest)
     r.values[0] = jnp.concatenate([r.pieces[j] for j in range(4)], 1).astype(F32)
 
     def tap(l, o, s):
@@ -777,10 +789,8 @@
         h_all[group.at(0)] = (xhat * r.gains[l : l + 1]).astype(BF)
         group.gather_start(h_all)
         if l == 0:
-            mixer_weights[0].forward()
-            ffn_weights[0].start()
-        mixer_weights[l].ready()
-        mlp_tables(r, l)
+            mixer_weights[0].forward((0,))
+        mixer_weights[l].ready((0,))
         saved("mixer")
 
         def project(which, chunk=None):
@@ -800,10 +810,13 @@
             group.gather_diagonal(h_all, chunk)
             project(3, chunk)
 
+        if l == 0:
+            mixer_weights[0].forward(rest)
+            ffn_weights[0].start()
         for t in range(tiles):
             at = pl.ds(t * size, size)
-            prev = r.mask_prev[at]
-            following = r.mask_next[at]
+            prev = r.masks[at, 0:1]
+            following = r.masks[at, 1:2]
             shorts = []
             for s in range(3):
                 shorts.append(
@@ -814,6 +827,8 @@
             r.mix[QUERY, at] = shorts[0].astype(BF)
             r.both[at, 0:lanes] = shorts[1].astype(BF)
             r.both[at, wide : wide + lanes] = shorts[2].astype(BF)
+        mixer_weights[l].ready(rest)
+        mlp_tables(r, l)
         if l == 0:
             for copy in tables:
                 copy.wait()
@@ -844,7 +859,6 @@
             mixed = nn_dot(r.cos[at], r.prod_re[...]) + nn_dot(r.sin[at], r.prod_im[...])
             r.mix[MIXED, at] = mixed.astype(BF)
             gated = (r.mix[QUERY, at].astype(F32) * mixed).astype(BF)
-            r.mix[GATED, at] = gated
             return nn_dot(gated, r.w_out[l])
 
         group.reduce_whole("diagonal", project_out(3))
@@ -877,10 +891,7 @@
         r.values[l + 1] = r.mids[l] + block(group.at(0))
         group.gather_peer(h_all)
         group.reduce_whole("peer", block(group.at(2)))
-        if l + 1 < layers:
-            mixer_weights[l + 1].forward()
-            ffn_weights[l + 1].start()
-        else:
+        if l + 1 == layers:
             cotangent.start()
         for chunk in range(CHUNKS):
             group.gather_near(h_all, chunk)
@@ -888,6 +899,9 @@
             group.gather_diagonal(h_all, chunk)
             group.reduce_peer(1, chunk, block(group.at(3, chunk)))
             group.reduce_near(chunk, r.near_part[group.piece(chunk)])
+        if l + 1 < layers:
+            mixer_weights[l + 1].forward()
+            ffn_weights[l + 1].start()
         save("ffn", (3, r.units, r.s_units.at[l]), (4, h_all, r.s_h_ffn.at[l]))
         for chunk in range(CHUNKS):
             r.values[l + 1, group.piece(chunk)] += group.reduce_end(chunk)
@@ -958,8 +972,7 @@
             carried=((rows, width), F32),
             gains=((gains, width), F32),
             taps_out=(taps.shape, F32),
-            mask_prev=((length, 1), F32),
-            mask_next=((length, 1), F32),
+            masks=((length, 2), F32),
             **saves,
             **kept,
         ),
@@ -1001,363 +1014,351 @@
     )
 
 
-def ffn_backward_body(l, last, r):
+GRADS = ("proj", "spec", "mlp", "small")
+SMALL_ROWS = 32
+
+
+def of(r, prefix):
+    return [getattr(r, prefix + n) for n in GRADS]
+
+
+def backward_body(r):
     place = Place()
-    rows, width = r.mids.shape[1:]
+    layers, rows, width = r.mids.shape
+    length = r.m_all.shape[0]
+    lanes = r.w_in.shape[3]
+    groups, feats, inner = r.w_ci.shape[1:]
     units = r.units.shape[2]
-    group = Group(place, r, rows)
-    load = Load(
+    half = feats // 2
+    wide = 256 * (-(-lanes // 256))
+    tiles = 4
+    size = length // tiles
+    w_gate, w_up, w_down = [r.w_ffn.at[pl.ds(i * width, width)] for i in range(3)]
+    hidden_all, gate_grads, up_grads = [r.work.at[i] for i in range(3)]
+    both_re, both_im = [r.work.at[i, :, pl.ds(0, 2 * wide)] for i in range(2)]
+    q_g = r.work.at[2, :, pl.ds(0, wide)]
+    proj_grads = [r.work.at[i, :, pl.ds(2 * wide, wide)] for i in range(3)]
+
+    hidden = groups * inner
+    sum_in, sum_out = [
+        [held.at[pl.ds(0, lanes), pl.ds(i * hidden, hidden)] for i in range(2)]
+        for held in (r.near_part, r.own_part)
+    ]
+
+    def load_ffn(l):
+        load = Load(
+            r,
+            [
+                (r.w_gate_out.at[l], w_gate),
+                (r.w_up_out.at[l], w_up),
+                (r.w_down_out.at[l], w_down),
+                (r.s_units.at[l], r.units),
+            ],
+        )
+        load.start()
+        return load
+
+    def load_mixer(l):
+        load = Load(
+            r,
+            [
+                (r.w_out_out.at[l], r.w_out.at[0]),
+                (r.w_ci_out.at[l], r.w_ci.at[0]),
+                (r.w_co_out.at[l], r.w_co.at[0]),
+                (r.s_mix.at[l], r.mix),
+                (r.s_pre.at[l], r.pre_all),
+                (r.w_in_out.at[l], r.w_in.at[0]),
+            ],
+            6,
+        )
+        load.start()
+        return load
+
+    def load_rows(rows_of, h_of):
+        load = Load(r, [(rows_of, r.row_in), (h_of, r.h_all)], 12)
+        load.start()
+        return load
+
+    first = Load(
         r,
         [
-            (r.w_gate_out.at[l], r.w_gate),
-            (r.w_up_out.at[l], r.w_up),
-            (r.w_down_out.at[l], r.w_down),
-            (r.s_units.at[l], r.units),
-            (r.s_h_ffn.at[l], r.h_all),
-        ],
-    )
-    load.start()
-    layers = r.gains.shape[0] // 2
-    gain = r.gains[layers + l : layers + l + 1]
-    r.g_all[group.at(0)] = r.carried[...].astype(BF)
-    if last:
-        shard = r.returned.shape[1]
-        for j in range(4):
-            r.leaving[j] = r.values[l + 1, :, j * shard : (j + 1) * shard].astype(BF)
-        back = Return(place, r, r.leaving, r.returned)
-    place.barrier()
-    group.gather_start(r.g_all)
-    if last:
-        back.start()
-    else:
-        spread = Spread(place, r, [r.ffn_total], [r.ffn_result])
-        scatter = Scatter(place, r, of(r, "g_"), of(r, "t_"))
-        scatter.start()
-        spread.start()
-
-    load.finish()
-
-    def block(at):
-        hidden_grad = nt_dot(r.g_all[at], r.w_down[...])
-        gate = r.units[0, at].astype(F32)
-        up = r.units[1, at].astype(F32)
-        cdf = normal_cdf(gate)
-        act = gate * cdf
-        r.hidden_all[at] = (act * up).astype(BF)
-        gate_grad = (hidden_grad * up * (cdf + gate * normal_pdf(gate))).astype(BF)
-        up_grad = (hidden_grad * act).astype(BF)
-        r.gate_grads[at] = gate_grad
-        r.up_grads[at] = up_grad
-        return nt_dot(gate_grad, r.w_gate[...]) + nt_dot(up_grad, r.w_up[...])
-
-    r.own_part[...] = block(group.at(0))
-    group.gather_peer(r.g_all)
-    group.reduce_whole("peer", block(group.at(2)))
-    if not last:
-        scatter.second()
-    for chunk in range(CHUNKS):
-        group.gather_near(r.g_all, chunk)
-        r.near_part[group.piece(chunk)] = block(group.at(1, chunk))
-        group.gather_diagonal(r.g_all, chunk)
-        group.reduce_peer(1, chunk, block(group.at(3, chunk)))
-        group.reduce_near(chunk, r.near_part[group.piece(chunk)])
-    if not last:
-        scatter.middle()
-        spread.forward()
-    step = 256
-    for u in range(units // step):
-        cols = pl.ds(u * step, step)
-        r.weight_grads[0 * width : 1 * width, cols] = tn_dot(r.h_all[...], r.gate_grads[:, cols]).astype(BF)
-        r.weight_grads[1 * width : 2 * width, cols] = tn_dot(r.h_all[...], r.up_grads[:, cols]).astype(BF)
-        r.weight_grads[pl.ds(2 * width + u * step, step)] = tn_dot(r.hidden_all[:, cols], r.g_all[...]).astype(BF)
-    for chunk in range(CHUNKS):
-        r.own_part[group.piece(chunk)] += group.reduce_end(chunk)
-    grad, gain_part = norm_grad_rows(r.own_part[...], r.mids[l], gain)
-    r.mid_grad[...] = r.carried[...] + grad
-    r.gain_grad[...] = gain_part
-    group.finish()
-    if last:
-        back.finish()
-        r.output[...] = r.returned[...].astype(F32)
-    else:
-        spread.finish()
-        scatter.finish()
-
-
-GRADS = ("proj", "spec", "mlp", "small")
-
-
-def of(r, prefix):
-    return [getattr(r, prefix + n) for n in GRADS]
-
-
-def totals_of(grads):
-    return {"t_" + n: ((grads[n].shape[0] // 8, grads[n].shape[1]), BF) for n in GRADS}
-
-
-def ffn_backward(l, fwd, carried, last, shard, pending):
-    layers, rows, width = fwd.mids.shape
-    units = fwd.w_gate_out.shape[2]
-    full = rows * 4
-    big = pltpu.VMEM((full, units), BF)
-    held = ("w_gate_out", "w_up_out", "w_down_out", "s_units", "s_h_ffn")
-    ins = dict(carried=carried, mids=fwd.mids, gains=fwd.gains)
-    ins.update({n: getattr(fwd, n) for n in held})
-    outs = dict(
-        mid_grad=((rows, width), F32),
-        weight_grads=((3 * width, units), BF),
-        gain_grad=((1, width), F32),
-    )
-    hbm = held
-    if last:
-        ins.update(values=fwd.values)
-        outs.update(output=((full, shard), F32))
-        scratch = dict(
-            leaving=pltpu.VMEM((4, rows, shard), BF),
-            returned=pltpu.VMEM((full, shard), BF),
-            **Return.scratch(),
-        )
-    else:
-        grads, ffn_total = pending
-        ins.update(ffn_total=ffn_total, **{"g_" + n: grads[n] for n in GRADS})
-        outs.update(
-            ffn_result=((8 * ffn_total.shape[0], ffn_total.shape[1]), BF),
-            **totals_of(grads),
-        )
-        scratch = dict(**Spread.scratch(1), **Scatter.scratch([grads[n].shape for n in GRADS]))
-        hbm += tuple("g_" + n for n in GRADS)
-    return call_kernel(
-        functools.partial(ffn_backward_body, l, last),
-        ins,
-        outs,
-        dict(
-            near_part=pltpu.VMEM((rows, width), F32),
-            own_part=pltpu.VMEM((rows, width), F32),
-            g_all=pltpu.VMEM((full, width), BF),
-            h_all=pltpu.VMEM((full, width), BF),
-            units=pltpu.VMEM((2, full, units), BF),
-            w_gate=pltpu.VMEM((width, units), BF),
-            w_up=pltpu.VMEM((width, units), BF),
-            w_down=pltpu.VMEM((units, width), BF),
-            load_sem=pltpu.SemaphoreType.DMA((5,)),
-            hidden_all=big,
-            gate_grads=big,
-            up_grads=big,
-            **Group.scratch(rows, width),
-            **scratch,
-        ),
-        20 + l,
-        12 * full * width * units,
-        hbm,
-    )
-
-
-def mixer_backward_body(l, above, r):
-    bottom = l == 0
-    place = Place()
-    rows = r.mid_grad.shape[0]
-    length, width = r.h_all.shape
-    lanes = r.w_in.shape[3]
-    groups, feats, units = r.w_ci.shape[1:]
-    half = feats // 2
-    wide = r.both_re.shape[1] // 2
-    tiles = 4
-    size = length // tiles
-    group = Group(place, r, rows)
-    load = Load(
-        r,
-        [
-            (r.w_out_out.at[l], r.w_out.at[0]),
-            (r.w_ci_out.at[l], r.w_ci.at[0]),
-            (r.w_co_out.at[l], r.w_co.at[0]),
-            (r.s_mix.at[l], r.mix),
-            (r.s_pre.at[l], r.pre_all),
-            (r.w_in_out.at[l], r.w_in.at[0]),
-            (r.s_h_mixer.at[l], r.h_all),
+            (r.values.at[layers], r.near_part),
+            (r.carried, r.grad),
             (r.cosine, r.cos),
             (r.sine, r.sin),
-            (r.values.at[l], r.layer_in),
         ],
+        14,
     )
-    load.start()
-    r.m_all[group.at(0)] = r.mid_grad[...].astype(BF)
-    place.barrier()
-    group.gather_start(r.m_all)
-    ffn_scatter = Scatter(place, r, [r.ffn_grads], [r.ffn_total], "fs")
-    ffn_scatter.start()
-    if above:
-        spread = Spread(place, r, of(r, "t_"), of(r, "r_"))
-        spread.start()
-    if bottom:
-        scatter = Scatter(place, r, of(r, "g_"), of(r, "u_"))
-        ffn_spread = Spread(place, r, [r.ffn_total], [r.ffn_result], "fp")
-        mix_spread = Spread(place, r, of(r, "u_"), of(r, "q_"), "mp")
+    first.start()
+    pending = {"ffn": load_ffn(layers - 1), "mixer": load_mixer(layers - 1)}
+
+    ffn_scatter = [Scatter(place, r, [r.weight_grads], [r.ffn_total], "fs", l) for l in range(layers)]
+    mix_scatter = [Scatter(place, r, of(r, "g_"), of(r, "u_"), "ms", l) for l in range(layers)]
+    freed = [
+        r.weight_grads.at[pl.ds(0, 4 * lanes)],
+        r.units.at[0, :, pl.ds(0, 2 * lanes)],
+        r.units.at[1, pl.ds(0, 2 * groups * feats), pl.ds(0, inner)],
+        r.units.at[1, pl.ds(0, 256), pl.ds(inner, 128)],
+    ]
+    ffn_spread, mix_spread = [], []
+    for l in range(layers):
+        ffn_to = r.r_ffn.at[l] if l else r.w_ffn
+        mix_to = [o.at[l] for o in of(r, "r_")] if l else freed
+        ffn_spread.append(Spread(place, r, [r.ffn_total], [ffn_to], "fp", l))
+        mix_spread.append(Spread(place, r, of(r, "u_"), mix_to, "mp", l))
+
+    shard = r.leaving.shape[2]
+    output = Return(place, r, r.leaving, r.output, 0)
+    stream_grad = Return(place, r, r.leaving, r.stream_grad, 1)
+
+    def leave(x):
+        for j in range(4):
+            r.leaving[j] = x[:, j * shard : (j + 1) * shard].astype(BF)
+
     for s in range(3):
         r.padded[s, 0:PAD] = jnp.zeros((PAD, lanes), F32)
         r.padded[s, PAD + length : 2 * PAD + length] = jnp.zeros((PAD, lanes), F32)
-    r.both_re[...] = jnp.zeros_like(r.both_re)
-    r.both_im[...] = jnp.zeros_like(r.both_im)
-    r.sum_in[...] = jnp.zeros_like(r.sum_in)
-    r.sum_out[...] = jnp.zeros_like(r.sum_out)
-    load.finish()
-    mlp_tables(r, 0)
-
-    def gated_back(which, chunk=None):
-        at = group.at(which, chunk)
-        gated_grad = nt_dot(r.m_all[at], r.w_out[0])
-        to = pl.ds(pl.multiple_of(at.start + PAD, 8), at.size)
-        r.padded[0, to] = gated_grad * r.mix[MIXED, at].astype(F32)
-        r.q_g[at] = (gated_grad * r.mix[QUERY, at].astype(F32)).astype(BF)
-
-    gated_back(0)
-    group.gather_peer(r.m_all)
-    gated_back(2)
-    for chunk in range(CHUNKS):
-        group.gather_near(r.m_all, chunk)
-        gated_back(1, chunk)
-        group.gather_diagonal(r.m_all, chunk)
-        gated_back(3, chunk)
-
-    @pl.loop(0, tiles)
-    def _(t):
-        at = aligned(t, size)
-        real = nn_dot(r.cos[at], r.q_g[...])
-        imag = nn_dot(r.sin[at], r.q_g[...])
-        value_re, value_im, kernel_re, kernel_im = [
-            r.mix[SPECTRA + i, at].astype(F32) for i in range(4)
-        ]
-        kernel_re_grad = real * value_re + imag * value_im
-        kernel_im_grad = imag * value_re - real * value_im
-        r.both_re[at, 0:lanes] = (real * kernel_re + imag * kernel_im).astype(BF)
-        r.both_im[at, 0:lanes] = (imag * kernel_re - real * kernel_im).astype(BF)
-        r.g_spec[at] = jnp.concatenate([kernel_re_grad, kernel_im_grad], 1).astype(BF)
-        kernel_re_grad = kernel_re_grad.astype(BF)
-        kernel_im_grad = kernel_im_grad.astype(BF)
-        pre = r.pre_all[at].astype(F32)
-        cdf = normal_cdf(pre)
-        inner = (pre * cdf).astype(BF)
-        inner_grad = nn_dot(kernel_re_grad, r.out_re[...]) + nn_dot(kernel_im_grad, r.out_im[...])
-        pre_grad = (inner_grad * (cdf + pre * normal_pdf(pre))).astype(BF)
-        r.both_re[at, wide : wide + lanes] = nt_dot(pre_grad, r.in_re[...]).astype(BF)
-        r.both_im[at, wide : wide + lanes] = nt_dot(pre_grad, r.in_im[...]).astype(BF)
-        r.sum_out[0] += tn_dot(kernel_re_grad, inner)
-        r.sum_out[1] += tn_dot(kernel_im_grad, inner)
-        r.sum_in[0] += tn_dot(r.mix[SPECTRA + 4, at], pre_grad)
-        r.sum_in[1] += tn_dot(r.mix[SPECTRA + 5, at], pre_grad)
-
-    ffn_scatter.second()
-    if above:
-        spread.forward()
-    for g in range(groups):
-        rows_at, cols = slice(g * half, (g + 1) * half), slice(g * units, (g + 1) * units)
-        at = g * feats
-        r.g_mlp[at : at + half] = r.sum_in[0, rows_at, cols].astype(BF)
-        r.g_mlp[at + half : at + feats] = r.sum_in[1, rows_at, cols].astype(BF)
-        turned = jnp.concatenate([r.sum_out[0, rows_at, cols], r.sum_out[1, rows_at, cols]], 0)
-        at += groups * feats
-        r.g_mlp[at : at + units] = turned.T.astype(BF)
-    if bottom:
-        scatter.start((1, 2))
-
-    @pl.loop(0, tiles)
-    def _(t):
-        at = aligned(t, size)
-        both = nn_dot(r.cos[at], r.both_re[...]) + nn_dot(r.sin[at], r.both_im[...])
-        to = pl.ds(pl.multiple_of(t * size + PAD, 8), size)
-        r.padded[1, to] = both[:, :lanes]
-        r.padded[2, to] = both[:, wide : wide + lanes]
-
-    def tap(o, s):
-        at = 9 * l + 3 * o + s
-        return r.taps[at : at + 1]
-
-    totals = [[None] * 3 for _ in range(3)]
-    for t in range(tiles):
-        at = pl.ds(t * size, size)
-        prev = r.mask_prev[at]
-        following = r.mask_next[at]
+    place.barrier()
+
+    def ffn(l):
+        top = l + 1 == layers
+        group = Group(place, r, rows, 1)
+        load = load_rows(r.mids.at[l], r.s_h_ffn.at[l])
+        gain = r.gains[layers + l : layers + l + 1]
+        if top:
+            first.finish((0, 1))
+        r.g_all[group.at(0)] = r.grad[...].astype(BF)
+        group.gather_start(r.g_all)
+        if top:
+            leave(r.near_part[...])
+            output.start()
+        pending["ffn"].finish()
+        if not top:
+            pending["mixer"] = load_mixer(l)
+
+        def block(at):
+            hidden_grad = nt_dot(r.g_all[at], w_down[...])
+            gate = r.units[0, at].astype(F32)
+            up = r.units[1, at].astype(F32)
+            cdf = normal_cdf(gate)
+            act = gate * cdf
+            hidden_all[at] = (act * up).astype(BF)
+            gate_grad = (hidden_grad * up * (cdf + gate * normal_pdf(gate))).astype(BF)
+            up_grad = (hidden_grad * act).astype(BF)
+            gate_grads[at] = gate_grad
+            up_grads[at] = up_grad
+            return nt_dot(gate_grad, w_gate[...]) + nt_dot(up_grad, w_up[...])
+
+        r.own_part[...] = block(group.at(0))
+        group.gather_peer(r.g_all)
+        group.reduce_whole("peer", block(group.at(2)))
+        if not top:
+            ffn_scatter[l + 1].finish()
+            ffn_spread[l + 1].start()
+        for chunk in range(CHUNKS):
+            group.gather_near(r.g_all, chunk)
+            r.near_part[group.piece(chunk)] = block(group.at(1, chunk))
+            group.gather_diagonal(r.g_all, chunk)
+            group.reduce_peer(1, chunk, block(group.at(3, chunk)))
+            group.reduce_near(chunk, r.near_part[group.piece(chunk)])
+        load.finish()
+        step = 256
+        for u in range(units // step):
+            cols = pl.ds(u * step, step)
+            r.weight_grads[0 * width : 1 * width, cols] = tn_dot(r.h_all[...], gate_grads[:, cols]).astype(BF)
+            r.weight_grads[1 * width : 2 * width, cols] = tn_dot(r.h_all[...], up_grads[:, cols]).astype(BF)
+            r.weight_grads[pl.ds(2 * width + u * step, step)] = tn_dot(hidden_all[:, cols], r.g_all[...]).astype(BF)
+        if not top:
+            mix_scatter[l + 1].second()
+        ffn_scatter[l].start()
+        for chunk in range(CHUNKS):
+            r.own_part[group.piece(chunk)] += group.reduce_end(chunk)
+        grad, gain_part = norm_grad_rows(r.own_part[...], r.row_in[...], gain)
+        r.grad[...] += grad
+        r.gain_two[...] = gain_part
+        group.finish()
+        if not top:
+            mix_scatter[l + 1].middle()
+
+    def mixer(l):
+        top, bottom = l + 1 == layers, l == 0
+        group = Group(place, r, rows, 0)
+        load = load_rows(r.values.at[l], r.s_h_mixer.at[l])
+        r.m_all[group.at(0)] = r.grad[...].astype(BF)
+        group.gather_start(r.m_all)
+        if not bottom:
+            pending["ffn"] = load_ffn(l - 1)
+        for i in range(2):
+            r.work[i, :, 0 : 2 * wide] = jnp.zeros((length, 2 * wide), BF)
+        r.near_part[...] = jnp.zeros_like(r.near_part)
+        r.own_part[...] = jnp.zeros_like(r.own_part)
+        pending["mixer"].finish()
+        mlp_tables(r, 0)
+
+        def gated_back(which, chunk=None):
+            at = group.at(which, chunk)
+            gated_grad = nt_dot(r.m_all[at], r.w_out[0])
+            to = pl.ds(pl.multiple_of(at.start + PAD, 8), at.size)
+            r.padded[0, to] = gated_grad * r.mix[MIXED, at].astype(F32)
+            q_g[at, 0:lanes] = (gated_grad * r.mix[QUERY, at].astype(F32)).astype(BF)
+
+        gated_back(0)
+        group.gather_peer(r.m_all)
+        gated_back(2)
+        for chunk in range(CHUNKS):
+            group.gather_near(r.m_all, chunk)
+            gated_back(1, chunk)
+            group.gather_diagonal(r.m_all, chunk)
+            gated_back(3, chunk)
+        if top:
+            first.finish((2, 3))
+        else:
+            mix_scatter[l + 1].finish()
+            mix_spread[l + 1].start()
+            ffn_spread[l + 1].forward()
+
+        @pl.loop(0, tiles)
+        def _(t):
+            at = aligned(t, size)
+            real = nn_dot(r.cos[at], q_g[:, 0:lanes])
+            imag = nn_dot(r.sin[at], q_g[:, 0:lanes])
+            value_re, value_im, kernel_re, kernel_im = [
+                r.mix[SPECTRA + i, at].astype(F32) for i in range(4)
+            ]
+            kernel_re_grad = real * value_re + imag * value_im
+            kernel_im_grad = imag * value_re - real * value_im
+            both_re[at, 0:lanes] = (real * kernel_re + imag * kernel_im).astype(BF)
+            both_im[at, 0:lanes] = (imag * kernel_re - real * kernel_im).astype(BF)
+            r.g_spec[at] = jnp.concatenate([kernel_re_grad, kernel_im_grad], 1).astype(BF)
+            kernel_re_grad = kernel_re_grad.astype(BF)
+            kernel_im_grad = kernel_im_grad.astype(BF)
+            pre = r.pre_all[at].astype(F32)
+            cdf = normal_cdf(pre)
+            act = (pre * cdf).astype(BF)
+            inner_grad = nn_dot(kernel_re_grad, r.out_re[...]) + nn_dot(kernel_im_grad, r.out_im[...])
+            pre_grad = (inner_grad * (cdf + pre * normal_pdf(pre))).astype(BF)
+            both_re[at, wide : wide + lanes] = nt_dot(pre_grad, r.in_re[...]).astype(BF)
+            both_im[at, wide : wide + lanes] = nt_dot(pre_grad, r.in_im[...]).astype(BF)
+            sum_out[0][...] += tn_dot(kernel_re_grad, act)
+            sum_out[1][...] += tn_dot(kernel_im_grad, act)
+            sum_in[0][...] += tn_dot(r.mix[SPECTRA + 4, at], pre_grad)
+            sum_in[1][...] += tn_dot(r.mix[SPECTRA + 5, at], pre_grad)
+
+        for g in range(groups):
+            rows_at, cols = slice(g * half, (g + 1) * half), slice(g * inner, (g + 1) * inner)
+            at = g * feats
+            r.g_mlp[at : at + half] = sum_in[0][rows_at, cols].astype(BF)
+            r.g_mlp[at + half : at + feats] = sum_in[1][rows_at, cols].astype(BF)
+            turned = jnp.concatenate([sum_out[0][rows_at, cols], sum_out[1][rows_at, cols]], 0)
+            at += groups * feats
+            r.g_mlp[at : at + inner] = turned.T.astype(BF)
+        ffn_scatter[l].second()
+        mix_scatter[l].start((1, 2))
+
+        @pl.loop(0, tiles)
+        def _(t):
+            at = aligned(t, size)
+            both = nn_dot(r.cos[at], both_re[...]) + nn_dot(r.sin[at], both_im[...])
+            to = pl.ds(pl.multiple_of(t * size + PAD, 8), size)
+            r.padded[1, to] = both[:, :lanes]
+            r.padded[2, to] = both[:, wide : wide + lanes]
+
+        def tap(o, s):
+            at = 9 * l + 3 * o + s
+            return r.taps_out[at : at + 1]
+
+        totals = [[None] * 3 for _ in range(3)]
+        for t in range(tiles):
+            at = pl.ds(t * size, size)
+            prev = r.masks[at, 0:1]
+            following = r.masks[at, 1:2]
+            for s in range(3):
+                here = shifted(r.padded, s, t, size, 0)
+                after = shifted(r.padded, s, t, size, 1) * following
+                before = shifted(r.padded, s, t, size, -1) * prev
+                proj_grads[s][at, 0:lanes] = (
+                    tap(0, s) * after + tap(1, s) * here + tap(2, s) * before
+                ).astype(BF)
+                proj = r.mix[PROJ + s, at].astype(F32)
+                for o, g in enumerate((after, here, before)):
+                    part = jnp.sum(g * proj, 0, keepdims=True)
+                    totals[o][s] = part if t == 0 else totals[o][s] + part
+
+        def feats_grad(which):
+            at = group.at(which)
+            return sum(nt_dot(proj_grads[s][at, 0:lanes], r.w_in[0, s]) for s in range(3))
+
+        group.reduce_whole("diagonal", feats_grad(3))
+        group.reduce_whole("near", feats_grad(1))
+        group.reduce_whole("peer", feats_grad(2))
+        load.finish()
         for s in range(3):
-            here = shifted(r.padded, s, t, size, 0)
-            after = shifted(r.padded, s, t, size, 1) * following
-            before = shifted(r.padded, s, t, size, -1) * prev
-            r.proj_grads[s, at] = (
-                tap(0, s) * after + tap(1, s) * here + tap(2, s) * before
-            ).astype(BF)
-            proj = r.mix[PROJ + s, at].astype(F32)
-            for o, g in enumerate((after, here, before)):
-                part = jnp.sum(g * proj, 0, keepdims=True)
-                totals[o][s] = part if t == 0 else totals[o][s] + part
-    ffn_scatter.middle()
-
-    def feats_grad(which):
-        at = group.at(which)
-        return sum(nt_dot(r.proj_grads[s, at], r.w_in[0, s]) for s in range(3))
-
-    group.reduce_whole("diagonal", feats_grad(3))
-    group.reduce_whole("near", feats_grad(1))
-    group.reduce_whole("peer", feats_grad(2))
-    for s in range(3):
-        r.g_proj[s * lanes : (s + 1) * lanes] = tn_dot(r.proj_grads[s], r.h_all[...]).astype(BF)
-    r.g_proj[3 * lanes :] = tn_dot(r.mix[GATED], r.m_all[...]).astype(BF)
-    if bottom:
-        scatter.start((0,))
-        scatter.second((1, 2))
-    r.own_part[...] = feats_grad(0)
-    for chunk in range(CHUNKS):
-        r.own_part[group.piece(chunk)] += group.reduce_end(chunk)
-    grad, gain_part = norm_grad_rows(r.own_part[...], r.layer_in[...], r.gains[l : l + 1])
-    carried = r.mid_grad[...] + grad
-    if bottom:
-        shard = r.returned.shape[1]
-        for j in range(4):
-            r.leaving[j] = carried[:, j * shard : (j + 1) * shard].astype(BF)
-        back = Return(place, r, r.leaving, r.returned)
-        back.start()
-    else:
-        r.carried[...] = carried
-    r.small_rows[...] = jnp.zeros_like(r.small_rows)
-    small = [totals[o][s] for o in range(3) for s in range(3)] + [gain_part, r.gain_two[...]]
-    at = 0
-    for x in small:
-        for start in range(0, x.shape[1], 128):
-            part = x[:, start : start + 128]
-            r.small_rows[at : at + 1, 0 : part.shape[1]] = part
-            at += 1
-    r.g_small[...] = jnp.zeros_like(r.g_small)
-    r.g_small[0 : r.small_rows.shape[0]] = r.small_rows[...].astype(BF)
-    if bottom:
-        scatter.start((3,))
-    ffn_scatter.finish()
-    if bottom:
-        ffn_spread.start()
-        scatter.middle((1, 2))
-        scatter.second((0, 3))
-        scatter.finish((1, 2))
-        mix_spread.start((1, 2))
-        scatter.middle((0, 3))
-        ffn_spread.forward()
-        scatter.finish((0, 3))
-        mix_spread.start((0, 3))
-        mix_spread.forward((1, 2))
-        back.finish()
-        r.stream_grad[...] = r.returned[...].astype(F32)
-        mix_spread.forward((0, 3))
-        mix_spread.finish((3,))
-        if above:
-            spread.finish()
-        gain_sums(place, r, above)
-        mix_spread.finish((0, 1, 2))
-        ffn_spread.finish()
-    elif above:
-        spread.finish()
-    group.finish()
-
-
-def gain_sums(place, r, above):
-    count = r.small_rows.shape[0]
-    r.gain_parts[0, 0] = r.q_small[0:count]
-    if above:
-        r.gain_parts[0, 1] = r.r_small[0:count]
+            r.g_proj[s * lanes : (s + 1) * lanes] = tn_dot(proj_grads[s][:, 0:lanes], r.h_all[...]).astype(BF)
+        q_g[:, 0:lanes] = (r.mix[QUERY].astype(F32) * r.mix[MIXED].astype(F32)).astype(BF)
+        r.g_proj[3 * lanes :] = tn_dot(q_g[:, 0:lanes], r.m_all[...]).astype(BF)
+        mix_scatter[l].start((0,))
+        ffn_scatter[l].middle()
+        if bottom:
+            mix_scatter[l].second((1, 2))
+        if not top:
+            mix_spread[l + 1].forward()
+        r.own_part[...] = feats_grad(0)
+        for chunk in range(CHUNKS):
+            r.own_part[group.piece(chunk)] += group.reduce_end(chunk)
+        grad, gain_part = norm_grad_rows(r.own_part[...], r.row_in[...], r.gains[l : l + 1])
+        if bottom:
+            output.finish()
+            leave(r.grad[...] + grad)
+            stream_grad.start()
+        else:
+            r.grad[...] += grad
+        r.small_rows[...] = jnp.zeros_like(r.small_rows)
+        small = [totals[o][s] for o in range(3) for s in range(3)] + [gain_part, r.gain_two[...]]
+        at = 0
+        for x in small:
+            for start in range(0, x.shape[1], 128):
+                part = x[:, start : start + 128]
+                r.small_rows[at : at + 1, 0 : part.shape[1]] = part
+                at += 1
+        r.g_small[...] = jnp.zeros_like(r.g_small)
+        r.g_small[0:SMALL_ROWS] = r.small_rows[...].astype(BF)
+        mix_scatter[l].start((3,))
+        group.finish()
+        if not top:
+            ffn_spread[l + 1].finish()
+            mix_spread[l + 1].finish()
+
+    for l in reversed(range(layers)):
+        ffn(l)
+        mixer(l)
+    above = [
+        pltpu.make_async_copy(
+            r.r_small.at[l, pl.ds(0, SMALL_ROWS)], r.gain_parts.at[0, l], r.end_sem.at[l]
+        )
+        for l in range(1, layers)
+    ]
+    for copy in above:
+        copy.start()
+    ffn_scatter[0].finish()
+    ffn_spread[0].start()
+    mix_scatter[0].middle((1, 2))
+    mix_scatter[0].second((0, 3))
+    mix_scatter[0].finish((1, 2))
+    mix_spread[0].start((1, 2))
+    mix_scatter[0].middle((0, 3))
+    ffn_spread[0].forward()
+    mix_scatter[0].finish((0, 3))
+    mix_spread[0].start((0, 3))
+    mix_spread[0].forward((1, 2))
+    stream_grad.finish()
+    ffn_spread[0].finish()
+    ends = [pltpu.make_async_copy(r.w_ffn, r.r_ffn.at[0], r.end_sem.at[0])]
+    ends[0].start()
+    mix_spread[0].forward((3, 0))
+    mix_spread[0].finish((3,))
+    r.gain_parts[0, 0] = freed[3][0:SMALL_ROWS, :]
+    for copy in above:
+        copy.wait()
 
     def gain_copy(j):
         chan = lax.rem(place.chan + j, 4)
@@ -1367,103 +1368,98 @@
 
     for j in range(1, 4):
         gain_copy(j).start()
+    mix_spread[0].finish((1, 2, 0))
+    for a, n in enumerate(GRADS):
+        ends.append(
+            pltpu.make_async_copy(
+                freed[a], getattr(r, "r_" + n).at[0], r.end_sem.at[layers + a]
+            )
+        )
+        ends[-1].start()
     for j in range(1, 4):
         gain_copy(j).wait()
     total = r.gain_parts[0].astype(F32)
     for j in range(1, 4):
         total += r.gain_parts[j].astype(F32)
     r.gain_grads[...] = total
-
-
-def mixer_backward(l, fwd, mid_grad, tables, gain_two, ffn_grads, pending):
-    rows, width = mid_grad.shape
-    layers, _, length, lanes = fwd.s_mix.shape
-    groups, feats, units = fwd.w_ci_out.shape[1:]
-    inner = groups * units
-    wide = -(-lanes // 128) * 128
-    above = pending is not None
-    held = ("w_out_out", "w_ci_out", "w_co_out", "s_mix", "s_pre", "w_in_out", "s_h_mixer")
-    ins = dict(
-        mid_grad=mid_grad, values=fwd.values, gains=fwd.gains, taps=fwd.taps_out,
-        mask_prev=fwd.mask_prev, mask_next=fwd.mask_next, cosine=tables[0], sine=tables[1],
-        gain_two=gain_two, ffn_grads=ffn_grads, **{n: getattr(fwd, n) for n in held},
+    for copy in ends:
+        copy.wait()
+
+
+def backward(fwd, tables):
+    layers, rows, width = fwd.mids.shape
+    units = fwd.w_gate_out.shape[2]
+    _, _, length, lanes = fwd.s_mix.shape
+    groups, feats, inner = fwd.w_ci_out.shape[1:]
+    hidden = groups * inner
+    held = (
+        "w_gate_out", "w_up_out", "w_down_out", "s_units", "s_h_ffn", "mids", "values", "carried",
+        "w_out_out", "w_ci_out", "w_co_out", "s_mix", "s_pre", "w_in_out", "s_h_mixer",
     )
+    near = ("gains", "taps_out", "masks")
+    ins = dict(cosine=tables[0], sine=tables[1], **{n: getattr(fwd, n) for n in held + near})
     grads = dict(
-        g_proj=((4 * lanes, width), BF),
-        g_spec=((length, 2 * lanes), BF),
-        g_mlp=((2 * groups * feats, units), BF),
-        g_small=((256, 128), BF),
+        proj=(4 * lanes, width),
+        spec=(length, 2 * lanes),
+        mlp=(2 * groups * feats, inner),
+        small=(256, 128),
     )
-    shapes = [g[0] for g in grads.values()]
-    ffn_total = ((ffn_grads.shape[0] // 8, ffn_grads.shape[1]), BF)
-    outs, scratch = {}, Scatter.scratch([ffn_grads.shape], "fs")
-    hbm = held + ("ffn_grads", "cosine", "sine", "values")
-    if above:
-        ins.update(**{"t_" + n: pending[n] for n in GRADS})
-        outs.update(
-            **{"r_" + n: ((pending[n].shape[0] * 8, pending[n].shape[1]), BF) for n in GRADS}
-        )
-        scratch.update(Spread.scratch(len(GRADS)))
-    count = 32
-    if l == 0:
-        shard = lanes
-        outs.update(
-            stream_grad=((length, shard), F32),
-            gain_grads=((2 if above else 1, count, 128), F32),
-            ffn_result=(ffn_grads.shape, BF),
-            **{"q_" + n: grads["g_" + n] for n in GRADS},
-        )
-        scratch.update(
-            ffn_total=pltpu.VMEM(*ffn_total),
-            leaving=pltpu.VMEM((4, rows, shard), BF),
-            returned=pltpu.VMEM((length, shard), BF),
-            gain_parts=pltpu.VMEM((4, 2 if above else 1, count, 128), BF),
-            gain_send=pltpu.SemaphoreType.DMA((4,)),
-            gain_recv=pltpu.SemaphoreType.DMA((4,)),
-            **{n: pltpu.VMEM(*g) for n, g in grads.items()},
-            **{
-                "u_" + n: pltpu.VMEM((g[0][0] // 8, g[0][1]), BF)
-                for n, g in zip(GRADS, grads.values())
-            },
-            **Return.scratch(),
-            **Scatter.scratch(shapes),
-            **Spread.scratch(1, "fp"),
-            **Spread.scratch(len(GRADS), "mp"),
-        )
-    else:
-        outs.update(carried=((rows, width), F32), ffn_total=ffn_total, **grads)
+    ffn_shape = (3 * width, units)
+    outs = dict(
+        output=((length, lanes), BF),
+        stream_grad=((length, lanes), BF),
+        r_ffn=((layers,) + ffn_shape, BF),
+        **{"r_" + n: ((layers,) + g, BF) for n, g in grads.items()},
+    )
+    hbm = held + ("cosine", "sine") + tuple(outs)
+    outs.update(gain_grads=((layers, SMALL_ROWS, 128), F32))
+    row = pltpu.VMEM((rows, width), F32)
     return call_kernel(
-        functools.partial(mixer_backward_body, l, above),
+        backward_body,
         ins,
         outs,
         dict(
+            grad=row,
+            own_part=row,
+            near_part=row,
+            row_in=row,
+            leaving=pltpu.VMEM((4, rows, lanes), BF),
+            gain_two=pltpu.VMEM((1, width), F32),
+            g_all=pltpu.VMEM((length, width), BF),
             m_all=pltpu.VMEM((length, width), BF),
+            work=pltpu.VMEM((3, length, width), BF),
+            w_ffn=pltpu.VMEM(ffn_shape, BF),
+            weight_grads=pltpu.VMEM(ffn_shape, BF),
+            units=pltpu.VMEM((2, length, units), BF),
+            ffn_total=pltpu.VMEM((ffn_shape[0] // 8, ffn_shape[1]), BF),
             h_all=pltpu.VMEM((length, width), BF),
             mix=pltpu.VMEM((MIX_ROWS, length, lanes), BF),
-            pre_all=pltpu.VMEM((length, inner), BF),
+            pre_all=pltpu.VMEM((length, hidden), BF),
             w_in=pltpu.VMEM((1,) + fwd.w_in_out.shape[1:], BF),
             w_out=pltpu.VMEM((1,) + fwd.w_out_out.shape[1:], BF),
             w_ci=pltpu.VMEM((1,) + fwd.w_ci_out.shape[1:], F32),
             w_co=pltpu.VMEM((1,) + fwd.w_co_out.shape[1:], F32),
             cos=pltpu.VMEM((length, length), BF),
             sin=pltpu.VMEM((length, length), BF),
-            load_sem=pltpu.SemaphoreType.DMA((10,)),
-            layer_in=pltpu.VMEM((rows, width), F32),
             padded=pltpu.VMEM((3, length + 2 * PAD, lanes), F32),
-            q_g=pltpu.VMEM((length, lanes), BF),
-            both_re=pltpu.VMEM((length, 2 * wide), BF),
-            both_im=pltpu.VMEM((length, 2 * wide), BF),
-            proj_grads=pltpu.VMEM((3, length, lanes), BF),
-            own_part=pltpu.VMEM((rows, width), F32),
-            sum_in=pltpu.VMEM((2, lanes, inner), F32),
-            sum_out=pltpu.VMEM((2, lanes, inner), F32),
-            small_rows=pltpu.VMEM((count, 128), F32),
-            **mlp_scratch(lanes, inner),
-            **Group.scratch(rows, width),
-            **scratch,
+            small_rows=pltpu.VMEM((SMALL_ROWS, 128), F32),
+            gain_parts=pltpu.VMEM((4, layers, SMALL_ROWS, 128), BF),
+            gain_send=pltpu.SemaphoreType.DMA((4,)),
+            gain_recv=pltpu.SemaphoreType.DMA((4,)),
+            load_sem=pltpu.SemaphoreType.DMA((18,)),
+            end_sem=pltpu.SemaphoreType.DMA((layers + len(GRADS),)),
+            **{"g_" + n: pltpu.VMEM(g, BF) for n, g in grads.items()},
+            **{"u_" + n: pltpu.VMEM((g[0] // 8, g[1]), BF) for n, g in grads.items()},
+            **mlp_scratch(lanes, hidden),
+            **Group.scratch(rows, width, 2),
+            **Return.scratch(),
+            **Scatter.scratch([ffn_shape], "fs", layers),
+            **Scatter.scratch(list(grads.values()), "ms", layers),
+            **Spread.scratch(1, "fp", layers),
+            **Spread.scratch(len(GRADS), "mp", layers),
         ),
-        40 + l,
-        9 * 10**9,
+        2,
+        40 * 10**9,
         hbm,
     )
 
@@ -1510,43 +1506,15 @@
         short_taps.reshape(-1, shard),
         tables,
     )
-    carried = fwd.carried
-    ffn_results, mixer_results = {}, {}
-    grads, ffn_total, output = None, None, None
-    for l in reversed(range(layers)):
-        last = l + 1 == layers
-        back = ffn_backward(
-            l, fwd, carried, last, shard, None if last else (grads, ffn_total)
-        )
-        if last:
-            output, pending = back.output, None
-        else:
-            ffn_results[l + 1] = back.ffn_result
-            pending = {n: getattr(back, "t_" + n) for n in GRADS}
-        down = mixer_backward(
-            l, fwd, back.mid_grad, tables, back.gain_grad, back.weight_grads, pending
-        )
-        if not last:
-            mixer_results[l + 1] = {n: getattr(down, "r_" + n) for n in GRADS}
-        if l > 0:
-            carried, ffn_total = down.carried, down.ffn_total
-            grads = {n: getattr(down, "g_" + n) for n in GRADS}
-    ffn_results[0] = down.ffn_result
-    mixer_results[0] = {n: getattr(down, "q_" + n) for n in GRADS}
+    back = backward(fwd, tables)
 
     def everywhere(x):
         return lax.psum(x, "outer") if lax.axis_size("outer") > 1 else x
 
-    def stacked(get):
-        return everywhere(jnp.stack([get(l) for l in range(layers)])).astype(F32)
-
-    def mixer_stack(name, get):
-        return stacked(lambda l: get(mixer_results[l][name]))
-
-    def ffn_stack(index):
-        return stacked(lambda l: ffn_results[l][index * width : (index + 1) * width])
-
-    gain_grads = everywhere(down.gain_grads)
+    def summed(name):
+        return everywhere(getattr(back, name))
+
+    gain_grads = summed("gain_grads")
     steps = -(-shard // 128)
     taps_rows, gain_rows = 9 * steps, width // 128
 
@@ -1554,25 +1522,28 @@
         whole = gain_grads[:, at : at + gain_rows].reshape(layers, width)
         return lax.dynamic_slice_in_dim(whole, chan * shard, shard, 1)
 
+    proj, spec, mlp = summed("r_proj"), summed("r_spec"), summed("r_mlp")
+    small, ffn = summed("r_small"), summed("r_ffn")
     mlp_rows = groups * feats
-    return (
-        output,
-        down.stream_grad,
+    g_in = proj[:, : 3 * shard].reshape(layers, 3, shard, width).transpose(0, 3, 1, 2)
+    g_taps = small[:, :taps_rows].reshape(layers, 9, steps * 128)[:, :, :shard]
+    g_spec = jnp.stack([spec[:, :, :shard], spec[:, :, shard:]], 1)
+    results = (
+        back.output,
+        back.stream_grad,
         gain_stack(taps_rows),
-        mixer_stack("proj", lambda x: x[: 3 * shard].reshape(3, shard, width).transpose(2, 0, 1)),
-        mixer_stack(
-            "small",
-            lambda x: x[:taps_rows].reshape(9, steps * 128)[:, :shard].reshape(short_taps.shape[1:]),
-        ),
-        mixer_stack("mlp", lambda x: x[:mlp_rows].reshape(cond_in.shape[1:])),
-        mixer_stack("mlp", lambda x: x[mlp_rows:].reshape(cond_out.shape[1:])),
-        mixer_stack("spec", lambda x: jnp.stack([x[:, :shard], x[:, shard:]])),
-        mixer_stack("proj", lambda x: x[3 * shard :]),
+        g_in,
+        g_taps.reshape(short_taps.shape),
+        mlp[:, :mlp_rows].reshape(cond_in.shape),
+        mlp[:, mlp_rows:].reshape(cond_out.shape),
+        g_spec,
+        proj[:, 3 * shard :],
         gain_stack(taps_rows + gain_rows),
-        ffn_stack(0),
-        ffn_stack(1),
-        ffn_stack(2),
+        ffn[:, :width],
+        ffn[:, width : 2 * width],
+        ffn[:, 2 * width :],
     )
+    return tuple(x.astype(F32) for x in results)
 
 
 def solution(mesh):

time: 524 us -> 455 us (0.87)
  Pallas kernels: 469 us -> 408 us
  local copies, waits for them, and re-layouts: 32.5 us -> 24.4 us
    pallas_call x5 -> x2, Pallas kernels: 469 us -> 408 us  [call_kernel(): pl.pallas_call(run, out_shape=[jax.ShapeDtypeStruct(*o) for o in outs.val...]
    unnamed x34 -> x31, local copies, waits for them, and re-layouts: 24.9 us -> 16.9 us
    convert_element_type x8 -> x7, other arithmetic: 14.1 us -> 16.1 us  [on_device(): return tuple((x.astype(F32) for x in results))]
where the time goes in v3:
time: 455 us; the launch traced here: 450 us
  Pallas kernels  408 us (90%)
  local copies, waits for them, and re-layouts  24.4 us (5%)
  other arithmetic  16.7 us (4%)
    pallas_call x2, Pallas kernels, call_kernel(): pl.pallas_call(run, out_shape=[jax.ShapeDtypeStruct(*o) for o in outs.val...  408 us
    unnamed x31, local copies, waits for them, and re-layouts  16.9 us
    convert_element_type x7, other arithmetic, on_device(): return tuple((x.astype(F32) for x in results))  16.1 us

profile of v3, /device:TPU:0, one launch (start us, length us, event | category | flops | bytes accessed | tf_op | source)
XLA Modules:
  0.0 449.8 jit_solution(15989679797567596027)
XLA Ops:
  0.7 5.1 %copy.53.refs_10_ = f32[2,2,1024,192]{3,2,1,0:T(8,128)} copy(f32[2,2,1024,192]{2,3,1,0:T(8,128)} %param.24) | data formatting | bytes 6291456 | tf_op args[8]
  5.8 2.4 copy.49
  8.2 1.0 copy.50.refs_0_
  9.2 1.0 copy.51.refs_1_
  10.2 1.0 copy.52.refs_2_
  11.2 0.6 reshape.50.refs_4_
  11.9 0.6 pad_maximum_fusion.refs_3_
  12.5 185.2 %shard_map.255 = (f32[3,256,768]{2,1,0:T(8,128)}, f32[2,256,768]{2,1,0:T(8,128)}, f32[256,768]{1,0:T(8,128)}, f32[4,768]{1,0:T(4,128)}, f32[18,192]{1,0:T(8,128)...) custom-call(bf16[1024,192]{1,0:T(8,128)(2,1)} %copy.50.refs_0_, ...), custom_call_target="tpu_custom_call" | custom-call | flops 30000001024 | bytes 20971520 | tf_op jit(solution)/shard_map/pallas_call | solution.py:626
  197.6 222.6 %shard_map.256 = (bf16[1024,192]{1,0:T(8,128)(2,1)}, bf16[1024,192]{1,0:T(8,128)(2,1)}, bf16[2,2304,768]{2,1,0:T(8,128)(2,1)}, bf16[2,768,768]{2,1,0:T(8,128)(2,...) custom-call(bf16[1024,1024]{1,0:T(8,128)(2,1)} %constant.14.clone.re, ...), custom_call_target="tpu_custom_call" | custom-call | flops 40000000000 | bytes 20971520 | tf_op jit(solution)/shard_map/pallas_call | solution.py:626
  420.2 2.0 slice_bitcast_fusion.1
  422.3 2.6 maximum_convert_fusion
  424.8 5.2 %copy.57 = f32[2,2,1024,192]{2,3,1,0:T(8,128)} copy(f32[2,2,1024,192]{3,2,0,1:T(8,128)} %maximum_convert_fusion) | data formatting | bytes 6291456
  430.0 8.8 %slice_convert_fusion = (f32[2,768,768]{2,1,0:T(8,128)}, f32[2,768,768]{2,1,0:T(8,128)}, f32[2,768,768]{2,1,0:T(8,128)}) fusion(bf16[2,2304,768]{2,1,0:T(8,128)(2,1)} %get-tuple-element.64), kind=kLoop, calls=%fused_computation.1 | loop fusion | flops 3538944 | bytes 21233664 | tf_op jit(solution)/shard_map/convert_element_type | solution.py:1546
  438.9 2.1 convert_bitcast_fusion
  441.1 0.7 constant_dynamic-slice_fusion
  441.7 0.7 constant_dynamic-slice_fusion.1
  442.4 1.1 slice_convert_fusion.3
  443.5 1.0 fusion
  444.5 0.8 convert.6
  445.3 0.8 convert.7
  446.1 1.1 copy.55
  447.1 1.1 copy.56
  448.2 0.7 slice.41
  448.9 0.6 copy.54
  (28 shorter events, 0.2 us)
Async XLA Ops:
  0.6 5.1 %copy-start.1 = (bf16[2,768,3,192]{1,3,2,0:T(8,128)(2,1)S(1)}, bf16[2,768,3,192]{1,3,2,0:T(8,128)(2,1)}, u32[]{:S(2)}) copy-start(bf16[2,768,3,192]{1,3,2,0:T(8,128)(2,1)} %param.20) | copy-start | bytes 5308420
  5.7 2.5 copy-start.4
  5.7 3.5 copy-start.5
  5.7 4.5 copy-start.8
  5.7 5.5 %copy-start.6 = (f32[2,3,3,192]{3,0,2,1:T(2,128)S(1)}, f32[2,3,3,192]{3,0,2,1:T(2,128)}, u32[]{:S(2)}) copy-start(f32[2,3,3,192]{3,0,2,1:T(2,128)} %param.21) | copy-start | bytes 41476
  5.7 6.1 %copy-start.9 = (f32[2,192]{1,0:T(2,128)S(1)}, f32[2,192]{1,0:T(2,128)}, u32[]{:S(2)}) copy-start(f32[2,192]{1,0:T(2,128)} %param.26) | copy-start | bytes 4612
  5.8 6.1 %copy-start.10 = (f32[2,192]{1,0:T(2,128)S(1)}, f32[2,192]{1,0:T(2,128)}, u32[]{:S(2)}) copy-start(f32[2,192]{1,0:T(2,128)} %param.19) | copy-start | bytes 4612
  430.0 8.8 %copy-start = (bf16[2,768,768]{2,1,0:T(8,128)(2,1)S(1)}, bf16[2,768,768]{2,1,0:T(8,128)(2,1)}, u32[]{:S(2)}) copy-start(bf16[2,768,768]{2,1,0:T(8,128)(2,1)} %get-tuple-element.60) | copy-start | bytes 7077892
  438.9 2.1 copy-start.7
  441.0 5.0 %copy-start.3 = (bf16[1024,192]{1,0:T(8,128)(2,1)S(1)}, bf16[1024,192]{1,0:T(8,128)(2,1)}, u32[]{:S(2)}) copy-start(bf16[1024,192]{1,0:T(8,128)(2,1)} %get-tuple-element.57) | copy-start | bytes 1179652
  442.4 4.8 %copy-start.2 = (bf16[1024,192]{1,0:T(8,128)(2,1)S(1)}, bf16[1024,192]{1,0:T(8,128)(2,1)}, u32[]{:S(2)}) copy-start(bf16[1024,192]{1,0:T(8,128)(2,1)} %get-tuple-element.58) | copy-start | bytes 1179652

commit v4 on v3

--- a/solution.py
+++ b/solution.py
@@ -494,8 +494,7 @@
             for copy in self.firsts(a) + self.keeps(a):
                 copy.wait()
             for k in range(4):
-                total = self.kept[a][k].astype(F32) + self.got[a][k].astype(F32)
-                self.kept[a][k] = total.astype(BF)
+                self.kept[a][k] = self.kept[a][k] + self.got[a][k]
             for copy in self.seconds(a):
                 copy.start()
 
@@ -507,7 +506,7 @@
             kept, late = self.kept[a], self.late[a]
             for part in range(2):
                 at = self.summed(part)
-                kept[at] = (kept[at].astype(F32) + late[part].astype(F32)).astype(BF)
+                kept[at] = kept[at] + late[part]
 
             @pl.when(p.own)
             def _():
@@ -527,15 +526,13 @@
 
             @pl.when(p.own)
             def _():
-                self.totals[a][...] = (
-                    cross[0].astype(F32) + self.kept[a][self.summed(p.half)].astype(F32)
-                ).astype(BF)
+                self.totals[a][...] = cross[0] + self.kept[a][self.summed(p.half)]
 
             @pl.when(jnp.logical_not(p.own))
             def _():
                 await_recv(cross.at[1], self.recv.at[a, 7], self.send.at[a, 7])
                 await_send(cross.at[1], self.send.at[a, 7], self.recv.at[a, 7])
-                self.totals[a][...] = (cross[0].astype(F32) + cross[1].astype(F32)).astype(BF)
+                self.totals[a][...] = cross[0] + cross[1]
 
 
 class Spread:
@@ -682,7 +679,7 @@
 
 MIXER = dict(in_proj="w_in", cond_in="w_ci", cond_out="w_co", out_proj="w_out", filter_spec="w_spec")
 FFN = dict(gate_proj="w_gate", up_proj="w_up", down_proj="w_down")
-CUTS = dict(in_proj=1, cond_in=1, cond_out=1, filter_spec=1, out_proj=0, gate_proj=0, up_proj=0, down_proj=0)
+CUTS = dict(in_proj=1, cond_in=1, cond_out=1, filter_spec=2, out_proj=0, gate_proj=0, up_proj=0, down_proj=0)
 PROJ, QUERY, MIXED, SPECTRA, MIX_ROWS = 0, 3, 4, 5, 11
 
 
@@ -802,6 +799,8 @@
                 r.mix[PROJ + s, at] = proj.astype(BF)
 
         project(0)
+        if l == 0:
+            ffn_weights[0].start()
         group.gather_peer(h_all)
         project(2)
         for chunk in range(CHUNKS):
@@ -812,7 +811,6 @@
 
         if l == 0:
             mixer_weights[0].forward(rest)
-            ffn_weights[0].start()
         for t in range(tiles):
             at = pl.ds(t * size, size)
             prev = r.masks[at, 0:1]
@@ -842,8 +840,8 @@
             value_im, cond_im = imag[:, :lanes], imag[:, wide : wide + lanes].astype(BF)
             pre = nn_dot(cond_re, r.in_re[...]) + nn_dot(cond_im, r.in_im[...])
             inner = (pre * normal_cdf(pre)).astype(BF)
-            kernel_re = r.w_spec[l, 0, at] + nt_dot(inner, r.out_re[...])
-            kernel_im = r.w_spec[l, 1, at] + nt_dot(inner, r.out_im[...])
+            kernel_re = r.w_spec[l, 0, :, at].T + nt_dot(inner, r.out_re[...])
+            kernel_im = r.w_spec[l, 1, :, at].T + nt_dot(inner, r.out_im[...])
             r.prod_re[at] = (value_re * kernel_re - value_im * kernel_im).astype(BF)
             r.prod_im[at] = (value_re * kernel_im + value_im * kernel_re).astype(BF)
             r.pre[at] = pre.astype(BF)
@@ -1096,7 +1094,7 @@
     mix_scatter = [Scatter(place, r, of(r, "g_"), of(r, "u_"), "ms", l) for l in range(layers)]
     freed = [
         r.weight_grads.at[pl.ds(0, 4 * lanes)],
-        r.units.at[0, :, pl.ds(0, 2 * lanes)],
+        r.cos.at[pl.ds(0, 2 * lanes)],
         r.units.at[1, pl.ds(0, 2 * groups * feats), pl.ds(0, inner)],
         r.units.at[1, pl.ds(0, 256), pl.ds(inner, 128)],
     ]
@@ -1152,9 +1150,6 @@
         r.own_part[...] = block(group.at(0))
         group.gather_peer(r.g_all)
         group.reduce_whole("peer", block(group.at(2)))
-        if not top:
-            ffn_scatter[l + 1].finish()
-            ffn_spread[l + 1].start()
         for chunk in range(CHUNKS):
             group.gather_near(r.g_all, chunk)
             r.near_part[group.piece(chunk)] = block(group.at(1, chunk))
@@ -1162,6 +1157,8 @@
             group.reduce_peer(1, chunk, block(group.at(3, chunk)))
             group.reduce_near(chunk, r.near_part[group.piece(chunk)])
         load.finish()
+        if not top:
+            ffn_spread[l + 1].forward()
         step = 256
         for u in range(units // step):
             cols = pl.ds(u * step, step)
@@ -1179,6 +1176,7 @@
         group.finish()
         if not top:
             mix_scatter[l + 1].middle()
+            ffn_spread[l + 1].finish()
 
     def mixer(l):
         top, bottom = l + 1 == layers, l == 0
@@ -1210,12 +1208,12 @@
             gated_back(1, chunk)
             group.gather_diagonal(r.m_all, chunk)
             gated_back(3, chunk)
+        ffn_scatter[l].second()
         if top:
             first.finish((2, 3))
         else:
             mix_scatter[l + 1].finish()
             mix_spread[l + 1].start()
-            ffn_spread[l + 1].forward()
 
         @pl.loop(0, tiles)
         def _(t):
@@ -1229,7 +1227,8 @@
             kernel_im_grad = imag * value_re - real * value_im
             both_re[at, 0:lanes] = (real * kernel_re + imag * kernel_im).astype(BF)
             both_im[at, 0:lanes] = (imag * kernel_re - real * kernel_im).astype(BF)
-            r.g_spec[at] = jnp.concatenate([kernel_re_grad, kernel_im_grad], 1).astype(BF)
+            r.g_spec[0:lanes, at] = kernel_re_grad.T.astype(BF)
+            r.g_spec[lanes : 2 * lanes, at] = kernel_im_grad.T.astype(BF)
             kernel_re_grad = kernel_re_grad.astype(BF)
             kernel_im_grad = kernel_im_grad.astype(BF)
             pre = r.pre_all[at].astype(F32)
@@ -1252,8 +1251,7 @@
             turned = jnp.concatenate([sum_out[0][rows_at, cols], sum_out[1][rows_at, cols]], 0)
             at += groups * feats
             r.g_mlp[at : at + inner] = turned.T.astype(BF)
-        ffn_scatter[l].second()
-        mix_scatter[l].start((1, 2))
+        ffn_scatter[l].middle()
 
         @pl.loop(0, tiles)
         def _(t):
@@ -1262,6 +1260,8 @@
             to = pl.ds(pl.multiple_of(t * size + PAD, 8), size)
             r.padded[1, to] = both[:, :lanes]
             r.padded[2, to] = both[:, wide : wide + lanes]
+
+        mix_scatter[l].start((1, 2))
 
         def tap(o, s):
             at = 9 * l + 3 * o + s
@@ -1288,16 +1288,17 @@
             at = group.at(which)
             return sum(nt_dot(proj_grads[s][at, 0:lanes], r.w_in[0, s]) for s in range(3))
 
-        group.reduce_whole("diagonal", feats_grad(3))
-        group.reduce_whole("near", feats_grad(1))
-        group.reduce_whole("peer", feats_grad(2))
         load.finish()
         for s in range(3):
             r.g_proj[s * lanes : (s + 1) * lanes] = tn_dot(proj_grads[s][:, 0:lanes], r.h_all[...]).astype(BF)
         q_g[:, 0:lanes] = (r.mix[QUERY].astype(F32) * r.mix[MIXED].astype(F32)).astype(BF)
         r.g_proj[3 * lanes :] = tn_dot(q_g[:, 0:lanes], r.m_all[...]).astype(BF)
         mix_scatter[l].start((0,))
-        ffn_scatter[l].middle()
+        group.reduce_whole("diagonal", feats_grad(3))
+        group.reduce_whole("near", feats_grad(1))
+        group.reduce_whole("peer", feats_grad(2))
+        ffn_scatter[l].finish()
+        ffn_spread[l].start()
         if bottom:
             mix_scatter[l].second((1, 2))
         if not top:
@@ -1325,7 +1326,6 @@
         mix_scatter[l].start((3,))
         group.finish()
         if not top:
-            ffn_spread[l + 1].finish()
             mix_spread[l + 1].finish()
 
     for l in reversed(range(layers)):
@@ -1339,8 +1339,6 @@
     ]
     for copy in above:
         copy.start()
-    ffn_scatter[0].finish()
-    ffn_spread[0].start()
     mix_scatter[0].middle((1, 2))
     mix_scatter[0].second((0, 3))
     mix_scatter[0].finish((1, 2))
@@ -1400,7 +1398,7 @@
     ins = dict(cosine=tables[0], sine=tables[1], **{n: getattr(fwd, n) for n in held + near})
     grads = dict(
         proj=(4 * lanes, width),
-        spec=(length, 2 * lanes),
+        spec=(2 * lanes, length),
         mlp=(2 * groups * feats, inner),
         small=(256, 128),
     )
@@ -1490,7 +1488,7 @@
         in_proj=in_proj.transpose(0, 2, 1, 3),
         cond_in=cond_in,
         cond_out=cond_out,
-        filter_spec=filter_spec,
+        filter_spec=filter_spec.transpose(0, 1, 3, 2),
         out_proj=out_proj,
         gate_proj=gate_proj,
         up_proj=up_proj,
@@ -1527,7 +1525,7 @@
     mlp_rows = groups * feats
     g_in = proj[:, : 3 * shard].reshape(layers, 3, shard, width).transpose(0, 3, 1, 2)
     g_taps = small[:, :taps_rows].reshape(layers, 9, steps * 128)[:, :, :shard]
-    g_spec = jnp.stack([spec[:, :, :shard], spec[:, :, shard:]], 1)
+    g_spec = spec.reshape(layers, 2, shard, length).transpose(0, 1, 3, 2)
     results = (
         back.output,
         back.stream_grad,

time: 455 us -> 436 us (0.958)
  local copies, waits for them, and re-layouts: 24.4 us -> 13.7 us
  Pallas kernels: 408 us -> 399 us
    pallas_call x2, Pallas kernels: 408 us -> 399 us  [call_kernel(): pl.pallas_call(run, out_shape=[jax.ShapeDtypeStruct(*o) for o in outs.val...]
    unnamed x31 -> x29, local copies, waits for them, and re-layouts: 16.9 us -> 8.25 us
where the time goes in v4:
time: 436 us; the launch traced here: 430 us
  Pallas kernels  399 us (92%)
  other arithmetic  16.2 us (4%)
  local copies, waits for them, and re-layouts  13.7 us (3%)
    pallas_call x2, Pallas kernels, call_kernel(): pl.pallas_call(run, out_shape=[jax.ShapeDtypeStruct(*o) for o in outs.val...  399 us
    convert_element_type x7, other arithmetic, on_device(): return tuple((x.astype(F32) for x in results))  15.6 us

profile of v4, /device:TPU:0, one launch (start us, length us, event | category | flops | bytes accessed | tf_op | source)
XLA Modules:
  0.0 429.8 jit_solution(8660678690412155890)
XLA Ops:
  0.6 0.0 copy-start.4
  0.7 0.0 copy-start.5
  0.7 4.1 copy.45
  4.8 1.0 copy.46.refs_0_
  5.8 1.0 copy.47.refs_1_
  6.8 1.0 copy.48.refs_2_
  7.8 0.6 reshape.53.refs_4_
  8.4 0.6 pad_maximum_fusion.refs_3_
  9.0 178.9 %shard_map.255 = (f32[3,256,768]{2,1,0:T(8,128)}, f32[2,256,768]{2,1,0:T(8,128)}, f32[256,768]{1,0:T(8,128)}, f32[4,768]{1,0:T(4,128)}, f32[18,192]{1,0:T(8,128)...) custom-call(bf16[1024,192]{1,0:T(8,128)(2,1)} %copy.46.refs_0_, ...), custom_call_target="tpu_custom_call" | custom-call | flops 30000001024 | bytes 20971520 | tf_op jit(solution)/shard_map/pallas_call | solution.py:623
  187.9 220.0 %shard_map.256 = (bf16[1024,192]{1,0:T(8,128)(2,1)}, bf16[1024,192]{1,0:T(8,128)(2,1)}, bf16[2,2304,768]{2,1,0:T(8,128)(2,1)}, bf16[2,768,768]{2,1,0:T(8,128)(2,...) custom-call(bf16[1024,1024]{1,0:T(8,128)(2,1)} %constant.14.clone.re, ...), custom_call_target="tpu_custom_call" | custom-call | flops 40000000000 | bytes 20971520 | tf_op jit(solution)/shard_map/pallas_call | solution.py:623
  407.9 8.8 %slice_convert_fusion = (f32[2,768,768]{2,1,0:T(8,128)}, f32[2,768,768]{2,1,0:T(8,128)}, f32[2,768,768]{2,1,0:T(8,128)}) fusion(bf16[2,2304,768]{2,1,0:T(8,128)(2,1)} %get-tuple-element.64), kind=kLoop, calls=%fused_computation.2 | loop fusion | flops 3538944 | bytes 21233664 | tf_op jit(solution)/shard_map/convert_element_type | solution.py:1544
  416.7 0.1 slice.34
  416.8 2.1 convert_bitcast_fusion
  419.0 2.1 convert_bitcast_fusion.1
  421.0 0.7 constant_dynamic-slice_fusion
  421.7 0.7 constant_dynamic-slice_fusion.1
  422.4 1.1 slice_convert_fusion.3
  423.4 1.0 fusion
  424.5 0.8 convert.8
  425.3 0.8 convert.9
  426.1 1.1 copy.50
  427.1 1.1 copy.51
  428.2 0.7 slice.35
  428.9 0.6 copy.49
  (25 shorter events, 0.1 us)
Async XLA Ops:
  0.6 4.1 copy-start.4
  0.7 5.1 %copy-start.5 = (bf16[1024,192]{0,1:T(8,128)(2,1)S(1)}, bf16[1024,192]{0,1:T(8,128)(2,1)}, u32[]{:S(2)}) copy-start(bf16[1024,192]{0,1:T(8,128)(2,1)} %param.18) | copy-start | bytes 1179652
  0.7 6.1 %copy-start.8 = (s32[1024]{0:T(1024)S(1)}, s32[1024]{0:T(1024)}, u32[]{:S(2)}) copy-start(s32[1024]{0:T(1024)} %param.17) | copy-start | bytes 12292
  0.7 7.1 %copy-start.6 = (f32[2,3,3,192]{3,0,2,1:T(2,128)S(1)}, f32[2,3,3,192]{3,0,2,1:T(2,128)}, u32[]{:S(2)}) copy-start(f32[2,3,3,192]{3,0,2,1:T(2,128)} %param.21) | copy-start | bytes 41476
  0.7 7.8 %copy-start.10 = (f32[2,192]{1,0:T(2,128)S(1)}, f32[2,192]{1,0:T(2,128)}, u32[]{:S(2)}) copy-start(f32[2,192]{1,0:T(2,128)} %param.19) | copy-start | bytes 4612
  0.7 7.7 %copy-start.9 = (f32[2,192]{1,0:T(2,128)S(1)}, f32[2,192]{1,0:T(2,128)}, u32[]{:S(2)}) copy-start(f32[2,192]{1,0:T(2,128)} %param.26) | copy-start | bytes 4612
  407.9 8.8 %copy-start = (bf16[2,768,768]{2,1,0:T(8,128)(2,1)S(1)}, bf16[2,768,768]{2,1,0:T(8,128)(2,1)}, u32[]{:S(2)}) copy-start(bf16[2,768,768]{2,1,0:T(8,128)(2,1)} %get-tuple-element.60) | copy-start | bytes 7077892
  416.8 2.1 copy-start.1
  419.0 2.1 copy-start.7
  421.0 5.0 %copy-start.3 = (bf16[1024,192]{1,0:T(8,128)(2,1)S(1)}, bf16[1024,192]{1,0:T(8,128)(2,1)}, u32[]{:S(2)}) copy-start(bf16[1024,192]{1,0:T(8,128)(2,1)} %get-tuple-element.57) | copy-start | bytes 1179652
  422.4 4.8 %copy-start.2 = (bf16[1024,192]{1,0:T(8,128)(2,1)S(1)}, bf16[1024,192]{1,0:T(8,128)(2,1)}, u32[]{:S(2)}) copy-start(bf16[1024,192]{1,0:T(8,128)(2,1)} %get-tuple-element.58) | copy-start | bytes 1179652
